TPU v7x, 512 devices: a whole 4x4x16 slice. The times are simulated.
512 devices in a mesh: curve: 128 (over z, x, core), head: 4 (over y).
Axes of the slice: x: 4, y: 4, z: 16, core: 2. Of those that a mesh axis runs over, the one named last changes fastest.
Arguments:
- features: float32 [65536, 512], P('curve', 'head')
- input_proj: float32 [512, 3, 512], P(None, None, 'head')
- output_proj: float32 [512, 512], P('head'), may hold values from -0.25 to 0.25
- destination: int32 [65536], P('curve'), may hold values from 0 to 65535, as said below
- real_points: int32 [65536], P('curve'), may hold values from 0 to 1, as said below
- cotangent: float32 [65536, 512], P('curve', 'head'), may hold values from -6 to 6
Outputs:
- branch_out: float32 [65536, 512], P('curve', 'head')
- grad_features: float32 [65536, 512], P('curve', 'head')
- grad_inproj: float32 [512, 3, 512], P(None, None, 'head')
- grad_outproj: float32 [512, 512], P('head')
Inputs may be any that keep to these rules, and one draw needn't show every extreme that they name: `destination`: A permutation of the points. Each aligned block of 512 points in the first order sends exactly 4 points to each aligned block of 512 positions in the second order. `real_points`: the first 128 points of every aligned block of 512 points are real.
All inputs are finite; a program needn't handle non-finite values.
Results may differ from a plain program's by a relative error of at most 0.0003.
Values sent between devices are 32-bit elements; how exact they have to be, the bound alone decides.
No kernel may reach another device: no remote copies, remote signals or barrier semaphores. Data moves between devices by JAX's collectives and lax.ppermute only.
A program may use at most 64 MiB of HBM per device.

v0:
```python
import math

import jax
import jax.numpy as jnp
import numpy as np
from jax import lax
from jax.sharding import PartitionSpec as P

D = 512
HEADS = 16
PATCH = 512


highest = lax.Precision.HIGHEST


def extended(shard, sides, width):
    for axis, dim in sides:
        size, length = (lax.axis_size(axis), shard.shape[dim])
        up = [(i, (i + 1) % size) for i in range(size)]
        down = [(j, i) for i, j in up]
        last = lax.slice_in_dim(shard, length - width, length, axis=dim)
        initial = lax.slice_in_dim(shard, 0, width, axis=dim)
        before = lax.ppermute(last, axis, up)
        after = lax.ppermute(initial, axis, down)
        shard = jnp.concatenate([before, shard, after], axis=dim)
    return shard


def shifted(shard, axis, by):
    size = lax.axis_size(axis)
    return lax.ppermute(shard, axis, [(i, (i + by) % size) for i in range(size)])


def attend(queries, key_rows, validity):
    scaling = 1.0 / math.sqrt(queries.shape[-1])
    scores = jnp.einsum("qhe,khe->hqk", queries, key_rows, precision=highest) * scaling
    scores = jnp.where(validity[None, None, :] > 0, scores, -jnp.inf)
    row_max = jnp.max(scores, axis=-1, keepdims=True)
    weights = jnp.exp(scores - row_max)
    return weights / jnp.sum(weights, axis=-1, keepdims=True)


def forward_block(operands):
    queries, key_rows, values, validity = operands
    probability = attend(queries, key_rows, validity)
    return jnp.einsum("hqk,khe->qhe", probability, values, precision=highest)


def backward_block(operands):
    queries, key_rows, values, validity, attended, grad_attended = operands
    scaling = 1.0 / math.sqrt(queries.shape[-1])
    probability = attend(queries, key_rows, validity)
    grad_probs = jnp.einsum("qhe,khe->hqk", grad_attended, values, precision=highest)
    row_inner = jnp.transpose(jnp.sum(grad_attended * attended, axis=-1))
    grad_scores = probability * (grad_probs - row_inner[:, :, None])
    grad_query = jnp.einsum("hqk,khe->qhe", grad_scores, key_rows, precision=highest) * scaling
    grad_keys = jnp.einsum("hqk,qhe->khe", grad_scores, queries, precision=highest) * scaling
    grad_values = jnp.einsum("hqk,qhe->khe", probability, grad_attended, precision=highest)
    return (grad_query, jnp.stack([grad_keys, grad_values], axis=1))


def shards(features, input_proj, output_proj, destination, real_points, cotangent):
    row_count = features.shape[0]
    shard_width = input_proj.shape[2]
    head_size = D // HEADS
    heads_here = shard_width // head_size
    position = lax.axis_index("curve")
    targets = destination // row_count
    sorting = jnp.argsort(targets, stable=True)
    sent_dest = destination[sorting]
    gathered = lax.all_gather(features, "head", axis=1, tiled=True)
    projected = jnp.einsum("nd,dtf->ntf", gathered, input_proj, precision=highest)
    arrived, landed = (
        lax.all_to_all(projected[sorting], "curve", split_axis=0, concat_axis=0, tiled=True),
        lax.all_to_all(sent_dest, "curve", split_axis=0, concat_axis=0, tiled=True),
    )
    placed = landed - position * row_count
    qkv = jnp.zeros_like(projected).at[placed].set(arrived)
    half_patch = PATCH // 2
    patch_count = row_count // PATCH
    key_value = qkv[:, 1:]
    kv_ext, valid_ext = (
        extended(key_value, (("curve", 0),), half_patch),
        extended(real_points, (("curve", 0),), half_patch),
    )
    kv_blocks = kv_ext.reshape(patch_count + 1, PATCH, 2, heads_here, head_size)
    valid_blocks = valid_ext.reshape(patch_count + 1, PATCH)
    owners = (np.arange(2 * patch_count) + 1) // 2
    query_blocks = qkv[:, 0].reshape(2 * patch_count, half_patch, heads_here, head_size)
    chosen = kv_blocks[owners]
    chosen_valid = valid_blocks[owners]
    attended = lax.map(
        forward_block, (query_blocks, chosen[:, :, 0], chosen[:, :, 1], chosen_valid)
    )
    attended = attended.reshape(row_count, shard_width)
    branch_out = lax.psum_scatter(
        jnp.dot(attended, output_proj, precision=highest), "head", scatter_dimension=1, tiled=True
    )
    full_cot = lax.all_gather(cotangent, "head", axis=1, tiled=True)
    grad_out_here = jnp.dot(attended.T, full_cot, precision=highest)
    grad_attended = jnp.dot(full_cot, output_proj.T, precision=highest)
    shaped = (2 * patch_count, half_patch, heads_here, head_size)
    grad_query, grad_pairs = lax.map(
        backward_block,
        (
            query_blocks,
            chosen[:, :, 0],
            chosen[:, :, 1],
            chosen_valid,
            attended.reshape(shaped),
            grad_attended.reshape(shaped),
        ),
    )
    padding = jnp.zeros((1,) + grad_pairs.shape[1:], jnp.float32)
    grad_ext = jnp.concatenate([padding, grad_pairs, padding], axis=0)
    grad_ext = grad_ext.reshape((patch_count + 1, 2) + grad_pairs.shape[1:]).sum(axis=1)
    grad_ext = grad_ext.reshape(row_count + PATCH, 2, shard_width)
    upper_rim = grad_ext[:half_patch]
    lower_rim = grad_ext[row_count + half_patch :]
    interior = grad_ext[half_patch : row_count + half_patch]
    from_next = shifted(upper_rim, "curve", -1)
    from_prev = shifted(lower_rim, "curve", 1)
    interior = interior.at[row_count - half_patch :].add(from_next)
    interior = interior.at[:half_patch].add(from_prev)
    grad_qkv = jnp.concatenate([grad_query.reshape(row_count, 1, shard_width), interior], axis=1)
    returned = lax.all_to_all(grad_qkv[placed], "curve", split_axis=0, concat_axis=0, tiled=True)
    grad_morton = jnp.zeros_like(grad_qkv).at[sorting].set(returned)
    grad_in_here = jnp.einsum("nd,ntf->dtf", gathered, grad_morton, precision=highest)
    partial_rows = jnp.einsum("ntf,dtf->nd", grad_morton, input_proj, precision=highest)
    grad_features = lax.psum_scatter(partial_rows, "head", scatter_dimension=1, tiled=True)
    grad_inproj, grad_outproj = lax.psum((grad_in_here, grad_out_here), "curve")
    return (branch_out, grad_features, grad_inproj, grad_outproj)


def solution(mesh):
    return jax.shard_map(
        shards,
        mesh=mesh,
        in_specs=(
            P("curve", "head"),
            P(None, None, "head"),
            P("head", None),
            P("curve"),
            P("curve"),
            P("curve", "head"),
        ),
        out_specs=(P("curve", "head"), P("curve", "head"), P(None, None, "head"), P("head", None)),
        check_vma=False,
    )
```

profile of v0, /device:TPU:1, one launch (start us, length us, event | category | flops | bytes accessed | tf_op | source)
XLA Modules:
  0.0 701.2 jit_solution(14134077020439933270)
XLA Ops:
  8.6 3.8 sort.17
  12.4 3.6 gather_fusion
  16.8 20.4 %all-to-all-start = ((s32[128,4,1]{1,2,0:T(1,128)}), s32[128,4,1]{1,2,0:T(1,128)S(1)}, u32[]{:S(2)}, u32[]{:S(2)}) async-start(s32[128,4,1]{1,2,0:T(1,128)} %bitcast.18), calls=%async_computation | async-start | bytes 131072 | tf_op jit(solution)/shard_map/all_to_all | solution.py:76
  37.2 11.0 %all-gather.3.cloned.1.call-done = f32[512,512]{1,0:T(8,128)} async-done(((f32[512,128]{1,0:T(8,128)}), f32[512,512]{1,0:T(8,128)}) %all-gather.3.cloned.1.call-update) | async-done | bytes 1048592 | tf_op jit(solution)/shard_map/all_gather | solution.py:72
  48.2 3.0 fusion.52
  51.8 2.6 gather_fusion.1
  54.4 17.5 %all-to-all-start.1 = ((f32[512,3,128]{2,1,0:T(4,128)}), f32[512,3,128]{2,1,0:T(4,128)S(1)}, u32[]{:S(2)}, u32[]{:S(2)}) async-start(f32[512,3,128]{2,1,0:T(4,128)} %gather_fusion.1), calls=%async_computation.1 | async-start | bytes 2097152 | tf_op jit(solution)/shard_map/all_to_all | solution.py:75
  72.7 3.5 collective-permute-start.2
  78.2 3.2 collective-permute-done.3
  82.3 41.5 %all-to-all-done.1 = f32[512,3,128]{2,1,0:T(4,128)S(1)} async-done(((f32[512,3,128]{2,1,0:T(4,128)}), f32[512,3,128]{2,1,0:T(4,128)S(1)}, u32[]{:S(2)}, u32[]{:S(2)}) %all-to-all-start.1) | async-done | bytes 786464 | tf_op jit(solution)/shard_map/all_to_all | solution.py:75
  123.9 13.6 %scatter_fusion = f32[512,3,128]{2,1,0:T(4,128)S(1)} fusion(f32[512,3,128]{2,1,0:T(4,128)S(1)} %broadcast.123.clone, s32[512]{0:T(512)S(1)} %bitcast.151, f32[512,3,128]{2,1,0:T(4,128)S(1)} %all-to-all-done.1), kind=kCustom, calls=%fused_computation.5 | custom fusion | bytes 2361344 | tf_op jit(solution)/shard_map/scatter | solution.py:79
  137.7 4.2 collective-permute-start
  141.9 2.6 collective-permute-start.1
  144.6 2.4 fusion.61
  155.2 10.0 %while.24 = (s32[]{:T(128)}, f32[2,256,4,32]{1,3,2,0:T(8,128)S(1)}, f32[2,512,4,32]{1,3,2,0:T(8,128)}, s32[2,512]{1,0:T(2,128)S(1)}, f32[2,256,4,32]{1,3,2,0:T(8...) while((s32[]{:T(128)}, f32[2,256,4,32]{1,3,2,0:T(8,128)S(1)}, f32[2,512,4,32]{1,3,2,0:T(8,128)}, ...), condition=%wide.region_5.6_spmd, body=%wide.region_2.5_spmd.sunk | while | flops 408418816 | bytes 9201773 | solution.py:93
  157.9 2.3 fusion.96
  162.9 2.3 fusion.96
  165.2 24.6 %while.25 = (s32[]{:T(128)}, f32[2,256,4,32]{1,0,3,2:T(2,128)S(1)}, f32[2,512,2,4,32]{1,4,3,2,0:T(8,128)}, f32[2,512,4,32]{1,3,2,0:T(8,128)S(1)}, s32[2,512]{1,0...) while((s32[]{:T(128)}, f32[2,256,4,32]{1,0,3,2:T(2,128)S(1)}, ...), condition=%wide.region_11.12_spmd, body=%wide.region_7.11_spmd.sunk | while | flops 1015838208 | bytes 29271776 | solution.py:104
  170.0 2.3 subtract_multiply_fusion.2
  182.3 2.3 subtract_multiply_fusion.2
  194.7 6.0 collective-permute-start.4
  201.5 2.1 collective-permute-start.5
  209.2 2.6 gather_fusion.4
  211.9 16.0 %all-to-all-start.2 = ((f32[512,3,128]{2,1,0:T(4,128)}), f32[512,3,128]{2,1,0:T(4,128)S(1)}, u32[]{:S(2)}, u32[]{:S(2)}) async-start(f32[512,3,128]{2,1,0:T(4,128)} %gather_fusion.4), calls=%async_computation.3 | async-start | bytes 2097152 | tf_op jit(solution)/shard_map/all_to_all | solution.py:127
  229.6 50.1 %all-to-all-done.2 = f32[512,3,128]{2,1,0:T(4,128)S(1)} async-done(((f32[512,3,128]{2,1,0:T(4,128)}), f32[512,3,128]{2,1,0:T(4,128)S(1)}, u32[]{:S(2)}, u32[]{:S(2)}) %all-to-all-start.2) | async-done | bytes 786464 | tf_op jit(solution)/shard_map/all_to_all | solution.py:127
  279.9 13.6 %scatter_fusion.1 = f32[512,3,128]{2,1,0:T(4,128)S(1)} fusion(f32[512,3,128]{2,1,0:T(4,128)S(1)} %broadcast.123, s32[512]{0:T(512)S(1)} %compare_select_fusion.1, f32[512,3,128]{2,1,0:T(4,128)S(1)} %all-to-all-done.2), kind=kCustom, calls=%fused_computation.6 | custom fusion | bytes 2361344 | tf_op jit(solution)/shard_map/scatter | solution.py:128
  293.7 3.6 convolution_bitcast_fusion.2
  299.5 3.7 convolution_bitcast_fusion.1
  303.2 324.1 %all-reduce.3.cloned.1.call-done = (f32[512,3,128]{0,2,1:T(8,128)}, f32[128,512]{1,0:T(8,128)}) async-done(((f32[512,3,128]{0,2,1:T(8,128)}, f32[128,512]{1,0:T(8,128)}), (f32[512,3,128]{0,2,1:T(8,128)}, f32[128,512]{1,0:T(8,128)})) %all-reduce.3.cloned.1.call-update) | async-done | bytes 1048592 | tf_op jit(solution)/shard_map/psum | solution.py:132
  627.3 2.3 copy.70
  629.6 28.8 %reduce-scatter.3.cloned.1.call-done = f32[512,128]{1,0:T(8,128)} async-done(((f32[512,512]{1,0:T(8,128)}), f32[512,128]{1,0:T(8,128)}) %reduce-scatter.3.cloned.1.call-update) | async-done | bytes 262160 | tf_op jit(solution)/shard_map/reduce_scatter | solution.py:97
  658.5 34.3 %reduce-scatter.5.cloned.1.call-done = f32[512,128]{1,0:T(8,128)} async-done(((f32[512,512]{1,0:T(8,128)}), f32[512,128]{1,0:T(8,128)}) %reduce-scatter.5.cloned.1.call-update) | async-done | bytes 262160 | tf_op jit(solution)/shard_map/reduce_scatter | solution.py:131
  (137 shorter events, 56.7 us)
Async XLA Ops:
  7.2 41.0 %copy-start = (f32[512,3,128]{2,0,1:T(8,128)S(1)}, f32[512,3,128]{2,0,1:T(8,128)}, u32[]{:S(2)}) copy-start(f32[512,3,128]{2,0,1:T(8,128)} %param.18) | copy-start | bytes 2359300
  7.2 41.0 %all-gather.3.cloned.1.call-start = ((), (), s32[]{:S(2)}) async-start(), calls=%async_computation.5 | async-start | bytes 1310720 | tf_op jit(solution)/shard_map/all_gather | solution.py:72
  16.8 37.6 %all-to-all-start = ((s32[128,4,1]{1,2,0:T(1,128)}), s32[128,4,1]{1,2,0:T(1,128)S(1)}, u32[]{:S(2)}, u32[]{:S(2)}) async-start(s32[128,4,1]{1,2,0:T(1,128)} %bitcast.18), calls=%async_computation | async-start | bytes 131072 | tf_op jit(solution)/shard_map/all_to_all | solution.py:76
  51.8 20.9 %copy-start.13 = (s32[512]{0:T(512)S(1)}, s32[512]{0:T(512)}, u32[]{:S(2)}) copy-start(s32[512]{0:T(512)} %param.21) | copy-start | bytes 6148
  54.4 69.3 %all-to-all-start.1 = ((f32[512,3,128]{2,1,0:T(4,128)}), f32[512,3,128]{2,1,0:T(4,128)S(1)}, u32[]{:S(2)}, u32[]{:S(2)}) async-start(f32[512,3,128]{2,1,0:T(4,128)} %gather_fusion.1), calls=%async_computation.1 | async-start | bytes 2097152 | tf_op jit(solution)/shard_map/all_to_all | solution.py:75
  71.9 72.7 %all-gather.5.cloned.1.call-start = ((), (), s32[]{:S(2)}) async-start(), calls=%async_computation.7 | async-start | bytes 1310720 | tf_op jit(solution)/shard_map/all_gather | solution.py:100
  72.7 5.5 collective-permute-start.2
  76.2 5.2 collective-permute-start.3
  123.9 20.7 %copy-start.7 = (f32[128,512]{1,0:T(8,128)S(1)}, f32[128,512]{1,0:T(8,128)}, u32[]{:S(2)}) copy-start(f32[128,512]{1,0:T(8,128)} %param.19) | copy-start | bytes 786436
  137.7 11.6 %collective-permute-start = (f32[256,2,128]{2,1,0:T(2,128)S(1)}, f32[256,2,128]{2,1,0:T(2,128)}, u32[]{:S(2)}, u32[]{:S(2)}) collective-permute-start(f32[256,2,128]{2,1,0:T(2,128)S(1)} %get-tuple-element.224), channel_id=1, source_target_pairs={{0,4},{4,8},{8,12},{12,16},{16,20},{20,24},{24,28},{28,32},{32,36}... | collective-permute-start | bytes 786440 | tf_op jit(solution)/shard_map/ppermute | solution.py:24
  141.9 8.4 %collective-permute-start.1 = (f32[256,2,128]{2,1,0:T(2,128)S(1)}, f32[256,2,128]{2,1,0:T(2,128)}, u32[]{:S(2)}, u32[]{:S(2)}) collective-permute-start(f32[256,2,128]{2,1,0:T(2,128)S(1)} %get-tuple-element.225), channel_id=1, source_target_pairs={{4,0},{8,4},{12,8},{16,12},{20,16},{24,20},{28,24},{32,28},{36,32}... | collective-permute-start | bytes 786440 | tf_op jit(solution)/shard_map/ppermute | solution.py:25
  154.1 1.0 copy-start.1
  154.1 1.1 copy-start.4
  155.2 10.1 %copy-start.3 = (f32[2,256,4,32]{1,0,3,2:T(2,128)S(1)}, f32[2,256,4,32]{1,0,3,2:T(2,128)}, u32[]{:S(2)}) copy-start(f32[2,256,4,32]{1,0,3,2:T(2,128)} %reshape.140) | copy-start | bytes 786436
  155.2 10.1 %copy-start.11 = (f32[2,256,4,32]{1,0,3,2:T(2,128)S(1)}, f32[2,256,4,32]{1,0,3,2:T(2,128)}, u32[]{:S(2)}) copy-start(f32[2,256,4,32]{1,0,3,2:T(2,128)} %custom-call.11) | copy-start | bytes 786436
  155.2 2.6 copy-start.9
  160.2 2.6 copy-start.9
  168.2 1.8 copy-start.10
  172.4 1.3 copy-start.5
  173.8 2.2 copy-start.6
  180.4 1.8 copy-start.10
  184.6 1.3 copy-start.5
  186.0 2.2 copy-start.6
  189.9 0.7 copy-start.12
  194.7 10.7 %collective-permute-start.4 = (f32[256,2,128]{2,1,0:T(2,128)}, f32[256,2,128]{2,1,0:T(2,128)}, u32[]{:S(2)}, u32[]{:S(2)}) collective-permute-start(f32[256,2,128]{2,1,0:T(2,128)} %copy.77), channel_id=1, source_target_pairs={{0,508},{4,0},{8,4},{12,8},{16,12},{20,16},{24,20},{28,24},{32,28}... | collective-permute-start | bytes 786440 | tf_op jit(solution)/shard_map/ppermute | solution.py:32
  201.5 7.0 %collective-permute-start.5 = (f32[256,2,128]{2,1,0:T(2,128)}, f32[256,2,128]{2,1,0:T(2,128)S(1)}, u32[]{:S(2)}, u32[]{:S(2)}) collective-permute-start(f32[256,2,128]{2,1,0:T(2,128)} %copy.78), channel_id=1, source_target_pairs={{0,4},{4,8},{8,12},{12,16},{16,20},{20,24},{24,28},{28,32},{32,36}... | collective-permute-start | bytes 786440 | tf_op jit(solution)/shard_map/ppermute | solution.py:32
  211.9 16.3 %copy-start.2 = (f32[512,512]{1,0:T(8,128)S(1)}, f32[512,512]{1,0:T(8,128)}, u32[]{:S(2)}) copy-start(f32[512,512]{1,0:T(8,128)} %all-gather.5.cloned.1.call-done) | copy-start | bytes 3145732
  211.9 67.8 %all-to-all-start.2 = ((f32[512,3,128]{2,1,0:T(4,128)}), f32[512,3,128]{2,1,0:T(4,128)S(1)}, u32[]{:S(2)}, u32[]{:S(2)}) async-start(f32[512,3,128]{2,1,0:T(4,128)} %gather_fusion.4), calls=%async_computation.3 | async-start | bytes 2097152 | tf_op jit(solution)/shard_map/all_to_all | solution.py:127
  227.9 399.5 %all-reduce.3.cloned.1.call-start = ((), (), s32[]{:S(2)}) async-start(), calls=%async_computation.9 | async-start | bytes 2097152 | tf_op jit(solution)/shard_map/psum | solution.py:132
  293.7 3.7 copy-start.8
  297.4 361.1 %reduce-scatter.3.cloned.1.call-start = ((), (), s32[]{:S(2)}) async-start(), calls=%async_computation.6 | async-start | bytes 1310720 | tf_op jit(solution)/shard_map/reduce_scatter | solution.py:97
  299.4 393.3 %reduce-scatter.5.cloned.1.call-start = ((), (), s32[]{:S(2)}) async-start(), calls=%async_computation.8 | async-start | bytes 1310720 | tf_op jit(solution)/shard_map/reduce_scatter | solution.py:131
Sparse Core Ops, SparseCore 0:
  10.1 38.0 all-gather.2
  74.8 33.2 all-gather.4
  297.5 329.7 all-reduce.2
  630.8 27.5 reduce-scatter.2
  661.7 30.9 reduce-scatter.4
where the time goes:
time: 710 us; the launch traced here: 701 us
  waiting for transfers between devices  498 us (70%)
  starting transfers between devices  74.4 us (10%)
  local copies, waits for them, and re-layouts  58.4 us (8%)
  matrix products  43.8 us (6%)
  between operations  14.5 us (2%)
  other arithmetic  12.1 us (2%)
    psum x1, waiting for transfers between devices, shards(): grad_inproj, grad_outproj = lax.psum((grad_in_here, grad_out_here), 'curve')  324 us
    all_to_all x1, waiting for transfers between devices, shards(): lax.all_to_all(grad_qkv[placed], 'curve', split_axis=0, concat_axis=0, ti...  50.1 us
    all_to_all x1, waiting for transfers between devices, shards(): lax.all_to_all(projected[sorting], 'curve', split_axis=0, concat_axis=0,...  41.5 us
    reduce_scatter x1, waiting for transfers between devices, shards(): lax.psum_scatter(partial_rows, 'head', scatter_dimension=1, tiled=True)  34.3 us
    reduce_scatter x1, waiting for transfers between devices, shards(): lax.psum_scatter(jnp.dot(attended, output_proj, precision=highest), 'head...  28.8 us
    all_to_all x1, starting transfers between devices, shards(): lax.all_to_all(sent_dest, 'curve', split_axis=0, concat_axis=0, tiled=True)  20.4 us
    all_to_all x1, starting transfers between devices, shards(): lax.all_to_all(projected[sorting], 'curve', split_axis=0, concat_axis=0,...  17.5 us
    all_to_all x1, starting transfers between devices, shards(): lax.all_to_all(grad_qkv[placed], 'curve', split_axis=0, concat_axis=0, ti...  16 us
  transfers between devices with their start and end apart: 14, of which 9 were waited for; matrix products, arithmetic and copies ran while one was open for 7% of the time, Pallas kernels for 0%

commit v1 on v0

v1 whole, which is shorter than its diff:
```python
import functools
import math

import jax
import jax.numpy as jnp
from jax import lax
from jax.experimental import pallas as pl
from jax.experimental.pallas import tpu as pltpu
from jax.sharding import PartitionSpec as P

D = 512
HEADS = 16
PATCH = 512
HALF = PATCH // 2
HEAD = D // HEADS
WIDTH = 128
HERE = WIDTH // HEAD
CURVE = ("z", "x", "core")
BF = jnp.bfloat16
F32 = jnp.float32
SCALE = 1.0 / math.sqrt(HEAD)
LOG2E = math.log2(math.e)

NN = (((1,), (0,)), ((), ()))
NT = (((1,), (1,)), ((), ()))


def mm(a, b, dims=NN):
    return lax.dot_general(a, b, dims, preferred_element_type=F32)


def split(x):
    high = x.astype(BF)
    return high, (x - high.astype(F32)).astype(BF)


def split3(x):
    high, rest = x.astype(BF), None
    rest = x - high.astype(F32)
    mid = rest.astype(BF)
    return high, mid, (rest - mid.astype(F32)).astype(BF)


def mm3(a, b, dims=NN):
    (ah, al), (bh, bl) = a, b
    return mm(ah, bh, dims) + (mm(ah, bl, dims) + mm(al, bh, dims))


def select_rows(pick, x):
    high, mid, low = split3(x)
    return mm(pick, high) + (mm(pick, mid) + mm(pick, low))


def column(row):
    return jnp.transpose(jnp.broadcast_to(row, (WIDTH, PATCH)))


def wide(col):
    return jnp.concatenate([col] * (PATCH // WIDTH), axis=1)


def iota(dim):
    return lax.broadcasted_iota(jnp.int32, (PATCH, PATCH), dim).astype(F32)


def rows_to_slots(slot_row):
    return jnp.where(iota(0) == slot_row, 1.0, 0.0).astype(BF)


def slots_to_rows(slot_row):
    return jnp.where(wide(column(slot_row)) == iota(1), 1.0, 0.0).astype(BF)


def sort_kernel(each, dest_ref, feat_ref, sorted_ref, local_ref, slot_ref):
    dest = dest_ref[...]
    block = dest // PATCH
    local = (dest - block * PATCH).astype(F32)
    block = block.astype(F32)
    lower = iota(0) < iota(1)
    same = (wide(column(block)) == block) & lower
    rank = jnp.sum(jnp.where(same, 1.0, 0.0), axis=0, keepdims=True)
    slot = block * each + rank
    slot_ref[...] = slot
    back = wide(column(slot)) == iota(1)
    local_ref[...] = jnp.sum(jnp.where(back, wide(column(local)), 0.0), axis=0, keepdims=True)
    sorted_ref[...] = select_rows(rows_to_slots(slot), feat_ref[...])


def place_kernel(local_ref, arrived_ref, low_ref, high_ref):
    placed = select_rows(rows_to_slots(local_ref[...]), arrived_ref[...])
    low_ref[...] = placed[:HALF]
    high_ref[...] = placed[HALF:]


def unplace_kernel(local_ref, low_ref, high_ref, out_ref):
    grads = jnp.concatenate([low_ref[...], high_ref[...]], axis=0)
    out_ref[...] = select_rows(slots_to_rows(local_ref[...]), grads)


def unsort_kernel(slot_ref, returned_ref, out_ref):
    out_ref[...] = select_rows(slots_to_rows(slot_ref[...]), returned_ref[...])


def cot_kernel(cot_ref, wout_ref, grad_ref):
    total = jnp.zeros((PATCH, WIDTH), F32)
    for part in range(D // WIDTH):
        total += mm3(split(cot_ref[part]), split(wout_ref[:, part * WIDTH : (part + 1) * WIDTH]), NT)
    grad_ref[...] = total


def head_mask(head):
    lanes = lax.broadcasted_iota(jnp.int32, (PATCH, WIDTH), 1)
    return (lanes // HEAD) == head


def scores_of(queries, key_rows, mask):
    qh, ql = split(queries)
    kh, kl = split(jnp.where(mask, key_rows, 0.0))
    keys = jnp.concatenate([kh, kl], axis=1)
    return mm(keys, jnp.concatenate([qh, qh], axis=1), NT) + mm(
        keys, jnp.concatenate([ql, ql], axis=1), NT
    )


def forward_kernel(x_ref, win_ref, wout_ref, bias_ref, qkv_ref, att_ref, lse_ref, out_ref, vt_ref):
    parts = [split(x_ref[part]) for part in range(D // WIDTH)]
    for t in range(3):
        total = jnp.zeros((PATCH, WIDTH), F32)
        for part in range(D // WIDTH):
            total += mm3(parts[part], split(win_ref[t, part * WIDTH : (part + 1) * WIDTH]))
        qkv_ref[t] = total
    vt_ref[...] = jnp.transpose(qkv_ref[2])
    bias = wide(bias_ref[...])

    def one(head, carry):
        mask = head_mask(head)
        scores = scores_of(qkv_ref[0] * (SCALE * LOG2E), qkv_ref[1], mask) + bias
        top = jnp.max(scores, axis=0, keepdims=True)
        weights = jnp.exp2(scores - top)
        total = jnp.sum(weights, axis=0, keepdims=True)
        rows = pl.ds(pl.multiple_of(head * HEAD, HEAD), HEAD)
        vh, vl = split(vt_ref[rows, :])
        wh, wl = split(weights)
        both = mm(jnp.concatenate([vh, vl], axis=0), wh)
        attended = both[:HEAD] + both[HEAD:] + mm(vh, wl)
        att_ref[rows, :] = attended / total
        lse_ref[pl.ds(head, 1), :] = top + jnp.log2(total)
        return carry

    lax.fori_loop(0, HERE, one, 0)
    attended = split(jnp.transpose(att_ref[...]))
    for part in range(D // WIDTH):
        out_ref[part] = mm3(attended, split(wout_ref[:, part * WIDTH : (part + 1) * WIDTH]))


def backward_kernel(qkv_ref, att_ref, lse_ref, grad_ref, bias_ref, dqkv_ref, kt_ref, gt_ref, dqt_ref):
    kt_ref[...] = jnp.transpose(qkv_ref[1])
    gt_ref[...] = jnp.transpose(grad_ref[...])
    bias = wide(bias_ref[...])
    dqkv_ref[1] = jnp.zeros((PATCH, WIDTH), F32)
    dqkv_ref[2] = jnp.zeros((PATCH, WIDTH), F32)

    def one(head, carry):
        mask = head_mask(head)
        rows = pl.ds(pl.multiple_of(head * HEAD, HEAD), HEAD)
        scores = scores_of(qkv_ref[0] * (SCALE * LOG2E), qkv_ref[1], mask) + bias
        probs = jnp.exp2(scores - lse_ref[pl.ds(head, 1), :])
        ph, plo = split(probs)
        grad_probs = scores_of(grad_ref[...], qkv_ref[2], mask)
        gh, gl = split(jnp.where(mask, grad_ref[...], 0.0))
        both = mm(ph, jnp.concatenate([gh, gl], axis=1))
        dqkv_ref[2] += both[:, :WIDTH] + both[:, WIDTH:] + mm(plo, gh)
        inner = jnp.sum(gt_ref[rows, :] * att_ref[rows, :], axis=0, keepdims=True)
        grad_scores = probs * (grad_probs - inner)
        sh, sl = split(grad_scores)
        qh, ql = split(jnp.where(mask, qkv_ref[0] * SCALE, 0.0))
        both = mm(sh, jnp.concatenate([qh, ql], axis=1))
        dqkv_ref[1] += both[:, :WIDTH] + both[:, WIDTH:] + mm(sl, qh)
        kh, kl = split(kt_ref[rows, :] * SCALE)
        both = mm(jnp.concatenate([kh, kl], axis=0), sh)
        dqt_ref[rows, :] = both[:HEAD] + both[HEAD:] + mm(kh, sl)
        return carry

    lax.fori_loop(0, HERE, one, 0)
    dqkv_ref[0] = jnp.transpose(dqt_ref[...])


def weights_kernel(x_ref, dqkv_ref, att_ref, cot_ref, din_ref, dout_ref):
    attended = split(att_ref[...])
    for part in range(D // WIDTH):
        dout_ref[part] = mm3(attended, split(cot_ref[part]))
    parts = [split(x_ref[part]) for part in range(D // WIDTH)]
    for t in range(3):
        grads = split(jnp.transpose(dqkv_ref[t]))
        for part in range(D // WIDTH):
            din_ref[t, part * WIDTH : (part + 1) * WIDTH] = jnp.transpose(mm3(grads, parts[part]))


def rows_kernel(dqkv_ref, win_ref, dx_ref):
    grads = [split(dqkv_ref[t]) for t in range(3)]
    for part in range(D // WIDTH):
        total = jnp.zeros((PATCH, WIDTH), F32)
        for t in range(3):
            total += mm3(grads[t], split(win_ref[t, part * WIDTH : (part + 1) * WIDTH]), NT)
        dx_ref[part] = total


def call(kernel, outs, *args, scratch=(), flops=10**9):
    size = sum(math.prod(a.shape) * 4 for a in (*args, *outs))
    return pl.pallas_call(
        kernel,
        out_shape=tuple(jax.ShapeDtypeStruct(o, F32) for o in [x.shape for x in outs]),
        in_specs=[pl.BlockSpec(memory_space=pltpu.VMEM)] * len(args),
        out_specs=tuple(pl.BlockSpec(memory_space=pltpu.VMEM) for _ in outs),
        scratch_shapes=[pltpu.VMEM(s, F32) for s in scratch],
        compiler_params=pltpu.CompilerParams(vmem_limit_bytes=40 * 2**20),
        cost_estimate=pl.CostEstimate(flops=flops, bytes_accessed=size, transcendentals=0),
    )(*args)


def of(*shape):
    return jax.ShapeDtypeStruct(shape, F32)


def gather_head(x):
    return lax.all_gather(x, "head", axis=0)


def scatter_head(x):
    return lax.psum_scatter(x, "head", scatter_dimension=0)


def total_over_curve(x):
    for axis in CURVE[::-1]:
        x = lax.psum_scatter(x, axis, scatter_dimension=0, tiled=True)
    for axis in CURVE:
        x = lax.all_gather(x, axis, axis=0, tiled=True)
    return x


def shards(features, input_proj, output_proj, destination, real_points, cotangent):
    peers = lax.axis_size(CURVE)
    up = [(i, (i + 1) % peers) for i in range(peers)]
    down = [(j, i) for i, j in up]

    def exchange(x):
        return lax.all_to_all(x, CURVE, split_axis=0, concat_axis=0, tiled=True)

    def to_patch(low, high):
        return jnp.concatenate([lax.ppermute(high, CURVE, up), low], axis=0)

    def from_patch(x):
        return x[HALF:], lax.ppermute(x[:HALF], CURVE, down)

    sorted_rows, local, slot = call(
        functools.partial(sort_kernel, PATCH // peers), [of(PATCH, WIDTH), of(1, PATCH), of(1, PATCH)],
        destination.reshape(1, PATCH), features,
    )
    local = exchange(local.reshape(PATCH)).reshape(1, PATCH)
    arrived = exchange(sorted_rows)
    win = jnp.transpose(input_proj, (1, 0, 2))
    cot = gather_head(to_patch(cotangent[:HALF], cotangent[HALF:]))
    valid = to_patch(real_points[:HALF], real_points[HALF:])
    bias = jnp.broadcast_to(jnp.where(valid > 0, 0.0, -jnp.inf).astype(F32)[:, None], (PATCH, WIDTH))
    (grad_attended,) = call(cot_kernel, [of(PATCH, WIDTH)], cot, output_proj)
    low, high = call(place_kernel, [of(HALF, WIDTH)] * 2, local, arrived)
    x = gather_head(to_patch(low, high))
    qkv, attended, lse, out = call(
        forward_kernel,
        [of(3, PATCH, WIDTH), of(WIDTH, PATCH), of(HERE, PATCH), of(D // WIDTH, PATCH, WIDTH)],
        x, win, output_proj, bias, scratch=[(WIDTH, PATCH)],
    )
    branch_out = jnp.concatenate(from_patch(scatter_head(out)), axis=0)
    (dqkv,) = call(
        backward_kernel, [of(3, PATCH, WIDTH)], qkv, attended, lse, grad_attended, bias,
        scratch=[(WIDTH, PATCH)] * 3,
    )
    (dx,) = call(rows_kernel, [of(D // WIDTH, PATCH, WIDTH)], dqkv, win)
    din, dout = call(
        weights_kernel, [of(3, D, WIDTH), of(D // WIDTH, WIDTH, WIDTH)], x, dqkv, attended, cot
    )
    low, high = from_patch(scatter_head(dx))
    (back,) = call(unplace_kernel, [of(PATCH, WIDTH)], local, low, high)
    (grad_features,) = call(unsort_kernel, [of(PATCH, WIDTH)], slot, exchange(back))
    both = jnp.concatenate([din.reshape(3 * D, WIDTH), dout.reshape(D, WIDTH)], axis=0)
    both = total_over_curve(both)
    grad_inproj = jnp.transpose(both[: 3 * D].reshape(3, D, WIDTH), (1, 0, 2))
    grad_outproj = jnp.transpose(both[3 * D :].reshape(D // WIDTH, WIDTH, WIDTH), (1, 0, 2)).reshape(WIDTH, D)
    return (branch_out, grad_features, grad_inproj, grad_outproj)


def solution(mesh):
    curve, head = mesh.devices.shape
    sizes = (curve // 8, 4, 2) if curve >= 16 else (curve // 2, 1, 2)
    fine = jax.sharding.Mesh(mesh.devices.reshape(*sizes, head), CURVE + ("head",))
    return jax.shard_map(
        shards,
        mesh=fine,
        in_specs=(
            P(CURVE, "head"),
            P(None, None, "head"),
            P("head", None),
            P(CURVE),
            P(CURVE),
            P(CURVE, "head"),
        ),
        out_specs=(P(CURVE, "head"), P(CURVE, "head"), P(None, None, "head"), P("head", None)),
        check_vma=False,
    )
```

time: 710 us -> 365 us (0.51); the launches traced: 701 us -> 364 us
  waiting for transfers between devices: 498 us -> 193 us
  blocking collectives: 0 us -> 65.2 us
  local copies, waits for them, and re-layouts: 58.4 us -> 10.6 us
  matrix products: 43.8 us -> 0 us
  Pallas kernels: 0 us -> 22.5 us
  starting transfers between devices: 74.4 us -> 54.2 us
  other arithmetic: 12.1 us -> 4.69 us
    psum x1 -> x0, waiting for transfers between devices: 324 us -> none  [shards(): grad_inproj, grad_outproj = lax.psum((grad_in_here, grad_out_here), 'curve')]
    all_to_all x3 -> x2, waiting for transfers between devices: 91.6 us -> 19.6 us  [exchange(): return lax.all_to_all(x, CURVE, split_axis=0, concat_axis=0, tiled=True)]
    reduce_scatter x2 -> x5, waiting for transfers between devices: 63.1 us -> 128 us  [the longest x3 86.8 us: total_over_curve(): x = lax.psum_scatter(x, axis, scatter_dimension=0, tiled=True)]
    dot_general x20 -> x0, matrix products: 43.8 us -> none  [the longest x4 8.11 us: attend(): jnp.einsum('qhe,khe->hqk', queries, key_rows, precision=highest) * scaling]
    all_to_all x0 -> x1, blocking collectives: none -> 32.6 us  [exchange(): return lax.all_to_all(x, CURVE, split_axis=0, concat_axis=0, tiled=True)]
    all_gather x0 -> x2, blocking collectives: none -> 32.6 us  [total_over_curve(): x = lax.all_gather(x, axis, axis=0, tiled=True)]
    all_to_all x3 -> x2, starting transfers between devices: 53.9 us -> 22.2 us  [exchange(): return lax.all_to_all(x, CURVE, split_axis=0, concat_axis=0, tiled=True)]
    scatter x3 -> x0, local copies, waits for them, and re-layouts: 27.4 us -> none  [the longest x2 13.9 us: shards(): grad_morton = jnp.zeros_like(grad_qkv).at[sorting].set(returned)]
  transfers between devices with their start and end apart: 14 -> 15, of which waited for: 9 -> 13; matrix products, arithmetic and copies ran while one was open for 7% -> 2% of each run, Pallas kernels for 0% -> 2%
where the time goes in v1:
time: 365 us; the launch traced here: 364 us
  waiting for transfers between devices  193 us (53%)
  blocking collectives  65.2 us (18%)
  starting transfers between devices  54.2 us (15%)
  Pallas kernels  22.5 us (6%)
  between operations  14.3 us (4%)
  local copies, waits for them, and re-layouts  10.6 us (3%)
  other arithmetic  4.69 us (1%)
    reduce_scatter x3, waiting for transfers between devices, total_over_curve(): x = lax.psum_scatter(x, axis, scatter_dimension=0, tiled=True)  86.8 us
    reduce_scatter x2, waiting for transfers between devices, scatter_head(): return lax.psum_scatter(x, 'head', scatter_dimension=0)  41.7 us
    all_to_all x1, blocking collectives, exchange(): return lax.all_to_all(x, CURVE, split_axis=0, concat_axis=0, tiled=True)  32.6 us
    all_gather x2, blocking collectives, total_over_curve(): x = lax.all_gather(x, axis, axis=0, tiled=True)  32.6 us
    pallas_call x9, Pallas kernels, call(): pl.pallas_call(kernel, out_shape=tuple((jax.ShapeDtypeStruct(o, F32) for...  22.5 us
    all_to_all x2, starting transfers between devices, exchange(): return lax.all_to_all(x, CURVE, split_axis=0, concat_axis=0, tiled=True)  22.2 us
    all_to_all x2, waiting for transfers between devices, exchange(): return lax.all_to_all(x, CURVE, split_axis=0, concat_axis=0, tiled=True)  19.6 us
    ppermute x2, starting transfers between devices, from_patch(): return (x[HALF:], lax.ppermute(x[:HALF], CURVE, down))  18.2 us
  transfers between devices with their start and end apart: 15, of which 13 were waited for; matrix products, arithmetic and copies ran while one was open for 2% of the time, Pallas kernels for 2%

profile of v1, /device:TPU:1, one launch (start us, length us, event | category | flops | bytes accessed | tf_op | source)
XLA Modules:
  0.0 364.4 jit_solution(1804212285537101412)
XLA Ops:
  8.2 4.5 %collective-permute-start.3 = (f32[256,128]{1,0:T(8,128)S(1)}, f32[256,128]{1,0:T(8,128)S(1)}, u32[]{:S(2)}, u32[]{:S(2)}) collective-permute-start(f32[256,128]{1,0:T(8,128)S(1)} %get-tuple-element.28), channel_id=1, source_target_pairs={{0,4},{4,8},{8,12},{12,16},{16,20},{20,24},{24,28},{28,32},{32,36}... | collective-permute-start | bytes 393224 | tf_op jit(solution)/shard_map/ppermute | solution.py:250
  12.7 5.1 %collective-permute-done.3 = f32[256,128]{1,0:T(8,128)S(1)} collective-permute-done((f32[256,128]{1,0:T(8,128)S(1)}, f32[256,128]{1,0:T(8,128)S(1)}, u32[]{:S(2)}, u32[]{:S(2)}) %collective-permute-start.3) | collective-permute-done | bytes 131104 | tf_op jit(solution)/shard_map/ppermute | solution.py:250
  19.5 1.5 shard_map.93
  22.3 32.6 %all_to_all.31 = f32[128,4,1]{1,2,0:T(1,128)S(1)} all-to-all(f32[128,4,1]{1,2,0:T(1,128)S(1)} %bitcast.44), channel_id=1, replica_groups=mesh['z'=16,'x'=4,'core'=2,'head'=4] {'z','x','core'}, dimensions={0} | all-to-all | bytes 4096 | tf_op jit(solution)/shard_map/all_to_all | solution.py:247
  54.9 5.7 %all-to-all-start.1 = ((f32[128,4,128]{2,1,0:T(4,128)}), f32[128,4,128]{2,1,0:T(4,128)S(1)}, u32[]{:S(2)}, u32[]{:S(2)}) async-start(f32[128,4,128]{2,1,0:T(4,128)} %bitcast.2), calls=%async_computation.1 | async-start | bytes 524288 | tf_op jit(solution)/shard_map/all_to_all | solution.py:247
  61.6 19.6 %all-to-all-done.1 = f32[128,4,128]{2,1,0:T(4,128)S(1)} async-done(((f32[128,4,128]{2,1,0:T(4,128)}), f32[128,4,128]{2,1,0:T(4,128)S(1)}, u32[]{:S(2)}, u32[]{:S(2)}) %all-to-all-start.1) | async-done | bytes 262176 | tf_op jit(solution)/shard_map/all_to_all | solution.py:247
  81.8 4.4 %collective-permute-start = (f32[256,128]{1,0:T(8,128)S(1)}, f32[256,128]{1,0:T(8,128)S(1)}, u32[]{:S(2)}, u32[]{:S(2)}) collective-permute-start(f32[256,128]{1,0:T(8,128)S(1)} %get-tuple-element.17), channel_id=1, source_target_pairs={{0,4},{4,8},{8,12},{12,16},{16,20},{20,24},{24,28},{28,32},{32,36}... | collective-permute-start | bytes 393224 | tf_op jit(solution)/shard_map/ppermute | solution.py:250
  86.2 1.9 collective-permute-done
  89.6 4.5 %collective-permute-start.1 = (s32[256]{0:T(256)S(1)}, s32[256]{0:T(256)S(1)}, u32[]{:S(2)}, u32[]{:S(2)}) collective-permute-start(s32[256]{0:T(256)S(1)} %get-tuple-element.32), channel_id=1, source_target_pairs={{0,4},{4,8},{8,12},{12,16},{16,20},{20,24},{24,28},{28,32},{32,36}... | collective-permute-start | bytes 3080 | tf_op jit(solution)/shard_map/ppermute | solution.py:250
  94.1 1.7 collective-permute-done.1
  95.9 1.2 copy-done
  97.7 18.0 %all-gather.8.cloned.1.call-done = f32[2048,128]{1,0:T(8,128)} async-done(((f32[512,128]{1,0:T(8,128)}), f32[2048,128]{1,0:T(8,128)}) %all-gather.8.cloned.1.call-update) | async-done | bytes 1048592 | tf_op jit(solution)/shard_map/all_gather | solution.py:226
  115.8 1.2 copy-done.2
  117.0 6.7 %shard_map.95 = (f32[3,512,128]{2,1,0:T(8,128)S(1)}, f32[128,512]{1,0:T(8,128)S(1)}, f32[4,512]{1,0:T(4,128)S(1)}, f32[4,512,128]{2,1,0:T(8,128)}) custom-call(f32[4,512,128]{2,1,0:T(8,128)S(1)} %bitcast.35, f32[3,512,128]{2,1,0:T(8,128)S(1)} %bitcast.37, f32[128,512]{1,0:T(8,128)S(1)} %copy-done.6, f32[512,128]{1,0:T(8,128)S(1)} %broadcast_in_dim.16.bias_ref), custom_call_target="tpu_custom_call" | custom-call | flops 1000000000 | bytes 4464640 | tf_op jit(solution)/shard_map/pallas_call | solution.py:210
  123.7 6.3 %shard_map.97.dqkv_ref = f32[3,512,128]{2,1,0:T(8,128)S(1)} custom-call(f32[3,512,128]{2,1,0:T(8,128)S(1)} %get-tuple-element.21.qkv_ref, f32[128,512]{1,0:T(8,128)S(1)} %get-tuple-element.22.att_ref, f32[4,512]{1,0:T(4,128)S(1)} %get-tuple-element.23.lse_ref, f32[512,128]{1,0:T(8,128)S(1)} %shard_map.96.grad_ref, f32[512,128]{1,0:T(8,128)S(1)} %broadcast_in_dim.16.bias_ref), custom_call_target="tpu_custom_call" | custom-call | flops 1000000000 | bytes 2367488 | tf_op jit(solution)/shard_map/pallas_call | solution.py:210
  130.0 1.9 shard_map.101
  133.0 21.9 %reduce-scatter.10.cloned.1.call-done = f32[1024,128]{1,0:T(8,128)} async-done(((f32[2048,128]{1,0:T(8,128)}), f32[1024,128]{1,0:T(8,128)}) %reduce-scatter.10.cloned.1.call-update) | async-done | bytes 524304 | tf_op jit(solution)/shard_map/reduce_scatter | solution.py:235
  155.0 2.4 shard_map.98
  157.4 27.7 %reduce-scatter.12.cloned.1.call-done = f32[256,128]{1,0:T(8,128)} async-done(((f32[1024,128]{1,0:T(8,128)}), f32[256,128]{1,0:T(8,128)}) %reduce-scatter.12.cloned.1.call-update) | async-done | bytes 131088 | tf_op jit(solution)/shard_map/reduce_scatter | solution.py:235
  185.9 33.5 %reduce-scatter.8.cloned.1.call-done = f32[1,512,128]{2,1,0:T(8,128)} async-done(((f32[4,512,128]{2,1,0:T(8,128)}), f32[1,512,128]{2,1,0:T(8,128)}) %reduce-scatter.8.cloned.1.call-update) | async-done | bytes 262160 | tf_op jit(solution)/shard_map/reduce_scatter | solution.py:230
  220.4 3.9 %collective-permute-start.4 = (f32[256,128]{1,0:T(8,128)S(1)}, f32[256,128]{1,0:T(8,128)S(1)}, u32[]{:S(2)}, u32[]{:S(2)}) collective-permute-start(f32[256,128]{1,0:T(8,128)S(1)} %get-tuple-element.26), channel_id=1, source_target_pairs={{4,0},{8,4},{12,8},{16,12},{20,16},{24,20},{28,24},{32,28},{36,32}... | collective-permute-start | bytes 393224 | tf_op jit(solution)/shard_map/ppermute | solution.py:253
  224.4 3.7 %collective-permute-done.4.high_ref = f32[256,128]{1,0:T(8,128)S(1)} collective-permute-done((f32[256,128]{1,0:T(8,128)S(1)}, f32[256,128]{1,0:T(8,128)S(1)}, u32[]{:S(2)}, u32[]{:S(2)}) %collective-permute-start.4) | collective-permute-done | bytes 131104 | tf_op jit(solution)/shard_map/ppermute | solution.py:253
  228.0 1.3 shard_map.99
  229.3 16.5 %all-to-all-start.2 = ((f32[128,4,128]{2,1,0:T(4,128)}), f32[128,4,128]{2,1,0:T(4,128)S(1)}, u32[]{:S(2)}, u32[]{:S(2)}) async-start(f32[128,4,128]{2,1,0:T(4,128)} %bitcast.11), calls=%async_computation.4 | async-start | bytes 524288 | tf_op jit(solution)/shard_map/all_to_all | solution.py:247
  245.9 37.2 %reduce-scatter.14.cloned.1.call-done = f32[16,128]{1,0:T(8,128)} async-done(((f32[256,128]{1,0:T(8,128)}), f32[16,128]{1,0:T(8,128)}) %reduce-scatter.14.cloned.1.call-update) | async-done | bytes 8208 | tf_op jit(solution)/shard_map/reduce_scatter | solution.py:235
  283.1 21.5 %all_gather.25 = f32[256,128]{1,0:T(8,128)S(1)} all-gather(f32[16,128]{1,0:T(8,128)} %reduce-scatter.14.cloned.1.call-done), channel_id=1, replica_groups=mesh['z'=16,'x'=4,'core'=2,'head'=4] {'z'}, dimensions={0}, use_global_device_ids=true | all-gather | bytes 139264 | tf_op jit(solution)/shard_map/all_gather | solution.py:237
  304.6 11.1 %all_gather.26 = f32[1024,128]{1,0:T(8,128)} all-gather(f32[256,128]{1,0:T(8,128)S(1)} %all_gather.25), channel_id=1, replica_groups=mesh['z'=16,'x'=4,'core'=2,'head'=4] {'x'}, dimensions={0}, use_global_device_ids=true | all-gather | bytes 655360 | tf_op jit(solution)/shard_map/all_gather | solution.py:237
  315.7 8.1 %reduce-scatter.6.cloned.1.call-done = f32[1,512,128]{2,1,0:T(8,128)} async-done(((f32[4,512,128]{2,1,0:T(8,128)}), f32[1,512,128]{2,1,0:T(8,128)}) %reduce-scatter.6.cloned.1.call-update) | async-done | bytes 262160 | tf_op jit(solution)/shard_map/reduce_scatter | solution.py:230
  324.9 14.3 %collective-permute-start.2 = (f32[256,128]{1,0:T(8,128)S(1)}, f32[256,128]{1,0:T(8,128)S(1)}, u32[]{:S(2)}, u32[]{:S(2)}) collective-permute-start(f32[256,128]{1,0:T(8,128)S(1)} %get-tuple-element.31), channel_id=1, source_target_pairs={{4,0},{8,4},{12,8},{16,12},{20,16},{24,20},{28,24},{32,28},{36,32}... | collective-permute-start | bytes 393224 | tf_op jit(solution)/shard_map/ppermute | solution.py:253
  339.2 3.5 collective-permute-done.2
  343.4 1.3 shard_map.100
  344.7 10.1 %all-gather.6.cloned.1.call-done = f32[2048,128]{1,0:T(8,128)} async-done(((f32[1024,128]{1,0:T(8,128)}), f32[2048,128]{1,0:T(8,128)}) %all-gather.6.cloned.1.call-update) | async-done | bytes 1048592 | tf_op jit(solution)/shard_map/all_gather | solution.py:237
  (58 shorter events, 15.2 us)
Async XLA Ops:
  7.2 88.7 %all-gather.10.cloned.1.call-start = ((), (), s32[]{:S(2)}) async-start(), calls=%async_computation.15 | async-start | bytes 1310720 | tf_op jit(solution)/shard_map/all_gather | solution.py:226
  8.2 9.6 %collective-permute-start.3 = (f32[256,128]{1,0:T(8,128)S(1)}, f32[256,128]{1,0:T(8,128)S(1)}, u32[]{:S(2)}, u32[]{:S(2)}) collective-permute-start(f32[256,128]{1,0:T(8,128)S(1)} %get-tuple-element.28), channel_id=1, source_target_pairs={{0,4},{4,8},{8,12},{12,16},{16,20},{20,24},{24,28},{28,32},{32,36}... | collective-permute-start | bytes 393224 | tf_op jit(solution)/shard_map/ppermute | solution.py:250
  18.5 0.9 copy-start.5
  18.5 1.0 copy-start.7
  54.9 26.3 %all-to-all-start.1 = ((f32[128,4,128]{2,1,0:T(4,128)}), f32[128,4,128]{2,1,0:T(4,128)S(1)}, u32[]{:S(2)}, u32[]{:S(2)}) async-start(f32[128,4,128]{2,1,0:T(4,128)} %bitcast.2), calls=%async_computation.1 | async-start | bytes 524288 | tf_op jit(solution)/shard_map/all_to_all | solution.py:247
  60.6 55.0 %all-gather.8.cloned.1.call-start = ((), (), s32[]{:S(2)}) async-start(), calls=%async_computation.14 | async-start | bytes 1310720 | tf_op jit(solution)/shard_map/all_gather | solution.py:226
  81.8 6.4 %collective-permute-start = (f32[256,128]{1,0:T(8,128)S(1)}, f32[256,128]{1,0:T(8,128)S(1)}, u32[]{:S(2)}, u32[]{:S(2)}) collective-permute-start(f32[256,128]{1,0:T(8,128)S(1)} %get-tuple-element.17), channel_id=1, source_target_pairs={{0,4},{4,8},{8,12},{12,16},{16,20},{20,24},{24,28},{28,32},{32,36}... | collective-permute-start | bytes 393224 | tf_op jit(solution)/shard_map/ppermute | solution.py:250
  88.9 7.0 %copy-start.6 = (f32[128,512]{1,0:T(8,128)S(1)}, f32[128,512]{1,0:T(8,128)}, u32[]{:S(2)}) copy-start(f32[128,512]{1,0:T(8,128)} %wout_ref.3) | copy-start | bytes 786436
  88.9 0.7 copy-start.9
  88.9 66.0 %reduce-scatter.10.cloned.1.call-start = ((), (), s32[]{:S(2)}) async-start(), calls=%async_computation.10 | async-start | bytes 1572864 | tf_op jit(solution)/shard_map/reduce_scatter | solution.py:235
  89.6 6.2 %collective-permute-start.1 = (s32[256]{0:T(256)S(1)}, s32[256]{0:T(256)S(1)}, u32[]{:S(2)}, u32[]{:S(2)}) collective-permute-start(s32[256]{0:T(256)S(1)} %get-tuple-element.32), channel_id=1, source_target_pairs={{0,4},{4,8},{8,12},{12,16},{16,20},{20,24},{24,28},{28,32},{32,36}... | collective-permute-start | bytes 3080 | tf_op jit(solution)/shard_map/ppermute | solution.py:250
  95.9 1.2 copy-start
  97.1 18.7 %copy-start.4 = (f32[512,3,128]{2,0,1:T(8,128)S(1)}, f32[512,3,128]{2,0,1:T(8,128)}, u32[]{:S(2)}) copy-start(f32[512,3,128]{2,0,1:T(8,128)} %param.7) | copy-start | bytes 2359300
  115.8 1.2 copy-start.2
  123.7 6.3 %copy-start.1 = (f32[2048,128]{1,0:T(8,128)S(1)}, f32[2048,128]{1,0:T(8,128)}, u32[]{:S(2)}) copy-start(f32[2048,128]{1,0:T(8,128)} %all-gather.10.cloned.1.call-done) | copy-start | bytes 3145732
  123.7 6.3 %copy-start.3 = (f32[2048,128]{1,0:T(8,128)S(1)}, f32[2048,128]{1,0:T(8,128)}, u32[]{:S(2)}) copy-start(f32[2048,128]{1,0:T(8,128)} %all-gather.8.cloned.1.call-done) | copy-start | bytes 3145732
  133.0 52.1 %reduce-scatter.12.cloned.1.call-start = ((), (), s32[]{:S(2)}) async-start(), calls=%async_computation.11 | async-start | bytes 655360 | tf_op jit(solution)/shard_map/reduce_scatter | solution.py:235
  154.9 64.5 %reduce-scatter.8.cloned.1.call-start = ((), (), s32[]{:S(2)}) async-start(), calls=%async_computation.9 | async-start | bytes 1310720 | tf_op jit(solution)/shard_map/reduce_scatter | solution.py:230
  157.3 125.8 %reduce-scatter.14.cloned.1.call-start = ((), (), s32[]{:S(2)}) async-start(), calls=%async_computation.12 | async-start | bytes 139264 | tf_op jit(solution)/shard_map/reduce_scatter | solution.py:235
  185.1 138.8 %reduce-scatter.6.cloned.1.call-start = ((), (), s32[]{:S(2)}) async-start(), calls=%async_computation.8 | async-start | bytes 1310720 | tf_op jit(solution)/shard_map/reduce_scatter | solution.py:230
  220.4 7.6 %collective-permute-start.4 = (f32[256,128]{1,0:T(8,128)S(1)}, f32[256,128]{1,0:T(8,128)S(1)}, u32[]{:S(2)}, u32[]{:S(2)}) collective-permute-start(f32[256,128]{1,0:T(8,128)S(1)} %get-tuple-element.26), channel_id=1, source_target_pairs={{4,0},{8,4},{12,8},{16,12},{20,16},{24,20},{28,24},{32,28},{36,32}... | collective-permute-start | bytes 393224 | tf_op jit(solution)/shard_map/ppermute | solution.py:253
  229.3 114.1 %all-to-all-start.2 = ((f32[128,4,128]{2,1,0:T(4,128)}), f32[128,4,128]{2,1,0:T(4,128)S(1)}, u32[]{:S(2)}, u32[]{:S(2)}) async-start(f32[128,4,128]{2,1,0:T(4,128)} %bitcast.11), calls=%async_computation.4 | async-start | bytes 524288 | tf_op jit(solution)/shard_map/all_to_all | solution.py:247
  245.8 108.9 %all-gather.6.cloned.1.call-start = ((), (), s32[]{:S(2)}) async-start(), calls=%async_computation.13 | async-start | bytes 1572864 | tf_op jit(solution)/shard_map/all_gather | solution.py:237
  324.9 17.8 %collective-permute-start.2 = (f32[256,128]{1,0:T(8,128)S(1)}, f32[256,128]{1,0:T(8,128)S(1)}, u32[]{:S(2)}, u32[]{:S(2)}) collective-permute-start(f32[256,128]{1,0:T(8,128)S(1)} %get-tuple-element.31), channel_id=1, source_target_pairs={{4,0},{8,4},{12,8},{16,12},{20,16},{24,20},{28,24},{32,28},{36,32}... | collective-permute-start | bytes 393224 | tf_op jit(solution)/shard_map/ppermute | solution.py:253
  354.8 0.9 slice-start
  354.8 1.8 copy-start.8
Sparse Core Ops, SparseCore 0:
  18.7 33.5 all-gather.9
  89.0 26.5 all-gather.7
  133.1 21.7 reduce-scatter.9
  157.8 27.2 reduce-scatter.11
  188.0 31.3 reduce-scatter.7
  222.1 61.0 reduce-scatter.13
  286.2 37.6 reduce-scatter.5
  326.0 28.7 all-gather.5

commit v2 on v1

--- a/solution.py
+++ b/solution.py
@@ -52,60 +52,95 @@
 
 
 def column(row):
-    return jnp.transpose(jnp.broadcast_to(row, (WIDTH, PATCH)))
-
-
-def wide(col):
-    return jnp.concatenate([col] * (PATCH // WIDTH), axis=1)
-
-
-def iota(dim):
-    return lax.broadcasted_iota(jnp.int32, (PATCH, PATCH), dim).astype(F32)
-
-
-def rows_to_slots(slot_row):
-    return jnp.where(iota(0) == slot_row, 1.0, 0.0).astype(BF)
-
-
-def slots_to_rows(slot_row):
-    return jnp.where(wide(column(slot_row)) == iota(1), 1.0, 0.0).astype(BF)
-
-
-def sort_kernel(each, dest_ref, feat_ref, sorted_ref, local_ref, slot_ref):
+    return jnp.transpose(jnp.broadcast_to(row, (WIDTH, row.shape[1])))
+
+
+def wide(col, width=PATCH):
+    return jnp.concatenate([col] * (width // WIDTH), axis=1)
+
+
+def iota(dim, shape=(PATCH, PATCH)):
+    return lax.broadcasted_iota(jnp.int32, shape, dim).astype(F32)
+
+
+def one_hot(condition):
+    return jnp.where(condition, 1.0, 0.0).astype(BF)
+
+
+def spread(each, rows, arrived):
+    total = arrived.shape[0]
+    place = iota(0, (rows, total))
+    peer = jnp.floor((place + 0.5) * (1.0 / each))
+    pick = one_hot(iota(1, (rows, total)) == peer * (each + 1) + each)
+    high, low = split(arrived)
+    listed = mm(pick, high) + mm(pick, low)
+    place = iota(0, (rows, WIDTH))
+    turn = place - jnp.floor((place + 0.5) * (1.0 / each)) * each
+    mine = jnp.where(iota(1, (rows, WIDTH)) == turn, listed, 0.0)
+    return jnp.broadcast_to(jnp.sum(mine, axis=1, keepdims=True), (rows, WIDTH))
+
+
+def sort_kernel(each, dest_ref, feat_ref, message_ref, slot_ref):
     dest = dest_ref[...]
     block = dest // PATCH
     local = (dest - block * PATCH).astype(F32)
     block = block.astype(F32)
-    lower = iota(0) < iota(1)
-    same = (wide(column(block)) == block) & lower
+    same = (wide(column(block)) == block) & (iota(0) < iota(1))
     rank = jnp.sum(jnp.where(same, 1.0, 0.0), axis=0, keepdims=True)
-    slot = block * each + rank
-    slot_ref[...] = slot
-    back = wide(column(slot)) == iota(1)
-    local_ref[...] = jnp.sum(jnp.where(back, wide(column(local)), 0.0), axis=0, keepdims=True)
-    sorted_ref[...] = select_rows(rows_to_slots(slot), feat_ref[...])
-
-
-def place_kernel(local_ref, arrived_ref, low_ref, high_ref):
-    placed = select_rows(rows_to_slots(local_ref[...]), arrived_ref[...])
+    slot_ref[...] = block * each + rank
+    shape = (message_ref.shape[0], PATCH)
+    rows = iota(0, shape)
+    first = block * (each + 1)
+    lists = jnp.where(iota(1, (PATCH, WIDTH)) == column(rank), column(local), 0.0)
+    high, low = split(lists)
+    last = one_hot(rows == first + each)
+    message = select_rows(one_hot(rows == first + rank), feat_ref[...])
+    message_ref[...] = message + (mm(last, high) + mm(last, low))
+
+
+def positions_kernel(each, arrived_ref, position_ref):
+    position_ref[...] = spread(each, PATCH, arrived_ref[...])
+
+
+def place_kernel(each, arrived_ref, low_ref, high_ref):
+    arrived = arrived_ref[...]
+    total = arrived.shape[0]
+    place = iota(0, (total, total))
+    peer = jnp.floor((place + 0.5) * (1.0 / (each + 1)))
+    pick = one_hot(iota(1, (total, total)) == peer * (each + 1) + each)
+    high, low = split(arrived)
+    listed = mm(pick, high) + mm(pick, low)
+    place = iota(0, (total, WIDTH))
+    turn = place - jnp.floor((place + 0.5) * (1.0 / (each + 1))) * (each + 1)
+    mine = jnp.where((iota(1, (total, WIDTH)) == turn) & (turn < each), listed, 0.0)
+    mine = jnp.sum(mine, axis=1, keepdims=True) - jnp.where(turn < each, 0.0, 1.0)
+    row = jnp.transpose(jnp.broadcast_to(mine, (total, WIDTH)))[:1]
+    placed = select_rows(one_hot(iota(0, (PATCH, total)) == row), arrived)
     low_ref[...] = placed[:HALF]
     high_ref[...] = placed[HALF:]
 
 
-def unplace_kernel(local_ref, low_ref, high_ref, out_ref):
-    grads = jnp.concatenate([low_ref[...], high_ref[...]], axis=0)
-    out_ref[...] = select_rows(slots_to_rows(local_ref[...]), grads)
+def add_kernel(parts_ref, total_ref):
+    total_ref[...] = parts_ref[0] + parts_ref[1] + (parts_ref[2] + parts_ref[3])
+
+
+def unplace_kernel(position_ref, low_ref, high_ref, out_ref):
+    low = low_ref[0] + low_ref[1] + (low_ref[2] + low_ref[3])
+    grads = jnp.concatenate([low, high_ref[...]], axis=0)
+    out_ref[...] = select_rows(one_hot(wide(position_ref[...]) == iota(1)), grads)
 
 
 def unsort_kernel(slot_ref, returned_ref, out_ref):
-    out_ref[...] = select_rows(slots_to_rows(slot_ref[...]), returned_ref[...])
-
-
-def cot_kernel(cot_ref, wout_ref, grad_ref):
+    pick = one_hot(wide(column(slot_ref[...])) == iota(1))
+    out_ref[...] = select_rows(pick, returned_ref[...])
+
+
+def cot_kernel(cot_ref, wout_ref, low_ref, high_ref):
     total = jnp.zeros((PATCH, WIDTH), F32)
     for part in range(D // WIDTH):
         total += mm3(split(cot_ref[part]), split(wout_ref[:, part * WIDTH : (part + 1) * WIDTH]), NT)
-    grad_ref[...] = total
+    low_ref[...] = total[:HALF]
+    high_ref[...] = total[HALF:]
 
 
 def head_mask(head):
@@ -122,7 +157,7 @@
     )
 
 
-def forward_kernel(x_ref, win_ref, wout_ref, bias_ref, qkv_ref, att_ref, lse_ref, out_ref, vt_ref):
+def forward_kernel(x_ref, win_ref, bias_ref, qkv_ref, att_ref, lse_ref, early_ref, late_ref, vt_ref):
     parts = [split(x_ref[part]) for part in range(D // WIDTH)]
     for t in range(3):
         total = jnp.zeros((PATCH, WIDTH), F32)
@@ -148,9 +183,8 @@
         return carry
 
     lax.fori_loop(0, HERE, one, 0)
-    attended = split(jnp.transpose(att_ref[...]))
-    for part in range(D // WIDTH):
-        out_ref[part] = mm3(attended, split(wout_ref[:, part * WIDTH : (part + 1) * WIDTH]))
+    late_ref[...] = jnp.transpose(att_ref[:, HALF:])
+    early_ref[...] = jnp.transpose(att_ref[:, :HALF])
 
 
 def backward_kernel(qkv_ref, att_ref, lse_ref, grad_ref, bias_ref, dqkv_ref, kt_ref, gt_ref, dqt_ref):
@@ -185,10 +219,16 @@
     dqkv_ref[0] = jnp.transpose(dqt_ref[...])
 
 
-def weights_kernel(x_ref, dqkv_ref, att_ref, cot_ref, din_ref, dout_ref):
-    attended = split(att_ref[...])
+def output_kernel(low_ref, high_ref, wout_ref, cot_ref, out_ref, dout_ref):
+    attended = jnp.concatenate([low_ref[...], high_ref[...]], axis=0)
+    parts = split(attended)
+    turned = split(jnp.transpose(attended))
     for part in range(D // WIDTH):
-        dout_ref[part] = mm3(attended, split(cot_ref[part]))
+        out_ref[part] = mm3(parts, split(wout_ref[:, part * WIDTH : (part + 1) * WIDTH]))
+        dout_ref[part] = mm3(turned, split(cot_ref[part]))
+
+
+def weights_kernel(x_ref, dqkv_ref, din_ref):
     parts = [split(x_ref[part]) for part in range(D // WIDTH)]
     for t in range(3):
         grads = split(jnp.transpose(dqkv_ref[t]))
@@ -222,66 +262,70 @@
     return jax.ShapeDtypeStruct(shape, F32)
 
 
-def gather_head(x):
-    return lax.all_gather(x, "head", axis=0)
-
-
-def scatter_head(x):
-    return lax.psum_scatter(x, "head", scatter_dimension=0)
+def swap(x, axis):
+    return lax.all_to_all(x, axis, split_axis=0, concat_axis=0, tiled=True)
+
+
+def spread_to(x, axis):
+    peers = lax.axis_size(axis)
+    return swap(jnp.broadcast_to(x[None], (peers,) + x.shape).reshape(-1, WIDTH), axis)
 
 
 def total_over_curve(x):
     for axis in CURVE[::-1]:
-        x = lax.psum_scatter(x, axis, scatter_dimension=0, tiled=True)
+        peers = lax.axis_size(axis)
+        x = jnp.sum(swap(x, axis).reshape(peers, -1, WIDTH), axis=0)
     for axis in CURVE:
-        x = lax.all_gather(x, axis, axis=0, tiled=True)
+        x = spread_to(x, axis)
     return x
 
 
 def shards(features, input_proj, output_proj, destination, real_points, cotangent):
     peers = lax.axis_size(CURVE)
+    each = PATCH // peers
+    message_rows = PATCH + peers
     up = [(i, (i + 1) % peers) for i in range(peers)]
     down = [(j, i) for i, j in up]
 
-    def exchange(x):
-        return lax.all_to_all(x, CURVE, split_axis=0, concat_axis=0, tiled=True)
-
     def to_patch(low, high):
         return jnp.concatenate([lax.ppermute(high, CURVE, up), low], axis=0)
 
-    def from_patch(x):
-        return x[HALF:], lax.ppermute(x[:HALF], CURVE, down)
-
-    sorted_rows, local, slot = call(
-        functools.partial(sort_kernel, PATCH // peers), [of(PATCH, WIDTH), of(1, PATCH), of(1, PATCH)],
+    cot = lax.all_gather(cotangent, "head", axis=0)
+    message, slot = call(
+        functools.partial(sort_kernel, each), [of(message_rows, WIDTH), of(1, PATCH)],
         destination.reshape(1, PATCH), features,
     )
-    local = exchange(local.reshape(PATCH)).reshape(1, PATCH)
-    arrived = exchange(sorted_rows)
+    arrived = swap(message.reshape(message_rows, 1, WIDTH), CURVE).reshape(message_rows, WIDTH)
     win = jnp.transpose(input_proj, (1, 0, 2))
-    cot = gather_head(to_patch(cotangent[:HALF], cotangent[HALF:]))
     valid = to_patch(real_points[:HALF], real_points[HALF:])
     bias = jnp.broadcast_to(jnp.where(valid > 0, 0.0, -jnp.inf).astype(F32)[:, None], (PATCH, WIDTH))
-    (grad_attended,) = call(cot_kernel, [of(PATCH, WIDTH)], cot, output_proj)
-    low, high = call(place_kernel, [of(HALF, WIDTH)] * 2, local, arrived)
-    x = gather_head(to_patch(low, high))
-    qkv, attended, lse, out = call(
+    grad_low, grad_high = call(cot_kernel, [of(HALF, WIDTH)] * 2, cot, output_proj)
+    grad_attended = to_patch(grad_low, grad_high)
+    low, high = call(functools.partial(place_kernel, each), [of(HALF, WIDTH)] * 2, arrived)
+    (position,) = call(functools.partial(positions_kernel, each), [of(PATCH, WIDTH)], arrived)
+    x = spread_to(to_patch(low, high), "head").reshape(D // WIDTH, PATCH, WIDTH)
+    qkv, attended, lse, early, late = call(
         forward_kernel,
-        [of(3, PATCH, WIDTH), of(WIDTH, PATCH), of(HERE, PATCH), of(D // WIDTH, PATCH, WIDTH)],
-        x, win, output_proj, bias, scratch=[(WIDTH, PATCH)],
-    )
-    branch_out = jnp.concatenate(from_patch(scatter_head(out)), axis=0)
+        [of(3, PATCH, WIDTH), of(WIDTH, PATCH), of(HERE, PATCH), of(HALF, WIDTH), of(HALF, WIDTH)],
+        x, win, bias, scratch=[(WIDTH, PATCH)],
+    )
     (dqkv,) = call(
         backward_kernel, [of(3, PATCH, WIDTH)], qkv, attended, lse, grad_attended, bias,
         scratch=[(WIDTH, PATCH)] * 3,
     )
+    out, dout = call(
+        output_kernel, [of(D // WIDTH, PATCH, WIDTH), of(D // WIDTH, WIDTH, WIDTH)],
+        late, lax.ppermute(early, CURVE, down), output_proj, cot,
+    )
+    branch_out = lax.psum_scatter(out, "head", scatter_dimension=0)
     (dx,) = call(rows_kernel, [of(D // WIDTH, PATCH, WIDTH)], dqkv, win)
-    din, dout = call(
-        weights_kernel, [of(3, D, WIDTH), of(D // WIDTH, WIDTH, WIDTH)], x, dqkv, attended, cot
-    )
-    low, high = from_patch(scatter_head(dx))
-    (back,) = call(unplace_kernel, [of(PATCH, WIDTH)], local, low, high)
-    (grad_features,) = call(unsort_kernel, [of(PATCH, WIDTH)], slot, exchange(back))
+    (din,) = call(weights_kernel, [of(3, D, WIDTH)], x, dqkv)
+    dx = swap(dx.reshape(-1, WIDTH), "head").reshape(D // WIDTH, PATCH, WIDTH)
+    (early,) = call(add_kernel, [of(HALF, WIDTH)], dx[:, :HALF])
+    (back,) = call(
+        unplace_kernel, [of(PATCH, WIDTH)], position, dx[:, HALF:], lax.ppermute(early, CURVE, down)
+    )
+    (grad_features,) = call(unsort_kernel, [of(PATCH, WIDTH)], slot, swap(back, CURVE))
     both = jnp.concatenate([din.reshape(3 * D, WIDTH), dout.reshape(D, WIDTH)], axis=0)
     both = total_over_curve(both)
     grad_inproj = jnp.transpose(both[: 3 * D].reshape(3, D, WIDTH), (1, 0, 2))

time: 365 us -> 235 us (0.64)
  waiting for transfers between devices: 193 us -> 83.8 us
  blocking collectives: 65.2 us -> 23.3 us
  starting transfers between devices: 54.2 us -> 77.7 us
    reduce_scatter x5 -> x1, waiting for transfers between devices: 128 us -> 0.01 us  [shards(): branch_out = lax.psum_scatter(out, 'head', scatter_dimension=0)]
    all_to_all x2 -> x7, waiting for transfers between devices: 19.6 us -> 72.6 us  [swap(): return lax.all_to_all(x, axis, split_axis=0, concat_axis=0, tiled=True)]
    all_gather x2 -> x0, blocking collectives: 32.6 us -> none  [total_over_curve(): x = lax.all_gather(x, axis, axis=0, tiled=True)]
    all_to_all x2 -> x7, starting transfers between devices: 22.2 us -> 52.8 us  [swap(): return lax.all_to_all(x, axis, split_axis=0, concat_axis=0, tiled=True)]
    all_gather x3 -> x1, waiting for transfers between devices: 28.1 us -> 0.01 us  [shards(): cot = lax.all_gather(cotangent, 'head', axis=0)]
    all_to_all x1 -> x3, blocking collectives: 32.6 us -> 23.3 us  [swap(): return lax.all_to_all(x, axis, split_axis=0, concat_axis=0, tiled=True)]
    ppermute x2, starting transfers between devices: 18.2 us -> 13.9 us  [shards(): lax.ppermute(early, CURVE, down)]
    ppermute x3, waiting for transfers between devices: 8.69 us -> 4.46 us  [to_patch(): return jnp.concatenate([lax.ppermute(high, CURVE, up), low], axis=0)]
  transfers between devices with their start and end apart: 15 -> 14, of which waited for: 13 -> 8; matrix products, arithmetic and copies ran while one was open for 2% -> 2% of each run, Pallas kernels for 2% -> 7%
where the time goes in v2:
time: 235 us; the launch traced here: 233 us
  waiting for transfers between devices  83.8 us (36%)
  starting transfers between devices  77.7 us (33%)
  Pallas kernels  24.8 us (11%)
  blocking collectives  23.3 us (10%)
  between operations  14.3 us (6%)
  local copies, waits for them, and re-layouts  7.55 us (3%)
    all_to_all x7, waiting for transfers between devices, swap(): return lax.all_to_all(x, axis, split_axis=0, concat_axis=0, tiled=True)  72.6 us
    all_to_all x7, starting transfers between devices, swap(): return lax.all_to_all(x, axis, split_axis=0, concat_axis=0, tiled=True)  52.8 us
    pallas_call x12, Pallas kernels, call(): pl.pallas_call(kernel, out_shape=tuple((jax.ShapeDtypeStruct(o, F32) for...  24.8 us
    all_to_all x3, blocking collectives, swap(): return lax.all_to_all(x, axis, split_axis=0, concat_axis=0, tiled=True)  23.3 us
    ppermute x2, starting transfers between devices, shards(): lax.ppermute(early, CURVE, down)  13.9 us
    ppermute x3, starting transfers between devices, to_patch(): return jnp.concatenate([lax.ppermute(high, CURVE, up), low], axis=0)  10.8 us
    ppermute x2, waiting for transfers between devices, shards(): lax.ppermute(early, CURVE, down)  5.39 us
  transfers between devices with their start and end apart: 14, of which 8 were waited for; matrix products, arithmetic and copies ran while one was open for 2% of the time, Pallas kernels for 7%

profile of v2, /device:TPU:1, one launch (start us, length us, event | category | flops | bytes accessed | tf_op | source)
XLA Modules:
  0.0 233.2 jit_solution(14631160589758676822)
XLA Ops:
  8.8 2.0 shard_map.93
  10.8 20.4 %all-to-all-start = ((f32[640,1,128]{2,1,0:T(1,128)}), f32[640,1,128]{2,1,0:T(1,128)S(1)}, u32[]{:S(2)}, u32[]{:S(2)}) async-start(f32[640,1,128]{2,1,0:T(1,128)} %bitcast.2), calls=%async_computation | async-start | bytes 655360 | tf_op jit(solution)/shard_map/all_to_all | solution.py:266
  31.9 22.3 %all-to-all-done = f32[640,1,128]{2,1,0:T(1,128)S(1)} async-done(((f32[640,1,128]{2,1,0:T(1,128)}), f32[640,1,128]{2,1,0:T(1,128)S(1)}, u32[]{:S(2)}, u32[]{:S(2)}) %all-to-all-start) | async-done | bytes 327712 | tf_op jit(solution)/shard_map/all_to_all | solution.py:266
  54.2 1.6 shard_map.94
  55.8 4.2 %collective-permute-start = (f32[256,128]{1,0:T(8,128)S(1)}, f32[256,128]{1,0:T(8,128)S(1)}, u32[]{:S(2)}, u32[]{:S(2)}) collective-permute-start(f32[256,128]{1,0:T(8,128)S(1)} %get-tuple-element.18), channel_id=1, source_target_pairs={{0,4},{4,8},{8,12},{12,16},{16,20},{20,24},{24,28},{28,32},{32,36}... | collective-permute-start | bytes 393224 | tf_op jit(solution)/shard_map/ppermute | solution.py:291
  60.0 1.9 collective-permute-done
  62.9 4.3 %all-to-all-start.1 = ((f32[4,512,128]{2,1,0:T(8,128)}), f32[4,512,128]{2,1,0:T(8,128)S(1)}, u32[]{:S(2)}, u32[]{:S(2)}) async-start(f32[4,512,128]{2,1,0:T(8,128)} %broadcast_in_dim.22), calls=%async_computation.1 | async-start | bytes 2097152 | tf_op jit(solution)/shard_map/all_to_all | solution.py:266
  69.1 4.8 %collective-permute-start.3 = (f32[256,128]{1,0:T(8,128)S(1)}, f32[256,128]{1,0:T(8,128)S(1)}, u32[]{:S(2)}, u32[]{:S(2)}) collective-permute-start(f32[256,128]{1,0:T(8,128)S(1)} %get-tuple-element.27), channel_id=1, source_target_pairs={{0,4},{4,8},{8,12},{12,16},{16,20},{20,24},{24,28},{28,32},{32,36}... | collective-permute-start | bytes 393224 | tf_op jit(solution)/shard_map/ppermute | solution.py:291
  73.9 1.9 collective-permute-start.1
  75.8 2.5 %collective-permute-done.1 = s32[256]{0:T(256)S(1)} collective-permute-done((s32[256]{0:T(256)S(1)}, s32[256]{0:T(256)S(1)}, u32[]{:S(2)}, u32[]{:S(2)}) %collective-permute-start.1) | collective-permute-done | bytes 1056 | tf_op jit(solution)/shard_map/ppermute | solution.py:291
  78.5 5.2 %shard_map.95 = (f32[3,512,128]{2,1,0:T(8,128)S(1)}, f32[128,512]{1,0:T(8,128)S(1)}, f32[4,512]{1,0:T(4,128)S(1)}, f32[256,128]{1,0:T(8,128)S(1)}, f32[256,128]{1,0:T(8,128)S(1)}) custom-call(f32[4,512,128]{2,1,0:T(8,128)S(1)} %all-to-all-done.1.x_ref, f32[3,512,128]{2,1,0:T(8,128)S(1)} %bitcast.32, f32[512,128]{1,0:T(8,128)S(1)} %broadcast_in_dim.45.bias_ref), custom_call_target="tpu_custom_call" | custom-call | flops 1000000000 | bytes 3416064 | tf_op jit(solution)/shard_map/pallas_call | solution.py:250
  83.7 7.6 %collective-permute-start.2 = (f32[256,128]{1,0:T(8,128)S(1)}, f32[256,128]{1,0:T(8,128)S(1)}, u32[]{:S(2)}, u32[]{:S(2)}) collective-permute-start(f32[256,128]{1,0:T(8,128)S(1)} %get-tuple-element.21), channel_id=1, source_target_pairs={{4,0},{8,4},{12,8},{16,12},{20,16},{24,20},{28,24},{32,28},{36,32}... | collective-permute-start | bytes 393224 | tf_op jit(solution)/shard_map/ppermute | solution.py:318
  91.3 6.3 %shard_map.99.dqkv_ref = f32[3,512,128]{2,1,0:T(8,128)S(1)} custom-call(f32[3,512,128]{2,1,0:T(8,128)S(1)} %get-tuple-element.24.qkv_ref, f32[128,512]{1,0:T(8,128)S(1)} %get-tuple-element.25.att_ref, f32[4,512]{1,0:T(4,128)S(1)} %get-tuple-element.26.lse_ref, f32[512,128]{1,0:T(8,128)S(1)} %pad_maximum_fusion.2.grad_ref, ...), custom_call_target="tpu_custom_call" | custom-call | flops 1000000000 | bytes 2367488 | tf_op jit(solution)/shard_map/pallas_call | solution.py:250
  97.6 1.6 shard_map.104
  99.2 2.0 shard_map.96
  101.3 6.4 %all_to_all.76 = f32[2,1024,128]{2,1,0:T(8,128)S(1)} all-to-all(f32[2,1024,128]{2,1,0:T(8,128)S(1)} %bitcast.37), channel_id=1, replica_groups=mesh['z'=16,'x'=4,'core'=2,'head'=4] {'core'}, dimensions={0} | all-to-all | bytes 2097152 | tf_op jit(solution)/shard_map/all_to_all | solution.py:266
  108.6 12.7 %all_to_all.77 = f32[4,256,128]{2,1,0:T(8,128)S(1)} all-to-all(f32[4,256,128]{2,1,0:T(8,128)} %bitcast.39), channel_id=1, replica_groups=mesh['z'=16,'x'=4,'core'=2,'head'=4] {'x'}, dimensions={0} | all-to-all | bytes 1048576 | tf_op jit(solution)/shard_map/all_to_all | solution.py:266
  122.0 6.4 %all-to-all-start.6 = ((f32[16,16,128]{2,1,0:T(8,128)}), f32[16,16,128]{2,1,0:T(8,128)S(1)}, u32[]{:S(2)}, u32[]{:S(2)}) async-start(f32[16,16,128]{2,1,0:T(8,128)} %bitcast.13), calls=%async_computation.7 | async-start | bytes 262144 | tf_op jit(solution)/shard_map/all_to_all | solution.py:266
  128.3 2.3 %shard_map.100 = f32[4,512,128]{2,1,0:T(8,128)} custom-call(f32[3,512,128]{2,1,0:T(8,128)S(1)} %shard_map.99.dqkv_ref, f32[3,512,128]{2,1,0:T(8,128)S(1)} %bitcast.33), custom_call_target="tpu_custom_call" | custom-call | flops 1000000000 | bytes 2621440 | tf_op jit(solution)/shard_map/pallas_call | solution.py:250
  130.7 9.6 %all-to-all-done.6 = f32[16,16,128]{2,1,0:T(8,128)S(1)} async-done(((f32[16,16,128]{2,1,0:T(8,128)}), f32[16,16,128]{2,1,0:T(8,128)S(1)}, u32[]{:S(2)}, u32[]{:S(2)}) %all-to-all-start.6) | async-done | bytes 131104 | tf_op jit(solution)/shard_map/all_to_all | solution.py:266
  140.3 3.5 %all-to-all-start.2 = ((f32[4,512,128]{2,1,0:T(8,128)}), f32[4,512,128]{2,1,0:T(8,128)S(1)}, u32[]{:S(2)}, u32[]{:S(2)}) async-start(f32[4,512,128]{2,1,0:T(8,128)} %shard_map.100), calls=%async_computation.3 | async-start | bytes 2097152 | tf_op jit(solution)/shard_map/all_to_all | solution.py:266
  143.9 10.9 %all-to-all-done.2 = f32[4,512,128]{2,1,0:T(8,128)S(1)} async-done(((f32[4,512,128]{2,1,0:T(8,128)}), f32[4,512,128]{2,1,0:T(8,128)S(1)}, u32[]{:S(2)}, u32[]{:S(2)}) %all-to-all-start.2) | async-done | bytes 1048608 | tf_op jit(solution)/shard_map/all_to_all | solution.py:266
  155.4 7.7 %all-to-all-start.7 = ((f32[16,16,128]{2,1,0:T(8,128)}), f32[16,16,128]{2,1,0:T(8,128)S(1)}, u32[]{:S(2)}, u32[]{:S(2)}) async-start(f32[16,16,128]{2,1,0:T(8,128)} %broadcast_in_dim.46), calls=%async_computation.8 | async-start | bytes 262144 | tf_op jit(solution)/shard_map/all_to_all | solution.py:266
  163.9 11.2 %all-to-all-done.7 = f32[16,16,128]{2,1,0:T(8,128)S(1)} async-done(((f32[16,16,128]{2,1,0:T(8,128)}), f32[16,16,128]{2,1,0:T(8,128)S(1)}, u32[]{:S(2)}, u32[]{:S(2)}) %all-to-all-start.7) | async-done | bytes 131104 | tf_op jit(solution)/shard_map/all_to_all | solution.py:266
  175.9 3.5 %all-to-all-start.8 = ((f32[4,256,128]{2,1,0:T(8,128)}), f32[4,256,128]{2,1,0:T(8,128)S(1)}, u32[]{:S(2)}, u32[]{:S(2)}) async-start(f32[4,256,128]{2,1,0:T(8,128)} %broadcast_in_dim.48), calls=%async_computation.9 | async-start | bytes 1048576 | tf_op jit(solution)/shard_map/all_to_all | solution.py:266
  179.5 6.3 %collective-permute-start.4 = (f32[256,128]{1,0:T(8,128)S(1)}, f32[256,128]{1,0:T(8,128)S(1)}, u32[]{:S(2)}, u32[]{:S(2)}) collective-permute-start(f32[256,128]{1,0:T(8,128)S(1)} %shard_map.101), channel_id=1, source_target_pairs={{4,0},{8,4},{12,8},{16,12},{20,16},{24,20},{28,24},{32,28},{36,32}... | collective-permute-start | bytes 393224 | tf_op jit(solution)/shard_map/ppermute | solution.py:326
  186.5 5.4 %collective-permute-done.4.high_ref = f32[256,128]{1,0:T(8,128)S(1)} collective-permute-done((f32[256,128]{1,0:T(8,128)S(1)}, f32[256,128]{1,0:T(8,128)S(1)}, u32[]{:S(2)}, u32[]{:S(2)}) %collective-permute-start.4) | collective-permute-done | bytes 131104 | tf_op jit(solution)/shard_map/ppermute | solution.py:326
  191.9 1.3 shard_map.102
  193.3 4.2 %all_to_all.78 = f32[2,1024,128]{2,1,0:T(8,128)S(1)} all-to-all(f32[2,1024,128]{2,1,0:T(8,128)S(1)} %broadcast_in_dim.50), channel_id=1, replica_groups=mesh['z'=16,'x'=4,'core'=2,'head'=4] {'core'}, dimensions={0} | all-to-all | bytes 2097152 | tf_op jit(solution)/shard_map/all_to_all | solution.py:266
  197.5 7.1 %all-to-all-start.3 = ((f32[128,4,128]{2,1,0:T(4,128)}), f32[128,4,128]{2,1,0:T(4,128)S(1)}, u32[]{:S(2)}, u32[]{:S(2)}) async-start(f32[128,4,128]{2,1,0:T(4,128)} %bitcast.7), calls=%async_computation.4 | async-start | bytes 524288 | tf_op jit(solution)/shard_map/all_to_all | solution.py:266
  206.5 18.5 %all-to-all-done.3 = f32[128,4,128]{2,1,0:T(4,128)S(1)} async-done(((f32[128,4,128]{2,1,0:T(4,128)}), f32[128,4,128]{2,1,0:T(4,128)S(1)}, u32[]{:S(2)}, u32[]{:S(2)}) %all-to-all-start.3) | async-done | bytes 262176 | tf_op jit(solution)/shard_map/all_to_all | solution.py:266
  225.1 1.3 shard_map.103
  (45 shorter events, 12.0 us)
Async XLA Ops:
  7.2 0.7 copy-start.5
  7.8 0.9 copy-start.3
  10.8 43.4 %all-to-all-start = ((f32[640,1,128]{2,1,0:T(1,128)}), f32[640,1,128]{2,1,0:T(1,128)S(1)}, u32[]{:S(2)}, u32[]{:S(2)}) async-start(f32[640,1,128]{2,1,0:T(1,128)} %bitcast.2), calls=%async_computation | async-start | bytes 655360 | tf_op jit(solution)/shard_map/all_to_all | solution.py:266
  31.2 36.1 %all-gather.3.cloned.1.call-start = ((), (), s32[]{:S(2)}) async-start(), calls=%async_computation.12 | async-start | bytes 1310720 | tf_op jit(solution)/shard_map/all_gather | solution.py:293
  55.8 6.1 %collective-permute-start = (f32[256,128]{1,0:T(8,128)S(1)}, f32[256,128]{1,0:T(8,128)S(1)}, u32[]{:S(2)}, u32[]{:S(2)}) collective-permute-start(f32[256,128]{1,0:T(8,128)S(1)} %get-tuple-element.18), channel_id=1, source_target_pairs={{0,4},{4,8},{8,12},{12,16},{16,20},{20,24},{24,28},{28,32},{32,36}... | collective-permute-start | bytes 393224 | tf_op jit(solution)/shard_map/ppermute | solution.py:291
  62.9 4.3 %copy-start.4 = (f32[128,512]{1,0:T(8,128)S(1)}, f32[128,512]{1,0:T(8,128)}, u32[]{:S(2)}) copy-start(f32[128,512]{1,0:T(8,128)} %wout_ref.3) | copy-start | bytes 786436
  62.9 15.4 %all-to-all-start.1 = ((f32[4,512,128]{2,1,0:T(8,128)}), f32[4,512,128]{2,1,0:T(8,128)S(1)}, u32[]{:S(2)}, u32[]{:S(2)}) async-start(f32[4,512,128]{2,1,0:T(8,128)} %broadcast_in_dim.22), calls=%async_computation.1 | async-start | bytes 2097152 | tf_op jit(solution)/shard_map/all_to_all | solution.py:266
  67.2 1.2 copy-start
  68.5 5.4 %copy-start.6 = (s32[512]{0:T(512)S(1)}, s32[512]{0:T(512)}, u32[]{:S(2)}) copy-start(s32[512]{0:T(512)} %param.10) | copy-start | bytes 6148
  69.1 9.4 %copy-start.2 = (f32[512,3,128]{2,0,1:T(8,128)S(1)}, f32[512,3,128]{2,0,1:T(8,128)}, u32[]{:S(2)}) copy-start(f32[512,3,128]{2,0,1:T(8,128)} %param.7) | copy-start | bytes 2359300
  69.1 9.3 %collective-permute-start.3 = (f32[256,128]{1,0:T(8,128)S(1)}, f32[256,128]{1,0:T(8,128)S(1)}, u32[]{:S(2)}, u32[]{:S(2)}) collective-permute-start(f32[256,128]{1,0:T(8,128)S(1)} %get-tuple-element.27), channel_id=1, source_target_pairs={{0,4},{4,8},{8,12},{12,16},{16,20},{20,24},{24,28},{28,32},{32,36}... | collective-permute-start | bytes 393224 | tf_op jit(solution)/shard_map/ppermute | solution.py:291
  73.9 4.5 %collective-permute-start.1 = (s32[256]{0:T(256)S(1)}, s32[256]{0:T(256)S(1)}, u32[]{:S(2)}, u32[]{:S(2)}) collective-permute-start(s32[256]{0:T(256)S(1)} %get-tuple-element.44), channel_id=1, source_target_pairs={{0,4},{4,8},{8,12},{12,16},{16,20},{20,24},{24,28},{28,32},{32,36}... | collective-permute-start | bytes 3080 | tf_op jit(solution)/shard_map/ppermute | solution.py:291
  83.7 15.5 %collective-permute-start.2 = (f32[256,128]{1,0:T(8,128)S(1)}, f32[256,128]{1,0:T(8,128)S(1)}, u32[]{:S(2)}, u32[]{:S(2)}) collective-permute-start(f32[256,128]{1,0:T(8,128)S(1)} %get-tuple-element.21), channel_id=1, source_target_pairs={{4,0},{8,4},{12,8},{16,12},{20,16},{24,20},{28,24},{32,28},{36,32}... | collective-permute-start | bytes 393224 | tf_op jit(solution)/shard_map/ppermute | solution.py:318
  97.6 1.6 copy-start.1
  122.0 18.4 %all-to-all-start.6 = ((f32[16,16,128]{2,1,0:T(8,128)}), f32[16,16,128]{2,1,0:T(8,128)S(1)}, u32[]{:S(2)}, u32[]{:S(2)}) async-start(f32[16,16,128]{2,1,0:T(8,128)} %bitcast.13), calls=%async_computation.7 | async-start | bytes 262144 | tf_op jit(solution)/shard_map/all_to_all | solution.py:266
  140.3 14.5 %all-to-all-start.2 = ((f32[4,512,128]{2,1,0:T(8,128)}), f32[4,512,128]{2,1,0:T(8,128)S(1)}, u32[]{:S(2)}, u32[]{:S(2)}) async-start(f32[4,512,128]{2,1,0:T(8,128)} %shard_map.100), calls=%async_computation.3 | async-start | bytes 2097152 | tf_op jit(solution)/shard_map/all_to_all | solution.py:266
  155.4 19.7 %all-to-all-start.7 = ((f32[16,16,128]{2,1,0:T(8,128)}), f32[16,16,128]{2,1,0:T(8,128)S(1)}, u32[]{:S(2)}, u32[]{:S(2)}) async-start(f32[16,16,128]{2,1,0:T(8,128)} %broadcast_in_dim.46), calls=%async_computation.8 | async-start | bytes 262144 | tf_op jit(solution)/shard_map/all_to_all | solution.py:266
  163.1 63.3 %reduce-scatter.2.cloned.1.call-start = ((), (), s32[]{:S(2)}) async-start(), calls=%async_computation.11 | async-start | bytes 1310720 | tf_op jit(solution)/shard_map/reduce_scatter | solution.py:320
  175.9 17.3 %all-to-all-start.8 = ((f32[4,256,128]{2,1,0:T(8,128)}), f32[4,256,128]{2,1,0:T(8,128)S(1)}, u32[]{:S(2)}, u32[]{:S(2)}) async-start(f32[4,256,128]{2,1,0:T(8,128)} %broadcast_in_dim.48), calls=%async_computation.9 | async-start | bytes 1048576 | tf_op jit(solution)/shard_map/all_to_all | solution.py:266
  179.5 12.4 %collective-permute-start.4 = (f32[256,128]{1,0:T(8,128)S(1)}, f32[256,128]{1,0:T(8,128)S(1)}, u32[]{:S(2)}, u32[]{:S(2)}) collective-permute-start(f32[256,128]{1,0:T(8,128)S(1)} %shard_map.101), channel_id=1, source_target_pairs={{4,0},{8,4},{12,8},{16,12},{20,16},{24,20},{28,24},{32,28},{36,32}... | collective-permute-start | bytes 393224 | tf_op jit(solution)/shard_map/ppermute | solution.py:326
  197.5 27.6 %all-to-all-start.3 = ((f32[128,4,128]{2,1,0:T(4,128)}), f32[128,4,128]{2,1,0:T(4,128)S(1)}, u32[]{:S(2)}, u32[]{:S(2)}) async-start(f32[128,4,128]{2,1,0:T(4,128)} %bitcast.7), calls=%async_computation.4 | async-start | bytes 524288 | tf_op jit(solution)/shard_map/all_to_all | solution.py:266
Sparse Core Ops, SparseCore 0:
  34.1 31.7 all-gather.2
  167.4 29.5 reduce-scatter.1

commit v3 on v2

v3 whole, which is shorter than its diff:
```python
import functools
import math

import jax
import jax.numpy as jnp
from jax import lax
from jax.experimental import pallas as pl
from jax.experimental.pallas import tpu as pltpu
from jax.sharding import PartitionSpec as P

D = 512
HEADS = 16
PATCH = 512
HALF = PATCH // 2
HEAD = D // HEADS
WIDTH = 128
HERE = WIDTH // HEAD
CURVE = ("far", "near", "x", "core")
PLANE = ("near", "x")
BLOCKS = 16
SIDE = WIDTH // 2
ADDED = 2
BF = jnp.bfloat16
F32 = jnp.float32
SCALE = 1.0 / math.sqrt(HEAD)
LOG2E = math.log2(math.e)

NN = (((1,), (0,)), ((), ()))
NT = (((1,), (1,)), ((), ()))


def mm(a, b, dims=NN):
    return lax.dot_general(a, b, dims, preferred_element_type=F32)


def split(x):
    high = x.astype(BF)
    return high, (x - high.astype(F32)).astype(BF)


def split3(x):
    high, rest = x.astype(BF), None
    rest = x - high.astype(F32)
    mid = rest.astype(BF)
    return high, mid, (rest - mid.astype(F32)).astype(BF)


def mm3(a, b, dims=NN):
    (ah, al), (bh, bl) = a, b
    return mm(ah, bh, dims) + (mm(ah, bl, dims) + mm(al, bh, dims))


def select_rows(pick, x):
    high, mid, low = split3(x)
    return mm(pick, high) + (mm(pick, mid) + mm(pick, low))


def column(row):
    return jnp.transpose(jnp.broadcast_to(row, (WIDTH, row.shape[1])))


def wide(col, width=PATCH):
    return jnp.concatenate([col] * (width // WIDTH), axis=1)


def iota(dim, shape=(PATCH, PATCH)):
    return lax.broadcasted_iota(jnp.int32, shape, dim).astype(F32)


def one_hot(condition):
    return jnp.where(condition, 1.0, 0.0).astype(BF)


def spread(each, size, rows, arrived):
    total = arrived.shape[0]
    place = iota(0, (rows, total))
    peer = jnp.floor((place + 0.5) * (1.0 / size))
    pick = one_hot(iota(1, (rows, total)) == peer * (each + 1) + each)
    high, low = split(arrived)
    listed = mm(pick, high) + mm(pick, low)
    place = iota(0, (rows, WIDTH))
    turn = place - jnp.floor((place + 0.5) * (1.0 / size)) * size
    mine = jnp.where((iota(1, (rows, WIDTH)) == turn) & (turn < each), listed, 0.0)
    mine = jnp.sum(mine, axis=1, keepdims=True)
    return jnp.where(turn < each, mine, -1.0)


def sort_kernel(each, dest_ref, feat_ref, message_ref, slot_ref):
    dest = dest_ref[...]
    block = dest // PATCH
    local = (dest - block * PATCH).astype(F32)
    block = block.astype(F32)
    same = (wide(column(block)) == block) & (iota(0) < iota(1))
    rank = jnp.sum(jnp.where(same, 1.0, 0.0), axis=0, keepdims=True)
    slot_ref[...] = block * each + rank
    shape = (message_ref.shape[0], PATCH)
    rows = iota(0, shape)
    first = block * (each + 1)
    lists = jnp.where(iota(1, (PATCH, WIDTH)) == column(rank), column(local), 0.0)
    high, low = split(lists)
    last = one_hot(rows == first + each)
    message = select_rows(one_hot(rows == first + rank), feat_ref[...])
    message_ref[...] = message + (mm(last, high) + mm(last, low))


def positions_kernel(each, arrived_ref, position_ref):
    position_ref[...] = spread(each, each + ADDED, position_ref.shape[0], arrived_ref[...])


def place_kernel(each, arrived_ref, low_ref, high_ref):
    arrived = arrived_ref[...]
    total = arrived.shape[0]
    row = jnp.transpose(spread(each, each + 1, total, arrived))[:1]
    placed = select_rows(one_hot(iota(0, (PATCH, total)) == row), arrived)
    low_ref[...] = placed[:HALF]
    high_ref[...] = placed[HALF:]


def add_kernel(first_ref, second_ref, third_ref, fourth_ref, early_ref, late_ref):
    total = first_ref[...] + second_ref[...] + (third_ref[...] + fourth_ref[...])
    early_ref[...] = total[:HALF]
    late_ref[...] = total[HALF:]


def remainder(x, by):
    return x - jnp.floor((x + 0.5) * (1.0 / by)) * by


def pack_kernel(each, position_ref, low_ref, high_ref, sums_ref, message_ref):
    size = each + ADDED
    total = message_ref.shape[0]
    grads = jnp.concatenate([low_ref[...], high_ref[...]], axis=0)
    sums = sums_ref[0]
    for part in range(1, sums_ref.shape[0]):
        sums += sums_ref[part]
    shape = (total, SIDE)
    row = iota(1, shape)
    added = jnp.floor((row + 0.5) * (1.0 / 32))
    rest = row - added * 32
    core = jnp.floor((rest + 0.5) * (1.0 / 16))
    peer = 2 * (rest - core * 16) + core
    pick = one_hot(remainder(iota(0, shape), size * SIDE // ADDED) == peer * size + each + added)
    message = select_rows(one_hot(wide(position_ref[...]) == iota(1, (total, PATCH))), grads)
    message_ref[...] = message + select_rows(pick, sums)


def unpack_kernel(each, message_ref, sums_ref):
    size = each + ADDED
    shape = (SIDE, message_ref.shape[0])
    row = iota(0, shape)
    peer = jnp.floor((row + 0.5) * (1.0 / ADDED))
    wanted = peer * size + each + (row - peer * ADDED)
    sums_ref[...] = select_rows(one_hot(remainder(iota(1, shape), size * SIDE // ADDED) == wanted), message_ref[...])


def unsort_kernel(each, slot_ref, message_ref, out_ref):
    slot = slot_ref[...]
    block = jnp.floor((slot + 0.5) * (1.0 / each))
    wanted = block * (each + ADDED) + (slot - block * each)
    total = message_ref.shape[0]
    pick = one_hot(wide(column(wanted), total) == iota(1, (PATCH, total)))
    out_ref[...] = select_rows(pick, message_ref[...])


def finish_kernel(core_ref, mine_ref, other_ref, din_ref, dout_ref):
    core = core_ref[0]
    for own, ref in ((core, mine_ref), (1 - core, other_ref)):
        for block in range(BLOCKS):
            for side in range(2):
                for added in range(ADDED):
                    got = ref[:, (2 * block + side) * ADDED + added, :]
                    rows = pl.ds(pl.multiple_of(side * SIDE + added * 32 + own * 16, 16), 16)
                    t, part = divmod(block, D // WIDTH)
                    lanes = slice(part * WIDTH, (part + 1) * WIDTH)
                    if t < 3:
                        rows = pl.ds(pl.multiple_of(part * WIDTH + side * SIDE + added * 32 + own * 16, 16), 16)
                        din_ref[t, rows] = got
                    else:
                        dout_ref[rows, lanes] = got


def cot_kernel(cot_ref, wout_ref, grad_ref):
    total = jnp.zeros((PATCH, WIDTH), F32)
    for part in range(D // WIDTH):
        total += mm3(split(cot_ref[part]), split(wout_ref[:, part * WIDTH : (part + 1) * WIDTH]), NT)
    grad_ref[...] = total


def head_mask(head):
    lanes = lax.broadcasted_iota(jnp.int32, (PATCH, WIDTH), 1)
    return (lanes // HEAD) == head


def scores_of(queries, key_rows, mask):
    qh, ql = split(queries)
    kh, kl = split(jnp.where(mask, key_rows, 0.0))
    keys = jnp.concatenate([kh, kl], axis=1)
    return mm(keys, jnp.concatenate([qh, qh], axis=1), NT) + mm(
        keys, jnp.concatenate([ql, ql], axis=1), NT
    )


def forward_kernel(x_ref, win_ref, wout_ref, bias_ref, qkv_ref, att_ref, lse_ref, out_ref, vt_ref):
    parts = [split(x_ref[part]) for part in range(D // WIDTH)]
    for t in range(3):
        total = jnp.zeros((PATCH, WIDTH), F32)
        for part in range(D // WIDTH):
            total += mm3(parts[part], split(win_ref[t, part * WIDTH : (part + 1) * WIDTH]))
        qkv_ref[t] = total
    vt_ref[...] = jnp.transpose(qkv_ref[2])
    bias = wide(bias_ref[...])

    def one(head, carry):
        mask = head_mask(head)
        scores = scores_of(qkv_ref[0] * (SCALE * LOG2E), qkv_ref[1], mask) + bias
        top = jnp.max(scores, axis=0, keepdims=True)
        weights = jnp.exp2(scores - top)
        total = jnp.sum(weights, axis=0, keepdims=True)
        rows = pl.ds(pl.multiple_of(head * HEAD, HEAD), HEAD)
        vh, vl = split(vt_ref[rows, :])
        wh, wl = split(weights)
        both = mm(jnp.concatenate([vh, vl], axis=0), wh)
        attended = both[:HEAD] + both[HEAD:] + mm(vh, wl)
        att_ref[rows, :] = attended / total
        lse_ref[pl.ds(head, 1), :] = top + jnp.log2(total)
        return carry

    lax.fori_loop(0, HERE, one, 0)
    attended = split(jnp.transpose(att_ref[...]))
    for part in range(D // WIDTH):
        out_ref[part] = mm3(attended, split(wout_ref[:, part * WIDTH : (part + 1) * WIDTH]))


def backward_kernel(qkv_ref, att_ref, lse_ref, grad_ref, bias_ref, dqkv_ref, kt_ref, gt_ref, dqt_ref):
    kt_ref[...] = jnp.transpose(qkv_ref[1])
    gt_ref[...] = jnp.transpose(grad_ref[...])
    bias = wide(bias_ref[...])
    dqkv_ref[1] = jnp.zeros((PATCH, WIDTH), F32)
    dqkv_ref[2] = jnp.zeros((PATCH, WIDTH), F32)

    def one(head, carry):
        mask = head_mask(head)
        rows = pl.ds(pl.multiple_of(head * HEAD, HEAD), HEAD)
        scores = scores_of(qkv_ref[0] * (SCALE * LOG2E), qkv_ref[1], mask) + bias
        probs = jnp.exp2(scores - lse_ref[pl.ds(head, 1), :])
        ph, plo = split(probs)
        grad_probs = scores_of(grad_ref[...], qkv_ref[2], mask)
        gh, gl = split(jnp.where(mask, grad_ref[...], 0.0))
        both = mm(ph, jnp.concatenate([gh, gl], axis=1))
        dqkv_ref[2] += both[:, :WIDTH] + both[:, WIDTH:] + mm(plo, gh)
        inner = jnp.sum(gt_ref[rows, :] * att_ref[rows, :], axis=0, keepdims=True)
        grad_scores = probs * (grad_probs - inner)
        sh, sl = split(grad_scores)
        qh, ql = split(jnp.where(mask, qkv_ref[0] * SCALE, 0.0))
        both = mm(sh, jnp.concatenate([qh, ql], axis=1))
        dqkv_ref[1] += both[:, :WIDTH] + both[:, WIDTH:] + mm(sl, qh)
        kh, kl = split(kt_ref[rows, :] * SCALE)
        both = mm(jnp.concatenate([kh, kl], axis=0), sh)
        dqt_ref[rows, :] = both[:HEAD] + both[HEAD:] + mm(kh, sl)
        return carry

    lax.fori_loop(0, HERE, one, 0)
    dqkv_ref[0] = jnp.transpose(dqt_ref[...])


def weights_kernel(core_ref, x_ref, dqkv_ref, att_ref, cot_ref, keep_ref, send_ref):
    second = core_ref[0] == 1

    def put(block, grads):
        top, bottom = grads[:SIDE], grads[SIDE:]
        keep_ref[block] = jnp.where(second, bottom, top)
        send_ref[block] = jnp.where(second, top, bottom)

    attended = split(att_ref[...])
    parts = [split(x_ref[part]) for part in range(D // WIDTH)]
    for t in range(3):
        grads = split(jnp.transpose(dqkv_ref[t]))
        for part in range(D // WIDTH):
            put(t * (D // WIDTH) + part, jnp.transpose(mm3(grads, parts[part])))
    for part in range(D // WIDTH):
        put(3 * (D // WIDTH) + part, mm3(attended, split(cot_ref[part])))


def rows_kernel(head_ref, dqkv_ref, win_ref, *out_refs):
    grads = [split(dqkv_ref[t]) for t in range(3)]
    for step, out_ref in enumerate(out_refs):
        part = lax.rem(head_ref[0] + step, D // WIDTH)
        rows = pl.ds(pl.multiple_of(part * WIDTH, WIDTH), WIDTH)
        total = jnp.zeros((PATCH, WIDTH), F32)
        for t in range(3):
            total += mm3(grads[t], split(win_ref[t, rows]), NT)
        out_ref[...] = total


def call(kernel, outs, *args, scratch=(), scalars=0, flops=10**9):
    size = sum(math.prod(a.shape) * 4 for a in (*args, *outs))
    return pl.pallas_call(
        kernel,
        out_shape=tuple(jax.ShapeDtypeStruct(o, F32) for o in [x.shape for x in outs]),
        in_specs=[pl.BlockSpec(memory_space=pltpu.SMEM)] * scalars
        + [pl.BlockSpec(memory_space=pltpu.VMEM)] * (len(args) - scalars),
        out_specs=tuple(pl.BlockSpec(memory_space=pltpu.VMEM) for _ in outs),
        scratch_shapes=[pltpu.VMEM(s, F32) for s in scratch],
        compiler_params=pltpu.CompilerParams(vmem_limit_bytes=40 * 2**20),
        cost_estimate=pl.CostEstimate(flops=flops, bytes_accessed=size, transcendentals=0),
    )(*args)


def of(*shape):
    return jax.ShapeDtypeStruct(shape, F32)


def swap(x, axis):
    return lax.all_to_all(x, axis, split_axis=0, concat_axis=0, tiled=True)


def spread_to(x, axis):
    peers = lax.axis_size(axis)
    return swap(jnp.broadcast_to(x[None], (peers,) + x.shape).reshape(-1, WIDTH), axis)


def shards(features, input_proj, output_proj, destination, real_points, cotangent):
    peers = lax.axis_size(CURVE)
    heads = lax.axis_size("head")
    each = PATCH // peers
    up = [(i, (i + 1) % peers) for i in range(peers)]
    down = [(j, i) for i, j in up]
    core = lax.axis_index("core").astype(jnp.int32).reshape(1)
    head = lax.axis_index("head").astype(jnp.int32).reshape(1)

    def to_patch(low, high):
        return jnp.concatenate([lax.ppermute(high, CURVE, up), low], axis=0)

    def exchange(message):
        rows = message.shape[0]
        return swap(message.reshape(rows, 1, WIDTH), CURVE).reshape(rows, WIDTH)

    message, slot = call(
        functools.partial(sort_kernel, each), [of(PATCH + peers, WIDTH), of(1, PATCH)],
        destination.reshape(1, PATCH), features,
    )
    arrived = exchange(message)
    cot = lax.all_gather(to_patch(cotangent[:HALF], cotangent[HALF:]), "head", axis=0)
    win = jnp.transpose(input_proj, (1, 0, 2))
    valid = to_patch(real_points[:HALF], real_points[HALF:])
    bias = jnp.broadcast_to(jnp.where(valid > 0, 0.0, -jnp.inf).astype(F32)[:, None], (PATCH, WIDTH))
    (grad_attended,) = call(cot_kernel, [of(PATCH, WIDTH)], cot, output_proj)
    low, high = call(functools.partial(place_kernel, each), [of(HALF, WIDTH)] * 2, arrived)
    (position,) = call(
        functools.partial(positions_kernel, each), [of(peers * (each + ADDED), WIDTH)], arrived
    )
    x = spread_to(to_patch(low, high), "head").reshape(D // WIDTH, PATCH, WIDTH)
    qkv, attended, lse, out = call(
        forward_kernel,
        [of(3, PATCH, WIDTH), of(WIDTH, PATCH), of(HERE, PATCH), of(D // WIDTH, PATCH, WIDTH)],
        x, win, output_proj, bias, scratch=[(WIDTH, PATCH)],
    )
    out = lax.psum_scatter(out, "head", scatter_dimension=0)
    branch_out = jnp.concatenate([out[HALF:], lax.ppermute(out[:HALF], CURVE, down)], axis=0)
    (dqkv,) = call(
        backward_kernel, [of(3, PATCH, WIDTH)], qkv, attended, lse, grad_attended, bias,
        scratch=[(WIDTH, PATCH)] * 3,
    )
    dx = call(rows_kernel, [of(PATCH, WIDTH)] * heads, head, dqkv, win, scalars=1)
    dx = [dx[0]] + [
        lax.ppermute(dx[s], "head", [(i, (i + s) % heads) for i in range(heads)]) for s in (2, 1, 3)
    ]
    keep, send = call(
        weights_kernel, [of(BLOCKS, SIDE, WIDTH)] * 2, core, x, dqkv, attended, cot, scalars=1
    )
    sums = keep + lax.ppermute(send, "core", [(0, 1), (1, 0)])
    sums = swap(sums.reshape(-1, WIDTH), PLANE).reshape(BLOCKS, SIDE, WIDTH)
    early, late = call(add_kernel, [of(HALF, WIDTH)] * 2, *dx)
    (message,) = call(
        functools.partial(pack_kernel, each), [of(peers * (each + ADDED), WIDTH)],
        position, late, lax.ppermute(early, CURVE, down), sums,
    )
    message = exchange(message)
    (sums,) = call(functools.partial(unpack_kernel, each), [of(SIDE, WIDTH)], message)
    (grad_features,) = call(functools.partial(unsort_kernel, each), [of(PATCH, WIDTH)], slot, message)
    sums = spread_to(sums, PLANE).reshape(BLOCKS, SIDE, WIDTH)
    grad_inproj, grad_outproj = call(
        finish_kernel, [of(3, D, WIDTH), of(WIDTH, D)],
        core, sums, lax.ppermute(sums, "core", [(0, 1), (1, 0)]), scalars=1,
    )
    return (branch_out, grad_features, jnp.transpose(grad_inproj, (1, 0, 2)), grad_outproj)


def solution(mesh):
    curve, head = mesh.devices.shape
    sizes = (curve // 32, 4, 4, 2)
    fine = jax.sharding.Mesh(mesh.devices.reshape(*sizes, head), CURVE + ("head",))
    return jax.shard_map(
        shards,
        mesh=fine,
        in_specs=(
            P(CURVE, "head"),
            P(None, None, "head"),
            P("head", None),
            P(CURVE),
            P(CURVE),
            P(CURVE, "head"),
        ),
        out_specs=(P(CURVE, "head"), P(CURVE, "head"), P(None, None, "head"), P("head", None)),
        check_vma=False,
    )
```

time: 235 us -> 228 us (0.970)
  waiting for transfers between devices: 83.8 us -> 75.1 us
  starting transfers between devices: 77.7 us -> 84.7 us
  blocking collectives: 23.3 us -> 19.6 us
  local copies, waits for them, and re-layouts: 7.55 us -> 5.09 us
    all_to_all x7 -> x4, waiting for transfers between devices: 72.6 us -> 43.5 us  [swap(): return lax.all_to_all(x, axis, split_axis=0, concat_axis=0, tiled=True)]
    ppermute x0 -> x6, starting transfers between devices: none -> 21.9 us  [the longest x3 11 us: shards(): lax.ppermute(dx[s], 'head', [(i, (i + s) % heads) for i in range(heads)])]
    ppermute x0 -> x6, waiting for transfers between devices: none -> 11.6 us  [the longest x3 5.74 us: shards(): lax.ppermute(dx[s], 'head', [(i, (i + s) % heads) for i in range(heads)])]
    ppermute x2 -> x1, starting transfers between devices: 13.9 us -> 2.91 us  [shards(): lax.ppermute(early, CURVE, down)]
    all_gather x1, waiting for transfers between devices: 0.01 us -> 8.9 us  [shards(): lax.all_gather(to_patch(cotangent[:HALF], cotangent[HALF:]), 'head', axis=0)]
    all_to_all x7 -> x4, starting transfers between devices: 52.8 us -> 47.5 us  [swap(): return lax.all_to_all(x, axis, split_axis=0, concat_axis=0, tiled=True)]
    all_to_all x3 -> x1, blocking collectives: 23.3 us -> 19.6 us  [swap(): return lax.all_to_all(x, axis, split_axis=0, concat_axis=0, tiled=True)]
    ppermute x3, waiting for transfers between devices: 4.46 us -> 7.37 us  [to_patch(): return jnp.concatenate([lax.ppermute(high, CURVE, up), low], axis=0)]
  transfers between devices with their start and end apart: 14 -> 16, of which waited for: 8 -> 11; matrix products, arithmetic and copies ran while one was open for 2% -> 2% of each run, Pallas kernels for 7% -> 3%
where the time goes in v3:
time: 228 us
  starting transfers between devices  84.7 us (37%)
  waiting for transfers between devices  75.1 us (33%)
  Pallas kernels  26.4 us (12%)
  blocking collectives  19.6 us (9%)
  between operations  14.3 us (6%)
  local copies, waits for them, and re-layouts  5.09 us (2%)
  other arithmetic  2.33 us (1%)
    all_to_all x4, starting transfers between devices, swap(): return lax.all_to_all(x, axis, split_axis=0, concat_axis=0, tiled=True)  47.5 us
    all_to_all x4, waiting for transfers between devices, swap(): return lax.all_to_all(x, axis, split_axis=0, concat_axis=0, tiled=True)  43.5 us
    pallas_call x13, Pallas kernels, call(): pl.pallas_call(kernel, out_shape=tuple((jax.ShapeDtypeStruct(o, F32) for...  26.4 us
    all_to_all x1, blocking collectives, swap(): return lax.all_to_all(x, axis, split_axis=0, concat_axis=0, tiled=True)  19.6 us
    ppermute x3, starting transfers between devices, to_patch(): return jnp.concatenate([lax.ppermute(high, CURVE, up), low], axis=0)  12.3 us
    ppermute x3, starting transfers between devices, shards(): lax.ppermute(dx[s], 'head', [(i, (i + s) % heads) for i in range(heads)])  11 us
    all_gather x1, waiting for transfers between devices, shards(): lax.all_gather(to_patch(cotangent[:HALF], cotangent[HALF:]), 'head', axis=0)  8.9 us
    ppermute x3, waiting for transfers between devices, to_patch(): return jnp.concatenate([lax.ppermute(high, CURVE, up), low], axis=0)  7.37 us
  transfers between devices with their start and end apart: 16, of which 11 were waited for; matrix products, arithmetic and copies ran while one was open for 2% of the time, Pallas kernels for 3%

profile of v3, /device:TPU:1, one launch (start us, length us, event | category | flops | bytes accessed | tf_op | source)
XLA Modules:
  0.0 227.5 jit_solution(17842230021633957825)
XLA Ops:
  8.8 2.0 shard_map.93
  10.8 20.5 %all-to-all-start = ((f32[640,1,128]{2,1,0:T(1,128)}), f32[640,1,128]{2,1,0:T(1,128)S(1)}, u32[]{:S(2)}, u32[]{:S(2)}) async-start(f32[640,1,128]{2,1,0:T(1,128)} %bitcast.2), calls=%async_computation | async-start | bytes 655360 | tf_op jit(solution)/shard_map/all_to_all | solution.py:314
  31.4 3.5 %collective-permute-start.3 = (f32[256,128]{1,0:T(8,128)S(1)}, f32[256,128]{1,0:T(8,128)S(1)}, u32[]{:S(2)}, u32[]{:S(2)}) collective-permute-start(f32[256,128]{1,0:T(8,128)S(1)} %get-tuple-element.40), channel_id=1, source_target_pairs={{0,4},{4,8},{8,12},{12,16},{16,20},{20,24},{24,28},{28,32},{32,36}... | collective-permute-start | bytes 393224 | tf_op jit(solution)/shard_map/ppermute | solution.py:332
  34.9 2.1 collective-permute-done.3
  37.7 16.6 %all-to-all-done = f32[640,1,128]{2,1,0:T(1,128)S(1)} async-done(((f32[640,1,128]{2,1,0:T(1,128)}), f32[640,1,128]{2,1,0:T(1,128)S(1)}, u32[]{:S(2)}, u32[]{:S(2)}) %all-to-all-start) | async-done | bytes 327712 | tf_op jit(solution)/shard_map/all_to_all | solution.py:314
  54.3 1.6 shard_map.94
  55.9 4.2 %collective-permute-start = (f32[256,128]{1,0:T(8,128)S(1)}, f32[256,128]{1,0:T(8,128)S(1)}, u32[]{:S(2)}, u32[]{:S(2)}) collective-permute-start(f32[256,128]{1,0:T(8,128)S(1)} %get-tuple-element.23), channel_id=1, source_target_pairs={{0,4},{4,8},{8,12},{12,16},{16,20},{20,24},{24,28},{28,32},{32,36}... | collective-permute-start | bytes 393224 | tf_op jit(solution)/shard_map/ppermute | solution.py:332
  60.1 1.9 collective-permute-done
  63.1 4.3 %all-to-all-start.1 = ((f32[4,512,128]{2,1,0:T(8,128)}), f32[4,512,128]{2,1,0:T(8,128)S(1)}, u32[]{:S(2)}, u32[]{:S(2)}) async-start(f32[4,512,128]{2,1,0:T(8,128)} %broadcast_in_dim.14), calls=%async_computation.1 | async-start | bytes 2097152 | tf_op jit(solution)/shard_map/all_to_all | solution.py:314
  67.4 4.6 %collective-permute-start.1 = (s32[256]{0:T(256)S(1)}, s32[256]{0:T(256)S(1)}, u32[]{:S(2)}, u32[]{:S(2)}) collective-permute-start(s32[256]{0:T(256)S(1)} %get-tuple-element.44), channel_id=1, source_target_pairs={{0,4},{4,8},{8,12},{12,16},{16,20},{20,24},{24,28},{28,32},{32,36}... | collective-permute-start | bytes 3080 | tf_op jit(solution)/shard_map/ppermute | solution.py:332
  72.1 3.4 %collective-permute-done.1 = s32[256]{0:T(256)S(1)} collective-permute-done((s32[256]{0:T(256)S(1)}, s32[256]{0:T(256)S(1)}, u32[]{:S(2)}, u32[]{:S(2)}) %collective-permute-start.1) | collective-permute-done | bytes 1056 | tf_op jit(solution)/shard_map/ppermute | solution.py:332
  75.4 8.9 %all-gather.3.cloned.1.call-done = f32[2048,128]{1,0:T(8,128)} async-done(((f32[512,128]{1,0:T(8,128)}), f32[2048,128]{1,0:T(8,128)}) %all-gather.3.cloned.1.call-update) | async-done | bytes 1048592 | tf_op jit(solution)/shard_map/all_gather | solution.py:343
  86.2 2.2 all-to-all-done.1.x_ref
  88.5 6.7 %shard_map.95 = (f32[3,512,128]{2,1,0:T(8,128)S(1)}, f32[128,512]{1,0:T(8,128)S(1)}, f32[4,512]{1,0:T(4,128)S(1)}, f32[4,512,128]{2,1,0:T(8,128)}) custom-call(f32[4,512,128]{2,1,0:T(8,128)S(1)} %all-to-all-done.1.x_ref, f32[3,512,128]{2,1,0:T(8,128)S(1)} %bitcast.24, f32[128,512]{1,0:T(8,128)S(1)} %copy-done.4, f32[512,128]{1,0:T(8,128)S(1)} %broadcast_in_dim.29.bias_ref), custom_call_target="tpu_custom_call" | custom-call | flops 1000000000 | bytes 4464640 | tf_op jit(solution)/shard_map/pallas_call | solution.py:297
  95.2 6.3 %shard_map.98.dqkv_ref = f32[3,512,128]{2,1,0:T(8,128)S(1)} custom-call(f32[3,512,128]{2,1,0:T(8,128)S(1)} %get-tuple-element.27.qkv_ref, f32[128,512]{1,0:T(8,128)S(1)} %get-tuple-element.28.att_ref, f32[4,512]{1,0:T(4,128)S(1)} %get-tuple-element.29.lse_ref, f32[512,128]{1,0:T(8,128)S(1)} %shard_map.97.grad_ref, f32[512,128]{1,0:T(8,128)S(1)} %broadcast_in_dim.29.bias_ref), custom_call_target="tpu_custom_call" | custom-call | flops 1000000000 | bytes 2367488 | tf_op jit(solution)/shard_map/pallas_call | solution.py:297
  101.5 1.9 shard_map.101
  103.5 4.4 %collective-permute-start.8 = (f32[16,64,128]{2,1,0:T(8,128)S(1)}, f32[16,64,128]{2,1,0:T(8,128)S(1)}, u32[]{:S(2)}, u32[]{:S(2)}) collective-permute-start(f32[16,64,128]{2,1,0:T(8,128)S(1)} %get-tuple-element.37), channel_id=1, source_target_pairs={{0,4},{4,0},{1,5},{5,1},{2,6},{6,2},{3,7},{7,3},{8,12},{12,8},{9,1... | collective-permute-start | bytes 1572872 | tf_op jit(solution)/shard_map/ppermute | solution.py:371
  110.2 6.8 %all-to-all-start.2 = ((f32[16,64,128]{2,1,0:T(8,128)}), f32[16,64,128]{2,1,0:T(8,128)S(1)}, u32[]{:S(2)}, u32[]{:S(2)}) async-start(f32[16,64,128]{2,1,0:T(8,128)} %add.5), calls=%async_computation.3 | async-start | bytes 1048576 | tf_op jit(solution)/shard_map/all_to_all | solution.py:314
  118.4 4.5 %collective-permute-start.4 = (f32[512,128]{1,0:T(8,128)S(1)}, f32[512,128]{1,0:T(8,128)S(1)}, u32[]{:S(2)}, u32[]{:S(2)}) collective-permute-start(f32[512,128]{1,0:T(8,128)S(1)} %get-tuple-element.31), channel_id=1, source_target_pairs={{0,2},{1,3},{2,0},{3,1},{4,6},{5,7},{6,4},{7,5},{8,10},{9,11},{10,... | collective-permute-start | bytes 786440 | tf_op jit(solution)/shard_map/ppermute | solution.py:366
  122.9 1.9 collective-permute-start.5
  124.8 4.6 %collective-permute-start.6 = (f32[512,128]{1,0:T(8,128)S(1)}, f32[512,128]{1,0:T(8,128)S(1)}, u32[]{:S(2)}, u32[]{:S(2)}) collective-permute-start(f32[512,128]{1,0:T(8,128)S(1)} %get-tuple-element.33), channel_id=1, source_target_pairs={{0,3},{1,0},{2,1},{3,2},{4,7},{5,4},{6,5},{7,6},{8,11},{9,8},{10,9... | collective-permute-start | bytes 786440 | tf_op jit(solution)/shard_map/ppermute | solution.py:366
  129.4 5.7 %collective-permute-done.5.third_ref = f32[512,128]{1,0:T(8,128)S(1)} collective-permute-done((f32[512,128]{1,0:T(8,128)S(1)}, f32[512,128]{1,0:T(8,128)S(1)}, u32[]{:S(2)}, u32[]{:S(2)}) %collective-permute-start.5) | collective-permute-done | bytes 262176 | tf_op jit(solution)/shard_map/ppermute | solution.py:366
  135.2 2.9 %collective-permute-start.7 = (f32[256,128]{1,0:T(8,128)S(1)}, f32[256,128]{1,0:T(8,128)S(1)}, u32[]{:S(2)}, u32[]{:S(2)}) collective-permute-start(f32[256,128]{1,0:T(8,128)S(1)} %get-tuple-element.35), channel_id=1, source_target_pairs={{4,0},{8,4},{12,8},{16,12},{20,16},{24,20},{28,24},{32,28},{36,32}... | collective-permute-start | bytes 393224 | tf_op jit(solution)/shard_map/ppermute | solution.py:376
  139.0 3.0 %collective-permute-done.7.high_ref = f32[256,128]{1,0:T(8,128)S(1)} collective-permute-done((f32[256,128]{1,0:T(8,128)S(1)}, f32[256,128]{1,0:T(8,128)S(1)}, u32[]{:S(2)}, u32[]{:S(2)}) %collective-permute-start.7) | collective-permute-done | bytes 131104 | tf_op jit(solution)/shard_map/ppermute | solution.py:376
  142.0 1.7 shard_map.102
  143.7 15.9 %all-to-all-start.3 = ((f32[768,1,128]{2,1,0:T(1,128)}), f32[768,1,128]{2,1,0:T(1,128)S(1)}, u32[]{:S(2)}, u32[]{:S(2)}) async-start(f32[768,1,128]{2,1,0:T(1,128)} %bitcast.11), calls=%async_computation.4 | async-start | bytes 786432 | tf_op jit(solution)/shard_map/all_to_all | solution.py:314
  160.3 24.7 %all-to-all-done.3 = f32[768,1,128]{2,1,0:T(1,128)S(1)} async-done(((f32[768,1,128]{2,1,0:T(1,128)}), f32[768,1,128]{2,1,0:T(1,128)S(1)}, u32[]{:S(2)}, u32[]{:S(2)}) %all-to-all-start.3) | async-done | bytes 393248 | tf_op jit(solution)/shard_map/all_to_all | solution.py:314
  185.4 19.6 %all_to_all.28.mine_ref = f32[16,64,128]{2,1,0:T(8,128)S(1)} all-to-all(f32[16,64,128]{2,1,0:T(8,128)S(1)} %broadcast_in_dim.30), channel_id=1, replica_groups=mesh['far'=4,'near'=4,'x'=4,'core'=2,'head'=4] {'near','x'}, dimensions={0} | all-to-all | bytes 1048576 | tf_op jit(solution)/shard_map/all_to_all | solution.py:314
  205.0 4.6 %collective-permute-start.9 = (f32[16,64,128]{2,1,0:T(8,128)S(1)}, f32[16,64,128]{2,1,0:T(8,128)S(1)}, u32[]{:S(2)}, u32[]{:S(2)}) collective-permute-start(f32[16,64,128]{2,1,0:T(8,128)S(1)} %all_to_all.28.mine_ref), channel_id=1, source_target_pairs={{0,4},{4,0},{1,5},{5,1},{2,6},{6,2},{3,7},{7,3},{8,12},{12,8},{9,1... | collective-permute-start | bytes 1572872 | tf_op jit(solution)/shard_map/ppermute | solution.py:384
  210.6 1.9 collective-permute-start.2
  212.5 4.4 %collective-permute-done.2 = f32[256,128]{1,0:T(8,128)S(1)} collective-permute-done((f32[256,128]{1,0:T(8,128)S(1)}, f32[256,128]{1,0:T(8,128)S(1)}, u32[]{:S(2)}, u32[]{:S(2)}) %collective-permute-start.2) | collective-permute-done | bytes 131104 | tf_op jit(solution)/shard_map/ppermute | solution.py:359
  217.6 1.5 shard_map.103
  (43 shorter events, 14.4 us)
Async XLA Ops:
  7.2 1.0 copy-start.3
  8.1 0.7 copy-start.5
  10.8 20.6 %copy-start.6 = (f32[512,128]{1,0:T(8,128)S(1)}, f32[512,128]{1,0:T(8,128)}, u32[]{:S(2)}) copy-start(f32[512,128]{1,0:T(8,128)} %param.11) | copy-start | bytes 786436
  10.8 43.5 %all-to-all-start = ((f32[640,1,128]{2,1,0:T(1,128)}), f32[640,1,128]{2,1,0:T(1,128)S(1)}, u32[]{:S(2)}, u32[]{:S(2)}) async-start(f32[640,1,128]{2,1,0:T(1,128)} %bitcast.2), calls=%async_computation | async-start | bytes 655360 | tf_op jit(solution)/shard_map/all_to_all | solution.py:314
  31.3 53.0 %all-gather.3.cloned.1.call-start = ((), (), s32[]{:S(2)}) async-start(), calls=%async_computation.7 | async-start | bytes 1310720 | tf_op jit(solution)/shard_map/all_gather | solution.py:343
  31.4 5.6 %collective-permute-start.3 = (f32[256,128]{1,0:T(8,128)S(1)}, f32[256,128]{1,0:T(8,128)S(1)}, u32[]{:S(2)}, u32[]{:S(2)}) collective-permute-start(f32[256,128]{1,0:T(8,128)S(1)} %get-tuple-element.40), channel_id=1, source_target_pairs={{0,4},{4,8},{8,12},{12,16},{16,20},{20,24},{24,28},{28,32},{32,36}... | collective-permute-start | bytes 393224 | tf_op jit(solution)/shard_map/ppermute | solution.py:332
  55.9 6.1 %collective-permute-start = (f32[256,128]{1,0:T(8,128)S(1)}, f32[256,128]{1,0:T(8,128)S(1)}, u32[]{:S(2)}, u32[]{:S(2)}) collective-permute-start(f32[256,128]{1,0:T(8,128)S(1)} %get-tuple-element.23), channel_id=1, source_target_pairs={{0,4},{4,8},{8,12},{12,16},{16,20},{20,24},{24,28},{28,32},{32,36}... | collective-permute-start | bytes 393224 | tf_op jit(solution)/shard_map/ppermute | solution.py:332
  63.1 4.3 %copy-start.7 = (s32[512]{0:T(512)S(1)}, s32[512]{0:T(512)}, u32[]{:S(2)}) copy-start(s32[512]{0:T(512)} %param.10) | copy-start | bytes 6148
  63.1 21.3 %copy-start.4 = (f32[128,512]{1,0:T(8,128)S(1)}, f32[128,512]{1,0:T(8,128)}, u32[]{:S(2)}) copy-start(f32[128,512]{1,0:T(8,128)} %wout_ref.3) | copy-start | bytes 786436
  63.1 25.3 %all-to-all-start.1 = ((f32[4,512,128]{2,1,0:T(8,128)}), f32[4,512,128]{2,1,0:T(8,128)S(1)}, u32[]{:S(2)}, u32[]{:S(2)}) async-start(f32[4,512,128]{2,1,0:T(8,128)} %broadcast_in_dim.14), calls=%async_computation.1 | async-start | bytes 2097152 | tf_op jit(solution)/shard_map/all_to_all | solution.py:314
  67.4 8.0 %collective-permute-start.1 = (s32[256]{0:T(256)S(1)}, s32[256]{0:T(256)S(1)}, u32[]{:S(2)}, u32[]{:S(2)}) collective-permute-start(s32[256]{0:T(256)S(1)} %get-tuple-element.44), channel_id=1, source_target_pairs={{0,4},{4,8},{8,12},{12,16},{16,20},{20,24},{24,28},{28,32},{32,36}... | collective-permute-start | bytes 3080 | tf_op jit(solution)/shard_map/ppermute | solution.py:332
  84.3 1.2 copy-start
  85.6 2.9 %copy-start.2 = (f32[512,3,128]{2,0,1:T(8,128)S(1)}, f32[512,3,128]{2,0,1:T(8,128)}, u32[]{:S(2)}) copy-start(f32[512,3,128]{2,0,1:T(8,128)} %param.7) | copy-start | bytes 2359300
  95.2 6.3 %copy-start.1 = (f32[2048,128]{1,0:T(8,128)S(1)}, f32[2048,128]{1,0:T(8,128)}, u32[]{:S(2)}) copy-start(f32[2048,128]{1,0:T(8,128)} %all-gather.3.cloned.1.call-done) | copy-start | bytes 3145732
  103.5 5.9 %collective-permute-start.8 = (f32[16,64,128]{2,1,0:T(8,128)S(1)}, f32[16,64,128]{2,1,0:T(8,128)S(1)}, u32[]{:S(2)}, u32[]{:S(2)}) collective-permute-start(f32[16,64,128]{2,1,0:T(8,128)S(1)} %get-tuple-element.37), channel_id=1, source_target_pairs={{0,4},{4,0},{1,5},{5,1},{2,6},{6,2},{3,7},{7,3},{8,12},{12,8},{9,1... | collective-permute-start | bytes 1572872 | tf_op jit(solution)/shard_map/ppermute | solution.py:371
  110.2 31.8 %all-to-all-start.2 = ((f32[16,64,128]{2,1,0:T(8,128)}), f32[16,64,128]{2,1,0:T(8,128)S(1)}, u32[]{:S(2)}, u32[]{:S(2)}) async-start(f32[16,64,128]{2,1,0:T(8,128)} %add.5), calls=%async_computation.3 | async-start | bytes 1048576 | tf_op jit(solution)/shard_map/all_to_all | solution.py:314
  118.4 11.0 %collective-permute-start.4 = (f32[512,128]{1,0:T(8,128)S(1)}, f32[512,128]{1,0:T(8,128)S(1)}, u32[]{:S(2)}, u32[]{:S(2)}) collective-permute-start(f32[512,128]{1,0:T(8,128)S(1)} %get-tuple-element.31), channel_id=1, source_target_pairs={{0,2},{1,3},{2,0},{3,1},{4,6},{5,7},{6,4},{7,5},{8,10},{9,11},{10,... | collective-permute-start | bytes 786440 | tf_op jit(solution)/shard_map/ppermute | solution.py:366
  122.9 12.3 %collective-permute-start.5 = (f32[512,128]{1,0:T(8,128)S(1)}, f32[512,128]{1,0:T(8,128)S(1)}, u32[]{:S(2)}, u32[]{:S(2)}) collective-permute-start(f32[512,128]{1,0:T(8,128)S(1)} %get-tuple-element.32), channel_id=1, source_target_pairs={{0,1},{1,2},{2,3},{3,0},{4,5},{5,6},{6,7},{7,4},{8,9},{9,10},{10,1... | collective-permute-start | bytes 786440 | tf_op jit(solution)/shard_map/ppermute | solution.py:366
  124.8 10.3 %collective-permute-start.6 = (f32[512,128]{1,0:T(8,128)S(1)}, f32[512,128]{1,0:T(8,128)S(1)}, u32[]{:S(2)}, u32[]{:S(2)}) collective-permute-start(f32[512,128]{1,0:T(8,128)S(1)} %get-tuple-element.33), channel_id=1, source_target_pairs={{0,3},{1,0},{2,1},{3,2},{4,7},{5,4},{6,5},{7,6},{8,11},{9,8},{10,9... | collective-permute-start | bytes 786440 | tf_op jit(solution)/shard_map/ppermute | solution.py:366
  135.2 6.8 %collective-permute-start.7 = (f32[256,128]{1,0:T(8,128)S(1)}, f32[256,128]{1,0:T(8,128)S(1)}, u32[]{:S(2)}, u32[]{:S(2)}) collective-permute-start(f32[256,128]{1,0:T(8,128)S(1)} %get-tuple-element.35), channel_id=1, source_target_pairs={{4,0},{8,4},{12,8},{16,12},{20,16},{24,20},{28,24},{32,28},{36,32}... | collective-permute-start | bytes 393224 | tf_op jit(solution)/shard_map/ppermute | solution.py:376
  143.7 41.3 %all-to-all-start.3 = ((f32[768,1,128]{2,1,0:T(1,128)}), f32[768,1,128]{2,1,0:T(1,128)S(1)}, u32[]{:S(2)}, u32[]{:S(2)}) async-start(f32[768,1,128]{2,1,0:T(1,128)} %bitcast.11), calls=%async_computation.4 | async-start | bytes 786432 | tf_op jit(solution)/shard_map/all_to_all | solution.py:314
  159.6 50.0 %reduce-scatter.2.cloned.1.call-start = ((), (), s32[]{:S(2)}) async-start(), calls=%async_computation.6 | async-start | bytes 1310720 | tf_op jit(solution)/shard_map/reduce_scatter | solution.py:358
  205.0 14.2 %collective-permute-start.9 = (f32[16,64,128]{2,1,0:T(8,128)S(1)}, f32[16,64,128]{2,1,0:T(8,128)S(1)}, u32[]{:S(2)}, u32[]{:S(2)}) collective-permute-start(f32[16,64,128]{2,1,0:T(8,128)S(1)} %all_to_all.28.mine_ref), channel_id=1, source_target_pairs={{0,4},{4,0},{1,5},{5,1},{2,6},{6,2},{3,7},{7,3},{8,12},{12,8},{9,1... | collective-permute-start | bytes 1572872 | tf_op jit(solution)/shard_map/ppermute | solution.py:384
  210.6 6.3 %collective-permute-start.2 = (f32[256,128]{1,0:T(8,128)S(1)}, f32[256,128]{1,0:T(8,128)S(1)}, u32[]{:S(2)}, u32[]{:S(2)}) collective-permute-start(f32[256,128]{1,0:T(8,128)S(1)} %get-tuple-element.43), channel_id=1, source_target_pairs={{4,0},{8,4},{12,8},{16,12},{20,16},{24,20},{28,24},{32,28},{36,32}... | collective-permute-start | bytes 393224 | tf_op jit(solution)/shard_map/ppermute | solution.py:359
Sparse Core Ops, SparseCore 0:
  37.9 46.4 all-gather.2
  163.2 29.4 reduce-scatter.1

commit v4 on v3

v4 whole, which is shorter than its diff:
```python
import functools
import math

import jax
import jax.numpy as jnp
from jax import lax
from jax.experimental import pallas as pl
from jax.experimental.pallas import tpu as pltpu
from jax.sharding import PartitionSpec as P

D = 512
HEADS = 16
PATCH = 512
HALF = PATCH // 2
HEAD = D // HEADS
WIDTH = 128
HERE = WIDTH // HEAD
CURVE = ("far", "near", "x", "core")
PLANE = ("near", "x")
BLOCKS = 16
SIDE = WIDTH // 2
ADDED = 2
BF = jnp.bfloat16
F32 = jnp.float32
SCALE = 1.0 / math.sqrt(HEAD)
LOG2E = math.log2(math.e)

NN = (((1,), (0,)), ((), ()))
NT = (((1,), (1,)), ((), ()))


def mm(a, b, dims=NN):
    return lax.dot_general(a, b, dims, preferred_element_type=F32)


def split(x):
    high = x.astype(BF)
    return high, (x - high.astype(F32)).astype(BF)


def split3(x):
    high, rest = x.astype(BF), None
    rest = x - high.astype(F32)
    mid = rest.astype(BF)
    return high, mid, (rest - mid.astype(F32)).astype(BF)


def mm3(a, b, dims=NN):
    (ah, al), (bh, bl) = a, b
    return mm(ah, bh, dims) + (mm(ah, bl, dims) + mm(al, bh, dims))


def select_rows(pick, x):
    high, mid, low = split3(x)
    return mm(pick, high) + (mm(pick, mid) + mm(pick, low))


def column(row):
    return jnp.transpose(jnp.broadcast_to(row, (WIDTH, row.shape[1])))


def wide(col, width=PATCH):
    return jnp.concatenate([col] * (width // WIDTH), axis=1)


def iota(dim, shape=(PATCH, PATCH)):
    return lax.broadcasted_iota(jnp.int32, shape, dim).astype(F32)


def one_hot(condition):
    return jnp.where(condition, 1.0, 0.0).astype(BF)


def every(ref, first, step):
    return ref[pl.ds(first, ref.shape[0] // step, stride=step), :]


def sort_kernel(each, dest_ref, feat_ref, message_ref, index_ref):
    peers = PATCH // each
    dest = dest_ref[...]
    block = dest // PATCH
    local = (dest - block * PATCH).astype(F32)
    block = block.astype(F32)
    same = (wide(column(block)) == block) & (iota(0) < iota(1))
    rank = jnp.sum(jnp.where(same, 1.0, 0.0), axis=0, keepdims=True)
    index = rank * peers + block
    index_ref[...] = index
    rows = select_rows(one_hot(iota(0) == index), feat_ref[...])
    for turn in range(each):
        message_ref[pl.ds(turn, peers, stride=each + 1), :] = rows[turn * peers : (turn + 1) * peers]
    high, low = split(jnp.where(iota(1, (PATCH, WIDTH)) == column(rank), column(local), 0.0))
    mine = one_hot(iota(0, (peers, PATCH)) == block)
    message_ref[pl.ds(each, peers, stride=each + 1), :] = mm(mine, high) + mm(mine, low)


def place_kernel(each, message_ref, valid_ref, after_ref, low_ref, high_ref, position_ref, bias_ref):
    del after_ref
    turned = jnp.transpose(every(message_ref, each, each + 1))
    position = jnp.concatenate([turned[turn : turn + 1] for turn in range(each)], axis=1)
    position_ref[...] = position
    arrived = jnp.concatenate([every(message_ref, turn, each + 1) for turn in range(each)], axis=0)
    placed = select_rows(one_hot(iota(0) == position), arrived)
    low_ref[...] = placed[:HALF]
    high_ref[...] = placed[HALF:]
    bias_ref[...] = column(jnp.where(valid_ref[...] > 0, 0.0, -jnp.inf))


def add_kernel(parts_ref, early_ref, late_ref):
    total = parts_ref[0] + parts_ref[1] + (parts_ref[2] + parts_ref[3])
    early_ref[...] = total[:HALF]
    late_ref[...] = total[HALF:]


def pack_kernel(each, position_ref, low_ref, high_ref, sums_ref, message_ref):
    peers = PATCH // each
    size = each + ADDED
    grads = jnp.concatenate([low_ref[...], high_ref[...]], axis=0)
    rows = select_rows(one_hot(wide(column(position_ref[...])) == iota(1)), grads)
    for turn in range(each):
        message_ref[pl.ds(turn, peers, stride=size), :] = rows[turn * peers : (turn + 1) * peers]
    sums = sums_ref[0]
    for part in range(1, sums_ref.shape[0]):
        sums += sums_ref[part]
    near = SIDE // ADDED
    for turn in range(ADDED):
        rows = jnp.concatenate([sums[turn * near : (turn + 1) * near]] * (peers // near), axis=0)
        message_ref[pl.ds(each + turn, peers, stride=size), :] = rows


def unpack_kernel(each, message_ref, sums_ref):
    near = SIDE // ADDED
    for turn in range(ADDED):
        rows = every(message_ref, each + turn, each + ADDED)
        total = rows[:near]
        for far in range(1, rows.shape[0] // near):
            total += rows[far * near : (far + 1) * near]
        sums_ref[turn * near : (turn + 1) * near] = total


def unsort_kernel(each, index_ref, message_ref, out_ref):
    returned = jnp.concatenate([every(message_ref, turn, each + ADDED) for turn in range(each)], axis=0)
    out_ref[...] = select_rows(one_hot(wide(column(index_ref[...])) == iota(1)), returned)


def finish_kernel(core_ref, mine_ref, other_ref, din_ref, dout_ref, out_ref):
    core = core_ref[0]
    near = SIDE // ADDED
    for own, ref in ((core, mine_ref), (1 - core, other_ref)):
        for block in range(BLOCKS):
            t, part = divmod(block, D // WIDTH)
            for side in range(2):
                for turn in range(ADDED):
                    got = ref[:, turn * near + 2 * block + side, :]
                    first = side * SIDE + turn * near + own
                    if t < 3:
                        din_ref[t, pl.ds(part * WIDTH + first, BLOCKS, stride=2), :] = got
                    else:
                        out_ref[part, pl.ds(first, BLOCKS, stride=2), :] = got
    for part in range(D // WIDTH):
        dout_ref[:, part * WIDTH : (part + 1) * WIDTH] = out_ref[part]


def head_mask(head):
    lanes = lax.broadcasted_iota(jnp.int32, (PATCH, WIDTH), 1)
    return (lanes // HEAD) == head


def scores_of(queries, key_rows, mask):
    qh, ql = split(queries)
    kh, kl = split(jnp.where(mask, key_rows, 0.0))
    keys = jnp.concatenate([kh, kl], axis=1)
    return mm(keys, jnp.concatenate([qh, qh], axis=1), NT) + mm(
        keys, jnp.concatenate([ql, ql], axis=1), NT
    )


def forward_kernel(x_ref, win_ref, wout_ref, bias_ref, qkv_ref, att_ref, lse_ref, out_ref, vt_ref):
    parts = [split(x_ref[part]) for part in range(D // WIDTH)]
    for t in range(3):
        total = jnp.zeros((PATCH, WIDTH), F32)
        for part in range(D // WIDTH):
            total += mm3(parts[part], split(win_ref[t, part * WIDTH : (part + 1) * WIDTH]))
        qkv_ref[t] = total
    vt_ref[...] = jnp.transpose(qkv_ref[2])
    bias = wide(bias_ref[...])

    def one(head, carry):
        mask = head_mask(head)
        scores = scores_of(qkv_ref[0] * (SCALE * LOG2E), qkv_ref[1], mask) + bias
        top = jnp.max(scores, axis=0, keepdims=True)
        weights = jnp.exp2(scores - top)
        total = jnp.sum(weights, axis=0, keepdims=True)
        rows = pl.ds(pl.multiple_of(head * HEAD, HEAD), HEAD)
        vh, vl = split(vt_ref[rows, :])
        wh, wl = split(weights)
        both = mm(jnp.concatenate([vh, vl], axis=0), wh)
        attended = both[:HEAD] + both[HEAD:] + mm(vh, wl)
        att_ref[rows, :] = attended / total
        lse_ref[pl.ds(head, 1), :] = top + jnp.log2(total)
        return carry

    lax.fori_loop(0, HERE, one, 0)
    attended = split(jnp.transpose(att_ref[...]))
    for part in range(D // WIDTH):
        out_ref[part] = mm3(attended, split(wout_ref[:, part * WIDTH : (part + 1) * WIDTH]))


def backward_kernel(
    qkv_ref, att_ref, lse_ref, before_ref, cot_ref, wout_ref, bias_ref, dqkv_ref, kt_ref, gt_ref, dqt_ref, grad_ref
):
    for rows, ref, first in ((slice(0, HALF), before_ref, 0), (slice(HALF, PATCH), cot_ref, 0)):
        total = jnp.zeros((HALF, WIDTH), F32)
        for part in range(D // WIDTH):
            lanes = slice(part * WIDTH, (part + 1) * WIDTH)
            total += mm3(split(ref[part, first : first + HALF]), split(wout_ref[:, lanes]), NT)
        grad_ref[rows] = total
    kt_ref[...] = jnp.transpose(qkv_ref[1])
    gt_ref[...] = jnp.transpose(grad_ref[...])
    bias = wide(bias_ref[...])
    dqkv_ref[1] = jnp.zeros((PATCH, WIDTH), F32)
    dqkv_ref[2] = jnp.zeros((PATCH, WIDTH), F32)

    def one(head, carry):
        mask = head_mask(head)
        rows = pl.ds(pl.multiple_of(head * HEAD, HEAD), HEAD)
        scores = scores_of(qkv_ref[0] * (SCALE * LOG2E), qkv_ref[1], mask) + bias
        probs = jnp.exp2(scores - lse_ref[pl.ds(head, 1), :])
        ph, plo = split(probs)
        grad_probs = scores_of(grad_ref[...], qkv_ref[2], mask)
        gh, gl = split(jnp.where(mask, grad_ref[...], 0.0))
        both = mm(ph, jnp.concatenate([gh, gl], axis=1))
        dqkv_ref[2] += both[:, :WIDTH] + both[:, WIDTH:] + mm(plo, gh)
        inner = jnp.sum(gt_ref[rows, :] * att_ref[rows, :], axis=0, keepdims=True)
        grad_scores = probs * (grad_probs - inner)
        sh, sl = split(grad_scores)
        qh, ql = split(jnp.where(mask, qkv_ref[0] * SCALE, 0.0))
        both = mm(sh, jnp.concatenate([qh, ql], axis=1))
        dqkv_ref[1] += both[:, :WIDTH] + both[:, WIDTH:] + mm(sl, qh)
        kh, kl = split(kt_ref[rows, :] * SCALE)
        both = mm(jnp.concatenate([kh, kl], axis=0), sh)
        dqt_ref[rows, :] = both[:HEAD] + both[HEAD:] + mm(kh, sl)
        return carry

    lax.fori_loop(0, HERE, one, 0)
    dqkv_ref[0] = jnp.transpose(dqt_ref[...])


def weights_kernel(core_ref, x_ref, dqkv_ref, att_ref, before_ref, cot_ref, after_ref, keep_ref, send_ref):
    del after_ref
    second = core_ref[0] == 1

    def put(block, grads):
        top, bottom = grads[:SIDE], grads[SIDE:]
        keep_ref[block] = jnp.where(second, bottom, top)
        send_ref[block] = jnp.where(second, top, bottom)

    attended = split(att_ref[...])
    parts = [split(x_ref[part]) for part in range(D // WIDTH)]
    for t in range(3):
        grads = split(jnp.transpose(dqkv_ref[t]))
        for part in range(D // WIDTH):
            put(t * (D // WIDTH) + part, jnp.transpose(mm3(grads, parts[part])))
    for part in range(D // WIDTH):
        cot = jnp.concatenate([before_ref[part], cot_ref[part, :HALF]], axis=0)
        put(3 * (D // WIDTH) + part, mm3(attended, split(cot)))


def rows_kernel(dqkv_ref, win_ref, dx_ref, done_ref):
    done_ref[...] = jnp.zeros_like(done_ref)
    grads = [split(dqkv_ref[t]) for t in range(3)]
    for part in range(D // WIDTH):
        total = jnp.zeros((PATCH, WIDTH), F32)
        for t in range(3):
            total += mm3(grads[t], split(win_ref[t, part * WIDTH : (part + 1) * WIDTH]), NT)
        dx_ref[part] = total


def call(kernel, outs, *args, scratch=(), scalars=0, room=8, flops=10**9):
    size = sum(math.prod(a.shape) * 4 for a in (*args, *outs))
    return pl.pallas_call(
        kernel,
        out_shape=tuple(jax.ShapeDtypeStruct(o, F32) for o in [x.shape for x in outs]),
        in_specs=[pl.BlockSpec(memory_space=pltpu.SMEM)] * scalars
        + [pl.BlockSpec(memory_space=pltpu.VMEM)] * (len(args) - scalars),
        out_specs=tuple(pl.BlockSpec(memory_space=pltpu.VMEM) for _ in outs),
        scratch_shapes=[pltpu.VMEM(s, F32) for s in scratch],
        compiler_params=pltpu.CompilerParams(vmem_limit_bytes=room * 2**20),
        cost_estimate=pl.CostEstimate(flops=flops, bytes_accessed=size, transcendentals=0),
    )(*args)


def of(*shape):
    return jax.ShapeDtypeStruct(shape, F32)


def swap(x, axis):
    return lax.all_to_all(x, axis, split_axis=0, concat_axis=0, tiled=True)


def spread_to(x, axis):
    peers = lax.axis_size(axis)
    return swap(jnp.broadcast_to(x[None], (peers,) + x.shape).reshape(-1, WIDTH), axis)


def shards(features, input_proj, output_proj, destination, real_points, cotangent):
    peers = lax.axis_size(CURVE)
    each = PATCH // peers
    up = [(i, (i + 1) % peers) for i in range(peers)]
    down = [(j, i) for i, j in up]
    core = lax.axis_index("core").astype(jnp.int32).reshape(1)

    def to_patch(low, high):
        return jnp.concatenate([lax.ppermute(high, CURVE, up), low], axis=0)

    def exchange(message):
        rows = message.shape[0]
        return swap(message.reshape(rows, 1, WIDTH), CURVE).reshape(rows, WIDTH)

    cot = lax.all_gather(cotangent, "head", axis=0)
    message, index = call(
        functools.partial(sort_kernel, each), [of(PATCH + peers, WIDTH), of(1, PATCH)],
        destination.reshape(1, PATCH), features,
    )
    arrived = exchange(message)
    win = jnp.transpose(input_proj, (1, 0, 2))
    valid = to_patch(real_points[:HALF], real_points[HALF:]).reshape(1, PATCH)
    low, high, position, bias = call(
        functools.partial(place_kernel, each),
        [of(HALF, WIDTH), of(HALF, WIDTH), of(1, PATCH), of(PATCH, WIDTH)], arrived, valid, cot[0, :8],
    )
    x = spread_to(to_patch(low, high), "head").reshape(D // WIDTH, PATCH, WIDTH)
    qkv, attended, lse, out = call(
        forward_kernel,
        [of(3, PATCH, WIDTH), of(WIDTH, PATCH), of(HERE, PATCH), of(D // WIDTH, PATCH, WIDTH)],
        x, win, output_proj, bias, scratch=[(WIDTH, PATCH)], room=16,
    )
    out = lax.psum_scatter(out, "head", scatter_dimension=0)
    branch_out = jnp.concatenate([out[HALF:], lax.ppermute(out[:HALF], CURVE, down)], axis=0)
    before = lax.ppermute(cot[:, HALF:], CURVE, up)
    (dqkv,) = call(
        backward_kernel, [of(3, PATCH, WIDTH)], qkv, attended, lse, before, cot, output_proj, bias,
        scratch=[(WIDTH, PATCH)] * 3 + [(PATCH, WIDTH)], room=16,
    )
    dx, done = call(rows_kernel, [of(D // WIDTH, PATCH, WIDTH), of(8, WIDTH)], dqkv, win)
    dx = swap(dx.reshape(-1, WIDTH), "head").reshape(D // WIDTH, PATCH, WIDTH)
    early, late = call(add_kernel, [of(HALF, WIDTH)] * 2, dx)
    keep, send = call(
        weights_kernel, [of(BLOCKS, SIDE, WIDTH)] * 2, core, x, dqkv, attended, before, cot, done, scalars=1
    )
    sums = keep + lax.ppermute(send, "core", [(0, 1), (1, 0)])
    sums, early = lax.optimization_barrier((sums, early))
    sums = swap(sums.reshape(-1, WIDTH), PLANE).reshape(BLOCKS, SIDE, WIDTH)
    (message,) = call(
        functools.partial(pack_kernel, each), [of(peers * (each + ADDED), WIDTH)],
        position, late, lax.ppermute(early, CURVE, down), sums,
    )
    message = exchange(message)
    (sums,) = call(functools.partial(unpack_kernel, each), [of(SIDE, WIDTH)], message)
    (grad_features,) = call(functools.partial(unsort_kernel, each), [of(PATCH, WIDTH)], index, message)
    sums, branch_out = lax.optimization_barrier((sums, branch_out))
    sums = spread_to(sums, PLANE).reshape(BLOCKS, SIDE, WIDTH)
    sums, grad_features = lax.optimization_barrier((sums, grad_features))
    grad_inproj, grad_outproj = call(
        finish_kernel, [of(3, D, WIDTH), of(WIDTH, D)],
        core, sums, lax.ppermute(sums, "core", [(0, 1), (1, 0)]), scalars=1,
        scratch=[(D // WIDTH, WIDTH, WIDTH)],
    )
    return (branch_out, grad_features, jnp.transpose(grad_inproj, (1, 0, 2)), grad_outproj)


def solution(mesh):
    curve, head = mesh.devices.shape
    sizes = (curve // 32, 4, 4, 2)
    fine = jax.sharding.Mesh(mesh.devices.reshape(*sizes, head), CURVE + ("head",))
    return jax.shard_map(
        shards,
        mesh=fine,
        in_specs=(
            P(CURVE, "head"),
            P(None, None, "head"),
            P("head", None),
            P(CURVE),
            P(CURVE),
            P(CURVE, "head"),
        ),
        out_specs=(P(CURVE, "head"), P(CURVE, "head"), P(None, None, "head"), P("head", None)),
        check_vma=False,
    )
```

time: 228 us -> 211 us (0.925)
  blocking collectives: 19.6 us -> 0 us
  starting transfers between devices: 84.7 us -> 93.9 us
  waiting for transfers between devices: 75.1 us -> 67.7 us
  local copies, waits for them, and re-layouts: 5.09 us -> 9.57 us
  Pallas kernels: 26.4 us -> 23.1 us
    all_to_all x1 -> x0, blocking collectives: 19.6 us -> none  [swap(): return lax.all_to_all(x, axis, split_axis=0, concat_axis=0, tiled=True)]
    all_to_all x4 -> x6, starting transfers between devices: 47.5 us -> 60 us  [swap(): return lax.all_to_all(x, axis, split_axis=0, concat_axis=0, tiled=True)]
    ppermute x3 -> x1, starting transfers between devices: 11 us -> 4.62 us  [shards(): before = lax.ppermute(cot[:, HALF:], CURVE, up)]
    ppermute x3 -> x1, waiting for transfers between devices: 5.74 us -> 0.01 us  [shards(): before = lax.ppermute(cot[:, HALF:], CURVE, up)]
    ppermute x3 -> x2, waiting for transfers between devices: 7.37 us -> 2.63 us  [to_patch(): return jnp.concatenate([lax.ppermute(high, CURVE, up), low], axis=0)]
    ppermute x3 -> x2, starting transfers between devices: 12.3 us -> 7.71 us  [to_patch(): return jnp.concatenate([lax.ppermute(high, CURVE, up), low], axis=0)]
    all_to_all x4 -> x6, waiting for transfers between devices: 43.5 us -> 38.9 us  [swap(): return lax.all_to_all(x, axis, split_axis=0, concat_axis=0, tiled=True)]
    ppermute x1, starting transfers between devices: 4.38 us -> 7.76 us  [shards(): sums = keep + lax.ppermute(send, 'core', [(0, 1), (1, 0)])]
  transfers between devices with their start and end apart: 16 -> 15, of which waited for: 11 -> 13; matrix products, arithmetic and copies ran while one was open for 2% -> 2% of each run, Pallas kernels for 3% -> 6%
where the time goes in v4:
time: 211 us; the launch traced here: 210 us
  starting transfers between devices  93.9 us (45%)
  waiting for transfers between devices  67.7 us (32%)
  Pallas kernels  23.1 us (11%)
  between operations  14.3 us (7%)
  local copies, waits for them, and re-layouts  9.57 us (5%)
    all_to_all x6, starting transfers between devices, swap(): return lax.all_to_all(x, axis, split_axis=0, concat_axis=0, tiled=True)  60 us
    all_to_all x6, waiting for transfers between devices, swap(): return lax.all_to_all(x, axis, split_axis=0, concat_axis=0, tiled=True)  38.9 us
    pallas_call x11, Pallas kernels, call(): pl.pallas_call(kernel, out_shape=tuple((jax.ShapeDtypeStruct(o, F32) for...  23.1 us
    all_gather x1, waiting for transfers between devices, shards(): cot = lax.all_gather(cotangent, 'head', axis=0)  11 us
    ppermute x1, starting transfers between devices, shards(): sums = keep + lax.ppermute(send, 'core', [(0, 1), (1, 0)])  7.76 us
    ppermute x2, starting transfers between devices, to_patch(): return jnp.concatenate([lax.ppermute(high, CURVE, up), low], axis=0)  7.71 us
    ppermute x1, waiting for transfers between devices, shards(): lax.ppermute(early, CURVE, down)  5.37 us
    unnamed x24, local copies, waits for them, and re-layouts  5.18 us
  transfers between devices with their start and end apart: 15, of which 13 were waited for; matrix products, arithmetic and copies ran while one was open for 2% of the time, Pallas kernels for 6%

profile of v4, /device:TPU:1, one launch (start us, length us, event | category | flops | bytes accessed | tf_op | source)
XLA Modules:
  0.0 210.2 jit_solution(11859024635630733854)
XLA Ops:
  8.8 1.6 shard_map.93
  10.4 20.5 %all-to-all-start = ((f32[640,1,128]{2,1,0:T(1,128)}), f32[640,1,128]{2,1,0:T(1,128)S(1)}, u32[]{:S(2)}, u32[]{:S(2)}) async-start(f32[640,1,128]{2,1,0:T(1,128)} %bitcast.2), calls=%async_computation | async-start | bytes 655360 | tf_op jit(solution)/shard_map/all_to_all | solution.py:297
  30.9 3.5 %collective-permute-start = (s32[256]{0:T(256)S(1)}, s32[256]{0:T(256)S(1)}, u32[]{:S(2)}, u32[]{:S(2)}) collective-permute-start(s32[256]{0:T(256)S(1)} %get-tuple-element.54), channel_id=1, source_target_pairs={{0,4},{4,8},{8,12},{12,16},{16,20},{20,24},{24,28},{28,32},{32,36}... | collective-permute-start | bytes 3080 | tf_op jit(solution)/shard_map/ppermute | solution.py:313
  35.2 11.0 %all-gather.3.cloned.1.call-done = f32[2048,128]{1,0:T(8,128)} async-done(((f32[512,128]{1,0:T(8,128)}), f32[2048,128]{1,0:T(8,128)}) %all-gather.3.cloned.1.call-update) | async-done | bytes 1048592 | tf_op jit(solution)/shard_map/all_gather | solution.py:319
  46.9 7.0 %all-to-all-done = f32[640,1,128]{2,1,0:T(1,128)S(1)} async-done(((f32[640,1,128]{2,1,0:T(1,128)}), f32[640,1,128]{2,1,0:T(1,128)S(1)}, u32[]{:S(2)}, u32[]{:S(2)}) %all-to-all-start) | async-done | bytes 327712 | tf_op jit(solution)/shard_map/all_to_all | solution.py:297
  54.5 4.2 %collective-permute-start.1 = (f32[256,128]{1,0:T(8,128)S(1)}, f32[256,128]{1,0:T(8,128)S(1)}, u32[]{:S(2)}, u32[]{:S(2)}) collective-permute-start(f32[256,128]{1,0:T(8,128)S(1)} %get-tuple-element.30), channel_id=1, source_target_pairs={{0,4},{4,8},{8,12},{12,16},{16,20},{20,24},{24,28},{28,32},{32,36}... | collective-permute-start | bytes 393224 | tf_op jit(solution)/shard_map/ppermute | solution.py:313
  58.7 1.9 collective-permute-done.1
  61.7 4.3 %all-to-all-start.1 = ((f32[4,512,128]{2,1,0:T(8,128)}), f32[4,512,128]{2,1,0:T(8,128)S(1)}, u32[]{:S(2)}, u32[]{:S(2)}) async-start(f32[4,512,128]{2,1,0:T(8,128)} %broadcast_in_dim.4), calls=%async_computation.1 | async-start | bytes 2097152 | tf_op jit(solution)/shard_map/all_to_all | solution.py:297
  66.9 4.6 %collective-permute-start.2 = (f32[4,256,128]{2,1,0:T(8,128)}, f32[4,256,128]{2,1,0:T(8,128)S(1)}, u32[]{:S(2)}, u32[]{:S(2)}) collective-permute-start(f32[4,256,128]{2,1,0:T(8,128)} %slice.33), channel_id=1, source_target_pairs={{0,4},{4,8},{8,12},{12,16},{16,20},{20,24},{24,28},{28,32},{32,36}... | collective-permute-start | bytes 1572872 | tf_op jit(solution)/shard_map/ppermute | solution.py:339
  71.5 4.7 %all-to-all-done.1.x_ref = f32[4,512,128]{2,1,0:T(8,128)S(1)} async-done(((f32[4,512,128]{2,1,0:T(8,128)}), f32[4,512,128]{2,1,0:T(8,128)S(1)}, u32[]{:S(2)}, u32[]{:S(2)}) %all-to-all-start.1) | async-done | bytes 1048608 | tf_op jit(solution)/shard_map/all_to_all | solution.py:297
  76.2 1.1 copy-done.7
  77.4 6.7 %shard_map.95 = (f32[3,512,128]{2,1,0:T(8,128)S(1)}, f32[128,512]{1,0:T(8,128)S(1)}, f32[4,512]{1,0:T(4,128)S(1)}, f32[4,512,128]{2,1,0:T(8,128)}) custom-call(f32[4,512,128]{2,1,0:T(8,128)S(1)} %all-to-all-done.1.x_ref, f32[3,512,128]{2,1,0:T(8,128)S(1)} %bitcast.28, f32[128,512]{1,0:T(8,128)S(1)} %copy-done.6, f32[512,128]{1,0:T(8,128)S(1)} %get-tuple-element.32.bias_ref), custom_call_target="tpu_custom_call" | custom-call | flops 1000000000 | bytes 4464640 | tf_op jit(solution)/shard_map/pallas_call | solution.py:280
  84.1 6.7 %shard_map.96.dqkv_ref = f32[3,512,128]{2,1,0:T(8,128)S(1)} custom-call(f32[3,512,128]{2,1,0:T(8,128)S(1)} %get-tuple-element.33.qkv_ref, f32[128,512]{1,0:T(8,128)S(1)} %get-tuple-element.34.att_ref, f32[4,512]{1,0:T(4,128)S(1)} %get-tuple-element.35.lse_ref, f32[4,256,128]{2,1,0:T(8,128)S(1)} %collective-permute-done.2.before_ref, ...), custom_call_target="tpu_custom_call" | custom-call | flops 1000000000 | bytes 3940352 | tf_op jit(solution)/shard_map/pallas_call | solution.py:280
  90.8 1.4 shard_map.97
  93.2 3.5 %all-to-all-start.2 = ((f32[4,512,128]{2,1,0:T(8,128)}), f32[4,512,128]{2,1,0:T(8,128)S(1)}, u32[]{:S(2)}, u32[]{:S(2)}) async-start(f32[4,512,128]{2,1,0:T(8,128)} %copy-done.1), calls=%async_computation.2 | async-start | bytes 2097152 | tf_op jit(solution)/shard_map/all_to_all | solution.py:297
  98.9 1.9 shard_map.99
  100.7 7.8 %collective-permute-start.3 = (f32[16,64,128]{2,1,0:T(8,128)S(1)}, f32[16,64,128]{2,1,0:T(8,128)S(1)}, u32[]{:S(2)}, u32[]{:S(2)}) collective-permute-start(f32[16,64,128]{2,1,0:T(8,128)S(1)} %get-tuple-element.40), channel_id=1, source_target_pairs={{0,4},{4,0},{1,5},{5,1},{2,6},{6,2},{3,7},{7,3},{8,12},{12,8},{9,1... | collective-permute-start | bytes 1572872 | tf_op jit(solution)/shard_map/ppermute | solution.py:350
  108.5 1.5 collective-permute-done.3
  110.9 8.8 %all-to-all-start.3 = ((f32[16,64,128]{2,1,0:T(8,128)}), f32[16,64,128]{2,1,0:T(8,128)S(1)}, u32[]{:S(2)}, u32[]{:S(2)}) async-start(f32[16,64,128]{2,1,0:T(8,128)} %add.5), calls=%async_computation.3 | async-start | bytes 1048576 | tf_op jit(solution)/shard_map/all_to_all | solution.py:297
  120.5 5.1 %collective-permute-start.4 = (f32[256,128]{1,0:T(8,128)S(1)}, f32[256,128]{1,0:T(8,128)S(1)}, u32[]{:S(2)}, u32[]{:S(2)}) collective-permute-start(f32[256,128]{1,0:T(8,128)S(1)} %get-tuple-element.42), channel_id=1, source_target_pairs={{4,0},{8,4},{12,8},{16,12},{20,16},{24,20},{28,24},{32,28},{36,32}... | collective-permute-start | bytes 393224 | tf_op jit(solution)/shard_map/ppermute | solution.py:355
  125.6 5.4 %collective-permute-done.4.high_ref = f32[256,128]{1,0:T(8,128)S(1)} collective-permute-done((f32[256,128]{1,0:T(8,128)S(1)}, f32[256,128]{1,0:T(8,128)S(1)}, u32[]{:S(2)}, u32[]{:S(2)}) %collective-permute-start.4) | collective-permute-done | bytes 131104 | tf_op jit(solution)/shard_map/ppermute | solution.py:355
  131.4 1.4 shard_map.100
  132.8 16.7 %all-to-all-start.4 = ((f32[768,1,128]{2,1,0:T(1,128)}), f32[768,1,128]{2,1,0:T(1,128)S(1)}, u32[]{:S(2)}, u32[]{:S(2)}) async-start(f32[768,1,128]{2,1,0:T(1,128)} %bitcast.10), calls=%async_computation.4 | async-start | bytes 786432 | tf_op jit(solution)/shard_map/all_to_all | solution.py:297
  151.5 4.0 %collective-permute-start.5 = (f32[256,128]{1,0:T(8,128)S(1)}, f32[256,128]{1,0:T(8,128)S(1)}, u32[]{:S(2)}, u32[]{:S(2)}) collective-permute-start(f32[256,128]{1,0:T(8,128)S(1)} %get-tuple-element.53), channel_id=1, source_target_pairs={{4,0},{8,4},{12,8},{16,12},{20,16},{24,20},{28,24},{32,28},{36,32}... | collective-permute-start | bytes 393224 | tf_op jit(solution)/shard_map/ppermute | solution.py:338
  155.5 4.5 %collective-permute-done.5 = f32[256,128]{1,0:T(8,128)S(1)} collective-permute-done((f32[256,128]{1,0:T(8,128)S(1)}, f32[256,128]{1,0:T(8,128)S(1)}, u32[]{:S(2)}, u32[]{:S(2)}) %collective-permute-start.5) | collective-permute-done | bytes 131104 | tf_op jit(solution)/shard_map/ppermute | solution.py:338
  160.7 14.3 %all-to-all-done.4 = f32[768,1,128]{2,1,0:T(1,128)S(1)} async-done(((f32[768,1,128]{2,1,0:T(1,128)}), f32[768,1,128]{2,1,0:T(1,128)S(1)}, u32[]{:S(2)}, u32[]{:S(2)}) %all-to-all-start.4) | async-done | bytes 393248 | tf_op jit(solution)/shard_map/all_to_all | solution.py:297
  175.9 6.1 %all-to-all-start.5 = ((f32[16,64,128]{2,1,0:T(8,128)}), f32[16,64,128]{2,1,0:T(8,128)S(1)}, u32[]{:S(2)}, u32[]{:S(2)}) async-start(f32[16,64,128]{2,1,0:T(8,128)} %broadcast_in_dim.5), calls=%async_computation.6 | async-start | bytes 1048576 | tf_op jit(solution)/shard_map/all_to_all | solution.py:297
  182.0 1.3 shard_map.102
  183.3 12.4 %all-to-all-done.5.mine_ref = f32[16,64,128]{2,1,0:T(8,128)S(1)} async-done(((f32[16,64,128]{2,1,0:T(8,128)}), f32[16,64,128]{2,1,0:T(8,128)S(1)}, u32[]{:S(2)}, u32[]{:S(2)}) %all-to-all-start.5) | async-done | bytes 524320 | tf_op jit(solution)/shard_map/all_to_all | solution.py:297
  195.7 4.6 %collective-permute-start.6 = (f32[16,64,128]{2,1,0:T(8,128)S(1)}, f32[16,64,128]{2,1,0:T(8,128)S(1)}, u32[]{:S(2)}, u32[]{:S(2)}) collective-permute-start(f32[16,64,128]{2,1,0:T(8,128)S(1)} %all-to-all-done.5.mine_ref), channel_id=1, source_target_pairs={{0,4},{4,0},{1,5},{5,1},{2,6},{6,2},{3,7},{7,3},{8,12},{12,8},{9,1... | collective-permute-start | bytes 1572872 | tf_op jit(solution)/shard_map/ppermute | solution.py:365
  200.3 1.5 collective-permute-done.6.other_ref
  201.8 1.6 shard_map.103
  (45 shorter events, 14.3 us)
Async XLA Ops:
  7.2 1.0 copy-start.9
  7.2 39.0 %all-gather.3.cloned.1.call-start = ((), (), s32[]{:S(2)}) async-start(), calls=%async_computation.8 | async-start | bytes 1310720 | tf_op jit(solution)/shard_map/all_gather | solution.py:319
  8.1 0.7 copy-start.10
  10.4 20.5 %copy-start.11 = (s32[512]{0:T(512)S(1)}, s32[512]{0:T(512)}, u32[]{:S(2)}) copy-start(s32[512]{0:T(512)} %param.10) | copy-start | bytes 6148
  10.4 43.5 %all-to-all-start = ((f32[640,1,128]{2,1,0:T(1,128)}), f32[640,1,128]{2,1,0:T(1,128)S(1)}, u32[]{:S(2)}, u32[]{:S(2)}) async-start(f32[640,1,128]{2,1,0:T(1,128)} %bitcast.2), calls=%async_computation | async-start | bytes 655360 | tf_op jit(solution)/shard_map/all_to_all | solution.py:297
  30.9 4.3 %collective-permute-start = (s32[256]{0:T(256)S(1)}, s32[256]{0:T(256)S(1)}, u32[]{:S(2)}, u32[]{:S(2)}) collective-permute-start(s32[256]{0:T(256)S(1)} %get-tuple-element.54), channel_id=1, source_target_pairs={{0,4},{4,8},{8,12},{12,16},{16,20},{20,24},{24,28},{28,32},{32,36}... | collective-permute-start | bytes 3080 | tf_op jit(solution)/shard_map/ppermute | solution.py:313
  54.5 6.1 %collective-permute-start.1 = (f32[256,128]{1,0:T(8,128)S(1)}, f32[256,128]{1,0:T(8,128)S(1)}, u32[]{:S(2)}, u32[]{:S(2)}) collective-permute-start(f32[256,128]{1,0:T(8,128)S(1)} %get-tuple-element.30), channel_id=1, source_target_pairs={{0,4},{4,8},{8,12},{12,16},{16,20},{20,24},{24,28},{28,32},{32,36}... | collective-permute-start | bytes 393224 | tf_op jit(solution)/shard_map/ppermute | solution.py:313
  61.7 4.3 %copy-start = (f32[2048,128]{1,0:T(8,128)S(1)}, f32[2048,128]{1,0:T(8,128)}, u32[]{:S(2)}) copy-start(f32[2048,128]{1,0:T(8,128)} %all-gather.3.cloned.1.call-done) | copy-start | bytes 3145732
  61.7 14.5 %all-to-all-start.1 = ((f32[4,512,128]{2,1,0:T(8,128)}), f32[4,512,128]{2,1,0:T(8,128)S(1)}, u32[]{:S(2)}, u32[]{:S(2)}) async-start(f32[4,512,128]{2,1,0:T(8,128)} %broadcast_in_dim.4), calls=%async_computation.1 | async-start | bytes 2097152 | tf_op jit(solution)/shard_map/all_to_all | solution.py:297
  66.0 10.2 %copy-start.6 = (f32[128,512]{1,0:T(8,128)S(1)}, f32[128,512]{1,0:T(8,128)}, u32[]{:S(2)}) copy-start(f32[128,512]{1,0:T(8,128)} %wout_ref.3) | copy-start | bytes 786436
  66.9 17.2 %collective-permute-start.2 = (f32[4,256,128]{2,1,0:T(8,128)}, f32[4,256,128]{2,1,0:T(8,128)S(1)}, u32[]{:S(2)}, u32[]{:S(2)}) collective-permute-start(f32[4,256,128]{2,1,0:T(8,128)} %slice.33), channel_id=1, source_target_pairs={{0,4},{4,8},{8,12},{12,16},{16,20},{20,24},{24,28},{28,32},{32,36}... | collective-permute-start | bytes 1572872 | tf_op jit(solution)/shard_map/ppermute | solution.py:339
  76.2 1.1 copy-start.7
  84.0 6.7 %copy-start.4 = (f32[4,256,128]{2,1,0:T(8,128)}, f32[4,256,128]{2,1,0:T(8,128)S(1)}, u32[]{:S(2)}) copy-start(f32[4,256,128]{2,1,0:T(8,128)S(1)} %collective-permute-done.2.before_ref) | copy-start | bytes 1572868
  84.0 6.7 %copy-start.8 = (f32[512,3,128]{2,0,1:T(8,128)S(1)}, f32[512,3,128]{2,0,1:T(8,128)}, u32[]{:S(2)}) copy-start(f32[512,3,128]{2,0,1:T(8,128)} %param.7) | copy-start | bytes 2359300
  90.8 1.4 copy-start.2
  92.2 1.0 copy-start.1
  93.2 17.7 %all-to-all-start.2 = ((f32[4,512,128]{2,1,0:T(8,128)}), f32[4,512,128]{2,1,0:T(8,128)S(1)}, u32[]{:S(2)}, u32[]{:S(2)}) async-start(f32[4,512,128]{2,1,0:T(8,128)} %copy-done.1), calls=%async_computation.2 | async-start | bytes 2097152 | tf_op jit(solution)/shard_map/all_to_all | solution.py:297
  96.7 1.1 copy-start.3
  97.8 1.0 copy-start.5
  100.7 9.3 %collective-permute-start.3 = (f32[16,64,128]{2,1,0:T(8,128)S(1)}, f32[16,64,128]{2,1,0:T(8,128)S(1)}, u32[]{:S(2)}, u32[]{:S(2)}) collective-permute-start(f32[16,64,128]{2,1,0:T(8,128)S(1)} %get-tuple-element.40), channel_id=1, source_target_pairs={{0,4},{4,0},{1,5},{5,1},{2,6},{6,2},{3,7},{7,3},{8,12},{12,8},{9,1... | collective-permute-start | bytes 1572872 | tf_op jit(solution)/shard_map/ppermute | solution.py:350
  110.9 20.5 %all-to-all-start.3 = ((f32[16,64,128]{2,1,0:T(8,128)}), f32[16,64,128]{2,1,0:T(8,128)S(1)}, u32[]{:S(2)}, u32[]{:S(2)}) async-start(f32[16,64,128]{2,1,0:T(8,128)} %add.5), calls=%async_computation.3 | async-start | bytes 1048576 | tf_op jit(solution)/shard_map/all_to_all | solution.py:297
  119.8 30.7 %reduce-scatter.2.cloned.1.call-start = ((), (), s32[]{:S(2)}) async-start(), calls=%async_computation.7 | async-start | bytes 1310720 | tf_op jit(solution)/shard_map/reduce_scatter | solution.py:337
  120.5 10.5 %collective-permute-start.4 = (f32[256,128]{1,0:T(8,128)S(1)}, f32[256,128]{1,0:T(8,128)S(1)}, u32[]{:S(2)}, u32[]{:S(2)}) collective-permute-start(f32[256,128]{1,0:T(8,128)S(1)} %get-tuple-element.42), channel_id=1, source_target_pairs={{4,0},{8,4},{12,8},{16,12},{20,16},{24,20},{28,24},{32,28},{36,32}... | collective-permute-start | bytes 393224 | tf_op jit(solution)/shard_map/ppermute | solution.py:355
  132.8 42.2 %all-to-all-start.4 = ((f32[768,1,128]{2,1,0:T(1,128)}), f32[768,1,128]{2,1,0:T(1,128)S(1)}, u32[]{:S(2)}, u32[]{:S(2)}) async-start(f32[768,1,128]{2,1,0:T(1,128)} %bitcast.10), calls=%async_computation.4 | async-start | bytes 786432 | tf_op jit(solution)/shard_map/all_to_all | solution.py:297
  151.5 8.5 %collective-permute-start.5 = (f32[256,128]{1,0:T(8,128)S(1)}, f32[256,128]{1,0:T(8,128)S(1)}, u32[]{:S(2)}, u32[]{:S(2)}) collective-permute-start(f32[256,128]{1,0:T(8,128)S(1)} %get-tuple-element.53), channel_id=1, source_target_pairs={{4,0},{8,4},{12,8},{16,12},{20,16},{24,20},{28,24},{32,28},{36,32}... | collective-permute-start | bytes 393224 | tf_op jit(solution)/shard_map/ppermute | solution.py:338
  175.9 19.8 %all-to-all-start.5 = ((f32[16,64,128]{2,1,0:T(8,128)}), f32[16,64,128]{2,1,0:T(8,128)S(1)}, u32[]{:S(2)}, u32[]{:S(2)}) async-start(f32[16,64,128]{2,1,0:T(8,128)} %broadcast_in_dim.5), calls=%async_computation.6 | async-start | bytes 1048576 | tf_op jit(solution)/shard_map/all_to_all | solution.py:297
  195.7 6.1 %collective-permute-start.6 = (f32[16,64,128]{2,1,0:T(8,128)S(1)}, f32[16,64,128]{2,1,0:T(8,128)S(1)}, u32[]{:S(2)}, u32[]{:S(2)}) collective-permute-start(f32[16,64,128]{2,1,0:T(8,128)S(1)} %all-to-all-done.5.mine_ref), channel_id=1, source_target_pairs={{0,4},{4,0},{1,5},{5,1},{2,6},{6,2},{3,7},{7,3},{8,12},{12,8},{9,1... | collective-permute-start | bytes 1572872 | tf_op jit(solution)/shard_map/ppermute | solution.py:365
Sparse Core Ops, SparseCore 0:
  10.1 36.0 all-gather.2
  123.4 27.0 reduce-scatter.1

commit v5 on v4

--- a/solution.py
+++ b/solution.py
@@ -47,7 +47,8 @@
 
 def mm3(a, b, dims=NN):
     (ah, al), (bh, bl) = a, b
-    return mm(ah, bh, dims) + (mm(ah, bl, dims) + mm(al, bh, dims))
+    (left,), (right,) = dims[0]
+    return mm(jnp.concatenate([ah, al, ah], axis=left), jnp.concatenate([bh, bh, bl], axis=right), dims)
 
 
 def select_rows(pick, x):
@@ -127,7 +128,7 @@
         message_ref[pl.ds(each + turn, peers, stride=size), :] = rows
 
 
-def unpack_kernel(each, message_ref, sums_ref):
+def unpack_kernel(each, message_ref, out_hbm, sums_ref, sems):
     near = SIDE // ADDED
     for turn in range(ADDED):
         rows = every(message_ref, each + turn, each + ADDED)
@@ -135,6 +136,11 @@
         for far in range(1, rows.shape[0] // near):
             total += rows[far * near : (far + 1) * near]
         sums_ref[turn * near : (turn + 1) * near] = total
+    copies = [pltpu.make_async_copy(sums_ref, out_hbm.at[i], sems.at[i]) for i in range(BLOCKS)]
+    for copy in copies:
+        copy.start()
+    for copy in copies:
+        copy.wait()
 
 
 def unsort_kernel(each, index_ref, message_ref, out_ref):
@@ -165,28 +171,39 @@
     return (lanes // HEAD) == head
 
 
-def scores_of(queries, key_rows, mask):
-    qh, ql = split(queries)
-    kh, kl = split(jnp.where(mask, key_rows, 0.0))
-    keys = jnp.concatenate([kh, kl], axis=1)
-    return mm(keys, jnp.concatenate([qh, qh], axis=1), NT) + mm(
-        keys, jnp.concatenate([ql, ql], axis=1), NT
-    )
-
-
-def forward_kernel(x_ref, win_ref, wout_ref, bias_ref, qkv_ref, att_ref, lse_ref, out_ref, vt_ref):
-    parts = [split(x_ref[part]) for part in range(D // WIDTH)]
+def turned(x, order):
+    high, low = split(x)
+    parts = {"h": high.astype(F32), "l": low.astype(F32)}
+    return [parts[o] if not i else pltpu.roll(parts[o], i * HEAD, 1) for i, o in enumerate(order)]
+
+
+def of_head(refs, head):
+    lanes = lax.broadcasted_iota(jnp.int32, (PATCH, WIDTH), 1)
+    turn = (lanes // HEAD - head) & (HERE - 1)
+    x = refs[0]
+    for i in range(1, HERE):
+        x = jnp.where(turn == i, refs[i], x)
+    return x.astype(BF)
+
+
+def keep(ref, parts):
+    for i, part in enumerate(parts):
+        ref[i] = part
+
+
+def forward_kernel(x_ref, win_ref, bias_ref, qkv_ref, att_ref, lse_ref, vt_ref, q_ref, k_ref):
+    x = jnp.concatenate([x_ref[part] for part in range(D // WIDTH)], axis=1)
+    win = jnp.concatenate([win_ref[t] for t in range(3)], axis=1)
+    qkv = mm3(split(x), split(win))
     for t in range(3):
-        total = jnp.zeros((PATCH, WIDTH), F32)
-        for part in range(D // WIDTH):
-            total += mm3(parts[part], split(win_ref[t, part * WIDTH : (part + 1) * WIDTH]))
-        qkv_ref[t] = total
+        qkv_ref[t] = qkv[:, t * WIDTH : (t + 1) * WIDTH]
     vt_ref[...] = jnp.transpose(qkv_ref[2])
+    keep(q_ref, turned(qkv_ref[0] * (SCALE * LOG2E), "hhll"))
+    keep(k_ref, turned(qkv_ref[1], "hlhl"))
     bias = wide(bias_ref[...])
 
     def one(head, carry):
-        mask = head_mask(head)
-        scores = scores_of(qkv_ref[0] * (SCALE * LOG2E), qkv_ref[1], mask) + bias
+        scores = mm(of_head(k_ref, head), of_head(q_ref, head), NT) + bias
         top = jnp.max(scores, axis=0, keepdims=True)
         weights = jnp.exp2(scores - top)
         total = jnp.sum(weights, axis=0, keepdims=True)
@@ -199,23 +216,30 @@
         lse_ref[pl.ds(head, 1), :] = top + jnp.log2(total)
         return carry
 
-    lax.fori_loop(0, HERE, one, 0)
-    attended = split(jnp.transpose(att_ref[...]))
+    lax.fori_loop(0, HERE, one, 0, unroll=True)
+
+
+def output_kernel(att_ref, wout_ref, after_ref, out_ref):
+    del after_ref
+    out = mm3(split(jnp.transpose(att_ref[...])), split(wout_ref[...]))
     for part in range(D // WIDTH):
-        out_ref[part] = mm3(attended, split(wout_ref[:, part * WIDTH : (part + 1) * WIDTH]))
+        out_ref[part] = out[:, part * WIDTH : (part + 1) * WIDTH]
 
 
 def backward_kernel(
-    qkv_ref, att_ref, lse_ref, before_ref, cot_ref, wout_ref, bias_ref, dqkv_ref, kt_ref, gt_ref, dqt_ref, grad_ref
+    qkv_ref, att_ref, lse_ref, before_ref, cot_ref, wout_ref, bias_ref,
+    dqkv_ref, kt_ref, gt_ref, dqt_ref, grad_ref, q_ref, k_ref, v_ref, g_ref,
 ):
-    for rows, ref, first in ((slice(0, HALF), before_ref, 0), (slice(HALF, PATCH), cot_ref, 0)):
-        total = jnp.zeros((HALF, WIDTH), F32)
-        for part in range(D // WIDTH):
-            lanes = slice(part * WIDTH, (part + 1) * WIDTH)
-            total += mm3(split(ref[part, first : first + HALF]), split(wout_ref[:, lanes]), NT)
-        grad_ref[rows] = total
+    wout = split(wout_ref[...])
+    for rows, ref in ((slice(0, HALF), before_ref), (slice(HALF, PATCH), cot_ref)):
+        cot = jnp.concatenate([ref[part, :HALF] for part in range(D // WIDTH)], axis=1)
+        grad_ref[rows] = mm3(split(cot), wout, NT)
     kt_ref[...] = jnp.transpose(qkv_ref[1])
     gt_ref[...] = jnp.transpose(grad_ref[...])
+    keep(q_ref, turned(qkv_ref[0] * (SCALE * LOG2E), "hhll"))
+    keep(k_ref, turned(qkv_ref[1], "hlhl"))
+    keep(g_ref, turned(grad_ref[...], "hhll"))
+    keep(v_ref, turned(qkv_ref[2], "hlhl"))
     bias = wide(bias_ref[...])
     dqkv_ref[1] = jnp.zeros((PATCH, WIDTH), F32)
     dqkv_ref[2] = jnp.zeros((PATCH, WIDTH), F32)
@@ -223,10 +247,10 @@
     def one(head, carry):
         mask = head_mask(head)
         rows = pl.ds(pl.multiple_of(head * HEAD, HEAD), HEAD)
-        scores = scores_of(qkv_ref[0] * (SCALE * LOG2E), qkv_ref[1], mask) + bias
+        scores = mm(of_head(k_ref, head), of_head(q_ref, head), NT) + bias
         probs = jnp.exp2(scores - lse_ref[pl.ds(head, 1), :])
         ph, plo = split(probs)
-        grad_probs = scores_of(grad_ref[...], qkv_ref[2], mask)
+        grad_probs = mm(of_head(v_ref, head), of_head(g_ref, head), NT)
         gh, gl = split(jnp.where(mask, grad_ref[...], 0.0))
         both = mm(ph, jnp.concatenate([gh, gl], axis=1))
         dqkv_ref[2] += both[:, :WIDTH] + both[:, WIDTH:] + mm(plo, gh)
@@ -241,7 +265,7 @@
         dqt_ref[rows, :] = both[:HEAD] + both[HEAD:] + mm(kh, sl)
         return carry
 
-    lax.fori_loop(0, HERE, one, 0)
+    lax.fori_loop(0, HERE, one, 0, unroll=True)
     dqkv_ref[0] = jnp.transpose(dqt_ref[...])
 
 
@@ -254,36 +278,38 @@
         keep_ref[block] = jnp.where(second, bottom, top)
         send_ref[block] = jnp.where(second, top, bottom)
 
-    attended = split(att_ref[...])
-    parts = [split(x_ref[part]) for part in range(D // WIDTH)]
+    x = split(jnp.concatenate([x_ref[part] for part in range(D // WIDTH)], axis=1))
     for t in range(3):
-        grads = split(jnp.transpose(dqkv_ref[t]))
+        grads = jnp.transpose(mm3(split(jnp.transpose(dqkv_ref[t])), x))
         for part in range(D // WIDTH):
-            put(t * (D // WIDTH) + part, jnp.transpose(mm3(grads, parts[part])))
+            put(t * (D // WIDTH) + part, grads[part * WIDTH : (part + 1) * WIDTH])
+    cot = [jnp.concatenate([ref[part, :HALF] for part in range(D // WIDTH)], axis=1) for ref in (before_ref, cot_ref)]
+    grads = mm3(split(att_ref[...]), split(jnp.concatenate(cot, axis=0)))
     for part in range(D // WIDTH):
-        cot = jnp.concatenate([before_ref[part], cot_ref[part, :HALF]], axis=0)
-        put(3 * (D // WIDTH) + part, mm3(attended, split(cot)))
+        put(3 * (D // WIDTH) + part, grads[:, part * WIDTH : (part + 1) * WIDTH])
 
 
 def rows_kernel(dqkv_ref, win_ref, dx_ref, done_ref):
     done_ref[...] = jnp.zeros_like(done_ref)
-    grads = [split(dqkv_ref[t]) for t in range(3)]
+    grads = split(jnp.concatenate([dqkv_ref[t] for t in range(3)], axis=1))
     for part in range(D // WIDTH):
-        total = jnp.zeros((PATCH, WIDTH), F32)
-        for t in range(3):
-            total += mm3(grads[t], split(win_ref[t, part * WIDTH : (part + 1) * WIDTH]), NT)
-        dx_ref[part] = total
-
-
-def call(kernel, outs, *args, scratch=(), scalars=0, room=8, flops=10**9):
+        rows = slice(part * WIDTH, (part + 1) * WIDTH)
+        win = jnp.concatenate([win_ref[t, rows] for t in range(3)], axis=1)
+        dx_ref[part] = mm3(grads, split(win), NT)
+
+
+def call(kernel, outs, *args, scratch=(), sems=(), scalars=0, sent=0, room=8, flops=10**9):
     size = sum(math.prod(a.shape) * 4 for a in (*args, *outs))
+    vmem = pl.BlockSpec(memory_space=pltpu.VMEM)
+    hbm = pl.BlockSpec(memory_space=pltpu.HBM)
     return pl.pallas_call(
         kernel,
         out_shape=tuple(jax.ShapeDtypeStruct(o, F32) for o in [x.shape for x in outs]),
         in_specs=[pl.BlockSpec(memory_space=pltpu.SMEM)] * scalars
-        + [pl.BlockSpec(memory_space=pltpu.VMEM)] * (len(args) - scalars),
-        out_specs=tuple(pl.BlockSpec(memory_space=pltpu.VMEM) for _ in outs),
-        scratch_shapes=[pltpu.VMEM(s, F32) for s in scratch],
+        + [vmem] * (len(args) - scalars),
+        out_specs=tuple([hbm] * sent + [vmem] * (len(outs) - sent)),
+        scratch_shapes=[pltpu.VMEM(x, F32) if isinstance(x, tuple) else x for x in scratch]
+        + [pltpu.SemaphoreType.DMA(n) for n in sems],
         compiler_params=pltpu.CompilerParams(vmem_limit_bytes=room * 2**20),
         cost_estimate=pl.CostEstimate(flops=flops, bytes_accessed=size, transcendentals=0),
     )(*args)
@@ -295,11 +321,6 @@
 
 def swap(x, axis):
     return lax.all_to_all(x, axis, split_axis=0, concat_axis=0, tiled=True)
-
-
-def spread_to(x, axis):
-    peers = lax.axis_size(axis)
-    return swap(jnp.broadcast_to(x[None], (peers,) + x.shape).reshape(-1, WIDTH), axis)
 
 
 def shards(features, input_proj, output_proj, destination, real_points, cotangent):
@@ -309,9 +330,6 @@
     down = [(j, i) for i, j in up]
     core = lax.axis_index("core").astype(jnp.int32).reshape(1)
 
-    def to_patch(low, high):
-        return jnp.concatenate([lax.ppermute(high, CURVE, up), low], axis=0)
-
     def exchange(message):
         rows = message.shape[0]
         return swap(message.reshape(rows, 1, WIDTH), CURVE).reshape(rows, WIDTH)
@@ -323,43 +341,52 @@
     )
     arrived = exchange(message)
     win = jnp.transpose(input_proj, (1, 0, 2))
-    valid = to_patch(real_points[:HALF], real_points[HALF:]).reshape(1, PATCH)
+    valid = jnp.concatenate([lax.ppermute(real_points[HALF:], CURVE, up), real_points[:HALF]], axis=0)
+    valid = valid.reshape(1, PATCH)
     low, high, position, bias = call(
         functools.partial(place_kernel, each),
         [of(HALF, WIDTH), of(HALF, WIDTH), of(1, PATCH), of(PATCH, WIDTH)], arrived, valid, cot[0, :8],
     )
-    x = spread_to(to_patch(low, high), "head").reshape(D // WIDTH, PATCH, WIDTH)
-    qkv, attended, lse, out = call(
+    x = jnp.concatenate([lax.ppermute(high, CURVE, up), low], axis=0)
+    x = jnp.broadcast_to(x[None], (D // WIDTH, PATCH, WIDTH))
+    x = swap(x.reshape(-1, WIDTH), "head").reshape(D // WIDTH, PATCH, WIDTH)
+    qkv, attended, lse = call(
         forward_kernel,
-        [of(3, PATCH, WIDTH), of(WIDTH, PATCH), of(HERE, PATCH), of(D // WIDTH, PATCH, WIDTH)],
-        x, win, output_proj, bias, scratch=[(WIDTH, PATCH)], room=16,
-    )
-    out = lax.psum_scatter(out, "head", scatter_dimension=0)
-    branch_out = jnp.concatenate([out[HALF:], lax.ppermute(out[:HALF], CURVE, down)], axis=0)
+        [of(3, PATCH, WIDTH), of(WIDTH, PATCH), of(HERE, PATCH)],
+        x, win, bias, scratch=[(WIDTH, PATCH)] + [(HERE, PATCH, WIDTH)] * 2, room=24,
+    )
     before = lax.ppermute(cot[:, HALF:], CURVE, up)
     (dqkv,) = call(
         backward_kernel, [of(3, PATCH, WIDTH)], qkv, attended, lse, before, cot, output_proj, bias,
-        scratch=[(WIDTH, PATCH)] * 3 + [(PATCH, WIDTH)], room=16,
-    )
-    dx, done = call(rows_kernel, [of(D // WIDTH, PATCH, WIDTH), of(8, WIDTH)], dqkv, win)
+        scratch=[(WIDTH, PATCH)] * 3 + [(PATCH, WIDTH)] + [(HERE, PATCH, WIDTH)] * 4, room=24,
+    )
+    dx, done = call(
+        rows_kernel, [of(D // WIDTH, PATCH, WIDTH), of(8, WIDTH)], dqkv, win
+    )
     dx = swap(dx.reshape(-1, WIDTH), "head").reshape(D // WIDTH, PATCH, WIDTH)
-    early, late = call(add_kernel, [of(HALF, WIDTH)] * 2, dx)
+    dx_early, dx_late = call(add_kernel, [of(HALF, WIDTH)] * 2, dx)
     keep, send = call(
         weights_kernel, [of(BLOCKS, SIDE, WIDTH)] * 2, core, x, dqkv, attended, before, cot, done, scalars=1
     )
+    (out,) = call(output_kernel, [of(D // WIDTH, PATCH, WIDTH)], attended, output_proj, done)
+    out = lax.psum_scatter(out, "head", scatter_dimension=0)
+    branch_out = jnp.concatenate([out[HALF:], lax.ppermute(out[:HALF], CURVE, down)], axis=0)
     sums = keep + lax.ppermute(send, "core", [(0, 1), (1, 0)])
-    sums, early = lax.optimization_barrier((sums, early))
+    sums, dx_early = lax.optimization_barrier((sums, dx_early))
     sums = swap(sums.reshape(-1, WIDTH), PLANE).reshape(BLOCKS, SIDE, WIDTH)
     (message,) = call(
         functools.partial(pack_kernel, each), [of(peers * (each + ADDED), WIDTH)],
-        position, late, lax.ppermute(early, CURVE, down), sums,
+        position, dx_late, lax.ppermute(dx_early, CURVE, down), sums,
     )
     message = exchange(message)
-    (sums,) = call(functools.partial(unpack_kernel, each), [of(SIDE, WIDTH)], message)
+    (sums,) = call(
+        functools.partial(unpack_kernel, each), [of(BLOCKS, SIDE, WIDTH)], message,
+        sent=1, scratch=[(SIDE, WIDTH)], sems=[(BLOCKS,)],
+    )
+    sums, branch_out = lax.optimization_barrier((sums, branch_out))
+    sums = swap(sums.reshape(-1, WIDTH), PLANE).reshape(BLOCKS, SIDE, WIDTH)
+    sums, message = lax.optimization_barrier((sums, message))
     (grad_features,) = call(functools.partial(unsort_kernel, each), [of(PATCH, WIDTH)], index, message)
-    sums, branch_out = lax.optimization_barrier((sums, branch_out))
-    sums = spread_to(sums, PLANE).reshape(BLOCKS, SIDE, WIDTH)
-    sums, grad_features = lax.optimization_barrier((sums, grad_features))
     grad_inproj, grad_outproj = call(
         finish_kernel, [of(3, D, WIDTH), of(WIDTH, D)],
         core, sums, lax.ppermute(sums, "core", [(0, 1), (1, 0)]), scalars=1,

time: 211 us -> 207 us (0.981)
  blocking collectives: 0 us -> 19.6 us
  waiting for transfers between devices: 67.7 us -> 52.6 us
  starting transfers between devices: 93.9 us -> 87.6 us
  Pallas kernels: 23.1 us -> 20.5 us
    all_to_all x0 -> x1, blocking collectives: none -> 19.6 us  [swap(): return lax.all_to_all(x, axis, split_axis=0, concat_axis=0, tiled=True)]
    all_to_all x6 -> x5, waiting for transfers between devices: 38.9 us -> 26 us  [swap(): return lax.all_to_all(x, axis, split_axis=0, concat_axis=0, tiled=True)]
    all_to_all x6 -> x5, starting transfers between devices: 60 us -> 53.7 us  [swap(): return lax.all_to_all(x, axis, split_axis=0, concat_axis=0, tiled=True)]
    pallas_call x11 -> x12, Pallas kernels: 23.1 us -> 20.5 us  [call(): pl.pallas_call(kernel, out_shape=tuple((jax.ShapeDtypeStruct(o, F32) for...]
    unnamed x24 -> x28, local copies, waits for them, and re-layouts: 5.18 us -> 6.16 us
  transfers between devices with their start and end apart: 15 -> 14, of which waited for: 13 -> 11; matrix products, arithmetic and copies ran while one was open for 2% -> 2% of each run, Pallas kernels for 6% -> 5%
where the time goes in v5:
time: 207 us; the launch traced here: 206 us
  starting transfers between devices  87.6 us (42%)
  waiting for transfers between devices  52.6 us (25%)
  Pallas kernels  20.5 us (10%)
  blocking collectives  19.6 us (9%)
  between operations  14.3 us (7%)
  local copies, waits for them, and re-layouts  9.7 us (5%)
    all_to_all x5, starting transfers between devices, swap(): return lax.all_to_all(x, axis, split_axis=0, concat_axis=0, tiled=True)  53.7 us
    all_to_all x5, waiting for transfers between devices, swap(): return lax.all_to_all(x, axis, split_axis=0, concat_axis=0, tiled=True)  26 us
    pallas_call x12, Pallas kernels, call(): pl.pallas_call(kernel, out_shape=tuple((jax.ShapeDtypeStruct(o, F32) for...  20.5 us
    all_to_all x1, blocking collectives, swap(): return lax.all_to_all(x, axis, split_axis=0, concat_axis=0, tiled=True)  19.6 us
    all_gather x1, waiting for transfers between devices, shards(): cot = lax.all_gather(cotangent, 'head', axis=0)  11 us
    ppermute x1, starting transfers between devices, shards(): sums = keep + lax.ppermute(send, 'core', [(0, 1), (1, 0)])  7.76 us
    unnamed x28, local copies, waits for them, and re-layouts  6.16 us
    ppermute x1, starting transfers between devices, shards(): lax.ppermute(dx_early, CURVE, down)  5.07 us
  transfers between devices with their start and end apart: 14, of which 11 were waited for; matrix products, arithmetic and copies ran while one was open for 2% of the time, Pallas kernels for 5%

profile of v5, /device:TPU:1, one launch (start us, length us, event | category | flops | bytes accessed | tf_op | source)
XLA Modules:
  0.0 205.9 jit_solution(7695102574259938418)
XLA Ops:
  8.8 1.6 shard_map.93
  10.4 20.5 %all-to-all-start = ((f32[640,1,128]{2,1,0:T(1,128)}), f32[640,1,128]{2,1,0:T(1,128)S(1)}, u32[]{:S(2)}, u32[]{:S(2)}) async-start(f32[640,1,128]{2,1,0:T(1,128)} %bitcast.2), calls=%async_computation | async-start | bytes 655360 | tf_op jit(solution)/shard_map/all_to_all | solution.py:323
  30.9 3.5 %collective-permute-start = (s32[256]{0:T(256)S(1)}, s32[256]{0:T(256)S(1)}, u32[]{:S(2)}, u32[]{:S(2)}) collective-permute-start(s32[256]{0:T(256)S(1)} %get-tuple-element.52), channel_id=1, source_target_pairs={{0,4},{4,8},{8,12},{12,16},{16,20},{20,24},{24,28},{28,32},{32,36}... | collective-permute-start | bytes 3080 | tf_op jit(solution)/shard_map/ppermute | solution.py:344
  35.2 11.0 %all-gather.3.cloned.1.call-done = f32[2048,128]{1,0:T(8,128)} async-done(((f32[512,128]{1,0:T(8,128)}), f32[2048,128]{1,0:T(8,128)}) %all-gather.3.cloned.1.call-update) | async-done | bytes 1048592 | tf_op jit(solution)/shard_map/all_gather | solution.py:337
  46.9 7.0 %all-to-all-done = f32[640,1,128]{2,1,0:T(1,128)S(1)} async-done(((f32[640,1,128]{2,1,0:T(1,128)}), f32[640,1,128]{2,1,0:T(1,128)S(1)}, u32[]{:S(2)}, u32[]{:S(2)}) %all-to-all-start) | async-done | bytes 327712 | tf_op jit(solution)/shard_map/all_to_all | solution.py:323
  54.5 4.2 %collective-permute-start.1 = (f32[256,128]{1,0:T(8,128)S(1)}, f32[256,128]{1,0:T(8,128)S(1)}, u32[]{:S(2)}, u32[]{:S(2)}) collective-permute-start(f32[256,128]{1,0:T(8,128)S(1)} %get-tuple-element.29), channel_id=1, source_target_pairs={{0,4},{4,8},{8,12},{12,16},{16,20},{20,24},{24,28},{28,32},{32,36}... | collective-permute-start | bytes 393224 | tf_op jit(solution)/shard_map/ppermute | solution.py:350
  58.7 1.9 collective-permute-done.1
  61.7 4.3 %all-to-all-start.1 = ((f32[4,512,128]{2,1,0:T(8,128)}), f32[4,512,128]{2,1,0:T(8,128)S(1)}, u32[]{:S(2)}, u32[]{:S(2)}) async-start(f32[4,512,128]{2,1,0:T(8,128)} %broadcast_in_dim.2), calls=%async_computation.1 | async-start | bytes 2097152 | tf_op jit(solution)/shard_map/all_to_all | solution.py:323
  66.9 4.8 %collective-permute-start.2 = (f32[4,256,128]{2,1,0:T(8,128)}, f32[4,256,128]{2,1,0:T(8,128)S(1)}, u32[]{:S(2)}, u32[]{:S(2)}) collective-permute-start(f32[4,256,128]{2,1,0:T(8,128)} %slice.33), channel_id=1, source_target_pairs={{0,4},{4,8},{8,12},{12,16},{16,20},{20,24},{24,28},{28,32},{32,36}... | collective-permute-start | bytes 1572872 | tf_op jit(solution)/shard_map/ppermute | solution.py:358
  71.7 4.6 %all-to-all-done.1.x_ref = f32[4,512,128]{2,1,0:T(8,128)S(1)} async-done(((f32[4,512,128]{2,1,0:T(8,128)}), f32[4,512,128]{2,1,0:T(8,128)S(1)}, u32[]{:S(2)}, u32[]{:S(2)}) %all-to-all-start.1) | async-done | bytes 1048608 | tf_op jit(solution)/shard_map/all_to_all | solution.py:323
  76.2 1.1 copy-done.10
  77.4 3.7 %shard_map.95 = (f32[3,512,128]{2,1,0:T(8,128)S(1)}, f32[128,512]{1,0:T(8,128)S(1)}, f32[4,512]{1,0:T(4,128)S(1)}) custom-call(f32[4,512,128]{2,1,0:T(8,128)S(1)} %all-to-all-done.1.x_ref, f32[3,512,128]{2,1,0:T(8,128)S(1)} %bitcast.28, f32[512,128]{1,0:T(8,128)S(1)} %get-tuple-element.31.bias_ref), custom_call_target="tpu_custom_call" | custom-call | flops 1000000000 | bytes 3153920 | tf_op jit(solution)/shard_map/pallas_call | solution.py:305
  81.1 5.3 %shard_map.96.dqkv_ref = f32[3,512,128]{2,1,0:T(8,128)S(1)} custom-call(f32[3,512,128]{2,1,0:T(8,128)S(1)} %get-tuple-element.32.qkv_ref, f32[128,512]{1,0:T(8,128)S(1)} %get-tuple-element.33.att_ref, f32[4,512]{1,0:T(4,128)S(1)} %get-tuple-element.34.lse_ref, f32[4,256,128]{2,1,0:T(8,128)S(1)} %collective-permute-done.2.before_ref, ...), custom_call_target="tpu_custom_call" | custom-call | flops 1000000000 | bytes 3940352 | tf_op jit(solution)/shard_map/pallas_call | solution.py:305
  86.5 1.4 shard_map.97
  88.9 3.5 %all-to-all-start.2 = ((f32[4,512,128]{2,1,0:T(8,128)}), f32[4,512,128]{2,1,0:T(8,128)S(1)}, u32[]{:S(2)}, u32[]{:S(2)}) async-start(f32[4,512,128]{2,1,0:T(8,128)} %copy-done.1), calls=%async_computation.2 | async-start | bytes 2097152 | tf_op jit(solution)/shard_map/all_to_all | solution.py:323
  92.4 1.1 copy-done.3
  95.6 1.2 shard_map.99
  96.7 7.8 %collective-permute-start.3 = (f32[16,64,128]{2,1,0:T(8,128)S(1)}, f32[16,64,128]{2,1,0:T(8,128)S(1)}, u32[]{:S(2)}, u32[]{:S(2)}) collective-permute-start(f32[16,64,128]{2,1,0:T(8,128)S(1)} %get-tuple-element.39), channel_id=1, source_target_pairs={{0,4},{4,0},{1,5},{5,1},{2,6},{6,2},{3,7},{7,3},{8,12},{12,8},{9,1... | collective-permute-start | bytes 1572872 | tf_op jit(solution)/shard_map/ppermute | solution.py:374
  104.5 1.5 collective-permute-done.3
  107.0 8.7 %all-to-all-start.3 = ((f32[16,64,128]{2,1,0:T(8,128)}), f32[16,64,128]{2,1,0:T(8,128)S(1)}, u32[]{:S(2)}, u32[]{:S(2)}) async-start(f32[16,64,128]{2,1,0:T(8,128)} %add.5), calls=%async_computation.3 | async-start | bytes 1048576 | tf_op jit(solution)/shard_map/all_to_all | solution.py:323
  115.7 1.5 shard_map.102
  117.2 5.1 %collective-permute-start.4 = (f32[256,128]{1,0:T(8,128)S(1)}, f32[256,128]{1,0:T(8,128)S(1)}, u32[]{:S(2)}, u32[]{:S(2)}) collective-permute-start(f32[256,128]{1,0:T(8,128)S(1)} %get-tuple-element.41), channel_id=1, source_target_pairs={{4,0},{8,4},{12,8},{16,12},{20,16},{24,20},{28,24},{32,28},{36,32}... | collective-permute-start | bytes 393224 | tf_op jit(solution)/shard_map/ppermute | solution.py:379
  122.3 5.1 %collective-permute-done.4.high_ref = f32[256,128]{1,0:T(8,128)S(1)} collective-permute-done((f32[256,128]{1,0:T(8,128)S(1)}, f32[256,128]{1,0:T(8,128)S(1)}, u32[]{:S(2)}, u32[]{:S(2)}) %collective-permute-start.4) | collective-permute-done | bytes 131104 | tf_op jit(solution)/shard_map/ppermute | solution.py:379
  127.4 1.4 shard_map.100
  128.7 16.7 %all-to-all-start.4 = ((f32[768,1,128]{2,1,0:T(1,128)}), f32[768,1,128]{2,1,0:T(1,128)S(1)}, u32[]{:S(2)}, u32[]{:S(2)}) async-start(f32[768,1,128]{2,1,0:T(1,128)} %bitcast.10), calls=%async_computation.4 | async-start | bytes 786432 | tf_op jit(solution)/shard_map/all_to_all | solution.py:323
  147.5 3.8 %collective-permute-start.5 = (f32[256,128]{1,0:T(8,128)S(1)}, f32[256,128]{1,0:T(8,128)S(1)}, u32[]{:S(2)}, u32[]{:S(2)}) collective-permute-start(f32[256,128]{1,0:T(8,128)S(1)} %get-tuple-element.51), channel_id=1, source_target_pairs={{4,0},{8,4},{12,8},{16,12},{20,16},{24,20},{28,24},{32,28},{36,32}... | collective-permute-start | bytes 393224 | tf_op jit(solution)/shard_map/ppermute | solution.py:373
  151.4 4.4 %collective-permute-done.5 = f32[256,128]{1,0:T(8,128)S(1)} collective-permute-done((f32[256,128]{1,0:T(8,128)S(1)}, f32[256,128]{1,0:T(8,128)S(1)}, u32[]{:S(2)}, u32[]{:S(2)}) %collective-permute-start.5) | collective-permute-done | bytes 131104 | tf_op jit(solution)/shard_map/ppermute | solution.py:373
  156.6 14.4 %all-to-all-done.4 = f32[768,1,128]{2,1,0:T(1,128)S(1)} async-done(((f32[768,1,128]{2,1,0:T(1,128)}), f32[768,1,128]{2,1,0:T(1,128)S(1)}, u32[]{:S(2)}, u32[]{:S(2)}) %all-to-all-start.4) | async-done | bytes 393248 | tf_op jit(solution)/shard_map/all_to_all | solution.py:323
  171.8 19.6 %all_to_all.34.mine_ref = f32[16,64,128]{2,1,0:T(8,128)S(1)} all-to-all(f32[16,64,128]{2,1,0:T(8,128)S(1)} %shard_map.101), channel_id=1, replica_groups=mesh['far'=4,'near'=4,'x'=4,'core'=2,'head'=4] {'near','x'}, dimensions={0} | all-to-all | bytes 1048576 | tf_op jit(solution)/shard_map/all_to_all | solution.py:323
  191.4 4.6 %collective-permute-start.6 = (f32[16,64,128]{2,1,0:T(8,128)S(1)}, f32[16,64,128]{2,1,0:T(8,128)S(1)}, u32[]{:S(2)}, u32[]{:S(2)}) collective-permute-start(f32[16,64,128]{2,1,0:T(8,128)S(1)} %all_to_all.34.mine_ref), channel_id=1, source_target_pairs={{0,4},{4,0},{1,5},{5,1},{2,6},{6,2},{3,7},{7,3},{8,12},{12,8},{9,1... | collective-permute-start | bytes 1572872 | tf_op jit(solution)/shard_map/ppermute | solution.py:392
  196.0 1.3 shard_map.103
  197.5 1.6 shard_map.104
  (48 shorter events, 13.3 us)
Async XLA Ops:
  7.2 1.0 copy-start.11
  7.2 39.0 %all-gather.3.cloned.1.call-start = ((), (), s32[]{:S(2)}) async-start(), calls=%async_computation.8 | async-start | bytes 1310720 | tf_op jit(solution)/shard_map/all_gather | solution.py:337
  8.1 0.7 copy-start.12
  10.4 20.5 %copy-start.13 = (s32[512]{0:T(512)S(1)}, s32[512]{0:T(512)}, u32[]{:S(2)}) copy-start(s32[512]{0:T(512)} %param.10) | copy-start | bytes 6148
  10.4 43.5 %all-to-all-start = ((f32[640,1,128]{2,1,0:T(1,128)}), f32[640,1,128]{2,1,0:T(1,128)S(1)}, u32[]{:S(2)}, u32[]{:S(2)}) async-start(f32[640,1,128]{2,1,0:T(1,128)} %bitcast.2), calls=%async_computation | async-start | bytes 655360 | tf_op jit(solution)/shard_map/all_to_all | solution.py:323
  30.9 4.3 %collective-permute-start = (s32[256]{0:T(256)S(1)}, s32[256]{0:T(256)S(1)}, u32[]{:S(2)}, u32[]{:S(2)}) collective-permute-start(s32[256]{0:T(256)S(1)} %get-tuple-element.52), channel_id=1, source_target_pairs={{0,4},{4,8},{8,12},{12,16},{16,20},{20,24},{24,28},{28,32},{32,36}... | collective-permute-start | bytes 3080 | tf_op jit(solution)/shard_map/ppermute | solution.py:344
  54.5 6.1 %collective-permute-start.1 = (f32[256,128]{1,0:T(8,128)S(1)}, f32[256,128]{1,0:T(8,128)S(1)}, u32[]{:S(2)}, u32[]{:S(2)}) collective-permute-start(f32[256,128]{1,0:T(8,128)S(1)} %get-tuple-element.29), channel_id=1, source_target_pairs={{0,4},{4,8},{8,12},{12,16},{16,20},{20,24},{24,28},{28,32},{32,36}... | collective-permute-start | bytes 393224 | tf_op jit(solution)/shard_map/ppermute | solution.py:350
  61.7 4.3 %copy-start = (f32[2048,128]{1,0:T(8,128)S(1)}, f32[2048,128]{1,0:T(8,128)}, u32[]{:S(2)}) copy-start(f32[2048,128]{1,0:T(8,128)} %all-gather.3.cloned.1.call-done) | copy-start | bytes 3145732
  61.7 14.5 %all-to-all-start.1 = ((f32[4,512,128]{2,1,0:T(8,128)}), f32[4,512,128]{2,1,0:T(8,128)S(1)}, u32[]{:S(2)}, u32[]{:S(2)}) async-start(f32[4,512,128]{2,1,0:T(8,128)} %broadcast_in_dim.2), calls=%async_computation.1 | async-start | bytes 2097152 | tf_op jit(solution)/shard_map/all_to_all | solution.py:323
  66.9 14.3 %collective-permute-start.2 = (f32[4,256,128]{2,1,0:T(8,128)}, f32[4,256,128]{2,1,0:T(8,128)S(1)}, u32[]{:S(2)}, u32[]{:S(2)}) collective-permute-start(f32[4,256,128]{2,1,0:T(8,128)} %slice.33), channel_id=1, source_target_pairs={{0,4},{4,8},{8,12},{12,16},{16,20},{20,24},{24,28},{28,32},{32,36}... | collective-permute-start | bytes 1572872 | tf_op jit(solution)/shard_map/ppermute | solution.py:358
  76.2 1.1 copy-start.10
  77.4 3.8 %copy-start.6 = (f32[128,512]{1,0:T(8,128)S(1)}, f32[128,512]{1,0:T(8,128)}, u32[]{:S(2)}) copy-start(f32[128,512]{1,0:T(8,128)} %wout_ref.3) | copy-start | bytes 786436
  81.1 5.4 %copy-start.7 = (f32[128,512]{1,0:T(8,128)}, f32[128,512]{1,0:T(8,128)S(1)}, u32[]{:S(2)}) copy-start(f32[128,512]{1,0:T(8,128)S(1)} %get-tuple-element.33.att_ref) | copy-start | bytes 786436
  81.1 5.4 %copy-start.4 = (f32[4,256,128]{2,1,0:T(8,128)}, f32[4,256,128]{2,1,0:T(8,128)S(1)}, u32[]{:S(2)}) copy-start(f32[4,256,128]{2,1,0:T(8,128)S(1)} %collective-permute-done.2.before_ref) | copy-start | bytes 1572868
  86.5 1.4 copy-start.2
  87.9 1.0 copy-start.1
  88.9 18.0 %all-to-all-start.2 = ((f32[4,512,128]{2,1,0:T(8,128)}), f32[4,512,128]{2,1,0:T(8,128)S(1)}, u32[]{:S(2)}, u32[]{:S(2)}) async-start(f32[4,512,128]{2,1,0:T(8,128)} %copy-done.1), calls=%async_computation.2 | async-start | bytes 2097152 | tf_op jit(solution)/shard_map/all_to_all | solution.py:323
  92.4 1.1 copy-start.3
  93.6 1.0 copy-start.5
  94.6 0.9 copy-start.8
  96.7 9.3 %collective-permute-start.3 = (f32[16,64,128]{2,1,0:T(8,128)S(1)}, f32[16,64,128]{2,1,0:T(8,128)S(1)}, u32[]{:S(2)}, u32[]{:S(2)}) collective-permute-start(f32[16,64,128]{2,1,0:T(8,128)S(1)} %get-tuple-element.39), channel_id=1, source_target_pairs={{0,4},{4,0},{1,5},{5,1},{2,6},{6,2},{3,7},{7,3},{8,12},{12,8},{9,1... | collective-permute-start | bytes 1572872 | tf_op jit(solution)/shard_map/ppermute | solution.py:374
  106.9 8.8 %copy-start.9 = (f32[128,512]{1,0:T(8,128)S(1)}, f32[128,512]{1,0:T(8,128)}, u32[]{:S(2)}) copy-start(f32[128,512]{1,0:T(8,128)} %copy-done.7) | copy-start | bytes 786436
  107.0 20.4 %all-to-all-start.3 = ((f32[16,64,128]{2,1,0:T(8,128)}), f32[16,64,128]{2,1,0:T(8,128)S(1)}, u32[]{:S(2)}, u32[]{:S(2)}) async-start(f32[16,64,128]{2,1,0:T(8,128)} %add.5), calls=%async_computation.3 | async-start | bytes 1048576 | tf_op jit(solution)/shard_map/all_to_all | solution.py:323
  115.7 30.9 %reduce-scatter.2.cloned.1.call-start = ((), (), s32[]{:S(2)}) async-start(), calls=%async_computation.7 | async-start | bytes 1310720 | tf_op jit(solution)/shard_map/reduce_scatter | solution.py:372
  117.2 10.1 %collective-permute-start.4 = (f32[256,128]{1,0:T(8,128)S(1)}, f32[256,128]{1,0:T(8,128)S(1)}, u32[]{:S(2)}, u32[]{:S(2)}) collective-permute-start(f32[256,128]{1,0:T(8,128)S(1)} %get-tuple-element.41), channel_id=1, source_target_pairs={{4,0},{8,4},{12,8},{16,12},{20,16},{24,20},{28,24},{32,28},{36,32}... | collective-permute-start | bytes 393224 | tf_op jit(solution)/shard_map/ppermute | solution.py:379
  128.7 42.2 %all-to-all-start.4 = ((f32[768,1,128]{2,1,0:T(1,128)}), f32[768,1,128]{2,1,0:T(1,128)S(1)}, u32[]{:S(2)}, u32[]{:S(2)}) async-start(f32[768,1,128]{2,1,0:T(1,128)} %bitcast.10), calls=%async_computation.4 | async-start | bytes 786432 | tf_op jit(solution)/shard_map/all_to_all | solution.py:323
  147.5 8.3 %collective-permute-start.5 = (f32[256,128]{1,0:T(8,128)S(1)}, f32[256,128]{1,0:T(8,128)S(1)}, u32[]{:S(2)}, u32[]{:S(2)}) collective-permute-start(f32[256,128]{1,0:T(8,128)S(1)} %get-tuple-element.51), channel_id=1, source_target_pairs={{4,0},{8,4},{12,8},{16,12},{20,16},{24,20},{28,24},{32,28},{36,32}... | collective-permute-start | bytes 393224 | tf_op jit(solution)/shard_map/ppermute | solution.py:373
  191.4 6.1 %collective-permute-start.6 = (f32[16,64,128]{2,1,0:T(8,128)S(1)}, f32[16,64,128]{2,1,0:T(8,128)S(1)}, u32[]{:S(2)}, u32[]{:S(2)}) collective-permute-start(f32[16,64,128]{2,1,0:T(8,128)S(1)} %all_to_all.34.mine_ref), channel_id=1, source_target_pairs={{0,4},{4,0},{1,5},{5,1},{2,6},{6,2},{3,7},{7,3},{8,12},{12,8},{9,1... | collective-permute-start | bytes 1572872 | tf_op jit(solution)/shard_map/ppermute | solution.py:392
Sparse Core Ops, SparseCore 0:
  10.1 36.0 all-gather.2
  119.3 27.1 reduce-scatter.1

commit v6 on v5

--- a/solution.py
+++ b/solution.py
@@ -94,8 +94,8 @@
     message_ref[pl.ds(each, peers, stride=each + 1), :] = mm(mine, high) + mm(mine, low)
 
 
-def place_kernel(each, message_ref, valid_ref, after_ref, low_ref, high_ref, position_ref, bias_ref):
-    del after_ref
+def place_kernel(each, after1_ref, after2_ref, after3_ref, message_ref, valid_ref, low_ref, high_ref, position_ref, bias_ref):
+    del after1_ref, after2_ref, after3_ref
     turned = jnp.transpose(every(message_ref, each, each + 1))
     position = jnp.concatenate([turned[turn : turn + 1] for turn in range(each)], axis=1)
     position_ref[...] = position
@@ -219,21 +219,32 @@
     lax.fori_loop(0, HERE, one, 0, unroll=True)
 
 
-def output_kernel(att_ref, wout_ref, after_ref, out_ref):
+def along(step):
+    part = lax.rem(step, D // WIDTH)
+    return part, pl.ds(pl.multiple_of(part * WIDTH, WIDTH), WIDTH)
+
+
+def output_kernel(head_ref, att_ref, wout_ref, after_ref, *out_refs):
     del after_ref
-    out = mm3(split(jnp.transpose(att_ref[...])), split(wout_ref[...]))
-    for part in range(D // WIDTH):
-        out_ref[part] = out[:, part * WIDTH : (part + 1) * WIDTH]
+    attended = split(jnp.transpose(att_ref[...]))
+    for step, out_ref in enumerate(out_refs):
+        out_ref[...] = mm3(attended, split(wout_ref[:, along(head_ref[0] + step)[1]]))
+
+
+def sum_kernel(first_ref, second_ref, third_ref, fourth_ref, early_ref, late_ref):
+    total = first_ref[...] + second_ref[...] + (third_ref[...] + fourth_ref[...])
+    early_ref[...] = total[:HALF]
+    late_ref[...] = total[HALF:]
 
 
 def backward_kernel(
-    qkv_ref, att_ref, lse_ref, before_ref, cot_ref, wout_ref, bias_ref,
+    head_ref, qkv_ref, att_ref, lse_ref, before_ref, cot_ref, cot1_ref, cot2_ref, cot3_ref, wout_ref, bias_ref,
     dqkv_ref, kt_ref, gt_ref, dqt_ref, grad_ref, q_ref, k_ref, v_ref, g_ref,
 ):
-    wout = split(wout_ref[...])
-    for rows, ref in ((slice(0, HALF), before_ref), (slice(HALF, PATCH), cot_ref)):
-        cot = jnp.concatenate([ref[part, :HALF] for part in range(D // WIDTH)], axis=1)
-        grad_ref[rows] = mm3(split(cot), wout, NT)
+    cots = [cot_ref, cot1_ref, cot2_ref, cot3_ref]
+    cots = [jnp.concatenate([before_ref[s], ref[:HALF]], axis=0) for s, ref in enumerate(cots)]
+    wout = [wout_ref[:, along(head_ref[0] + (D // WIDTH - s))[1]] for s in range(D // WIDTH)]
+    grad_ref[...] = mm3(split(jnp.concatenate(cots, axis=1)), split(jnp.concatenate(wout, axis=1)), NT)
     kt_ref[...] = jnp.transpose(qkv_ref[1])
     gt_ref[...] = jnp.transpose(grad_ref[...])
     keep(q_ref, turned(qkv_ref[0] * (SCALE * LOG2E), "hhll"))
@@ -269,7 +280,9 @@
     dqkv_ref[0] = jnp.transpose(dqt_ref[...])
 
 
-def weights_kernel(core_ref, x_ref, dqkv_ref, att_ref, before_ref, cot_ref, after_ref, keep_ref, send_ref):
+def weights_kernel(
+    core_ref, head_ref, x_ref, dqkv_ref, att_ref, before_ref, cot_ref, cot1_ref, cot2_ref, cot3_ref, after_ref, keep_ref, send_ref
+):
     del after_ref
     second = core_ref[0] == 1
 
@@ -283,10 +296,12 @@
         grads = jnp.transpose(mm3(split(jnp.transpose(dqkv_ref[t])), x))
         for part in range(D // WIDTH):
             put(t * (D // WIDTH) + part, grads[part * WIDTH : (part + 1) * WIDTH])
-    cot = [jnp.concatenate([ref[part, :HALF] for part in range(D // WIDTH)], axis=1) for ref in (before_ref, cot_ref)]
-    grads = mm3(split(att_ref[...]), split(jnp.concatenate(cot, axis=0)))
-    for part in range(D // WIDTH):
-        put(3 * (D // WIDTH) + part, grads[:, part * WIDTH : (part + 1) * WIDTH])
+    cots = [cot_ref, cot1_ref, cot2_ref, cot3_ref]
+    cots = [jnp.concatenate([before_ref[s], ref[:HALF]], axis=0) for s, ref in enumerate(cots)]
+    grads = mm3(split(att_ref[...]), split(jnp.concatenate(cots, axis=1)))
+    for s in range(D // WIDTH):
+        part = along(head_ref[0] + (D // WIDTH - s))[0]
+        put(3 * (D // WIDTH) + part, grads[:, s * WIDTH : (s + 1) * WIDTH])
 
 
 def rows_kernel(dqkv_ref, win_ref, dx_ref, done_ref):
@@ -298,7 +313,7 @@
         dx_ref[part] = mm3(grads, split(win), NT)
 
 
-def call(kernel, outs, *args, scratch=(), sems=(), scalars=0, sent=0, room=8, flops=10**9):
+def call(kernel, outs, *args, scratch=(), sems=(), scalars=0, held=0, sent=0, room=8, flops=10**9):
     size = sum(math.prod(a.shape) * 4 for a in (*args, *outs))
     vmem = pl.BlockSpec(memory_space=pltpu.VMEM)
     hbm = pl.BlockSpec(memory_space=pltpu.HBM)
@@ -306,7 +321,8 @@
         kernel,
         out_shape=tuple(jax.ShapeDtypeStruct(o, F32) for o in [x.shape for x in outs]),
         in_specs=[pl.BlockSpec(memory_space=pltpu.SMEM)] * scalars
-        + [vmem] * (len(args) - scalars),
+        + [hbm] * held
+        + [vmem] * (len(args) - scalars - held),
         out_specs=tuple([hbm] * sent + [vmem] * (len(outs) - sent)),
         scratch_shapes=[pltpu.VMEM(x, F32) if isinstance(x, tuple) else x for x in scratch]
         + [pltpu.SemaphoreType.DMA(n) for n in sems],
@@ -328,25 +344,31 @@
     each = PATCH // peers
     up = [(i, (i + 1) % peers) for i in range(peers)]
     down = [(j, i) for i, j in up]
+    heads = lax.axis_size("head")
+    head = lax.axis_index("head").astype(jnp.int32).reshape(1)
     core = lax.axis_index("core").astype(jnp.int32).reshape(1)
+
+    def ahead(x, step):
+        return lax.ppermute(x, "head", [(i, (i + step) % heads) for i in range(heads)])
 
     def exchange(message):
         rows = message.shape[0]
         return swap(message.reshape(rows, 1, WIDTH), CURVE).reshape(rows, WIDTH)
 
-    cot = lax.all_gather(cotangent, "head", axis=0)
     message, index = call(
         functools.partial(sort_kernel, each), [of(PATCH + peers, WIDTH), of(1, PATCH)],
         destination.reshape(1, PATCH), features,
     )
     arrived = exchange(message)
+    cots = [cotangent] + [ahead(cotangent, s) for s in (1, 2, 3)]
     win = jnp.transpose(input_proj, (1, 0, 2))
     valid = jnp.concatenate([lax.ppermute(real_points[HALF:], CURVE, up), real_points[:HALF]], axis=0)
     valid = valid.reshape(1, PATCH)
     low, high, position, bias = call(
         functools.partial(place_kernel, each),
-        [of(HALF, WIDTH), of(HALF, WIDTH), of(1, PATCH), of(PATCH, WIDTH)], arrived, valid, cot[0, :8],
-    )
+        [of(HALF, WIDTH), of(HALF, WIDTH), of(1, PATCH), of(PATCH, WIDTH)], *cots[1:], arrived, valid, held=3,
+    )
+    before = lax.ppermute(jnp.stack([c[HALF:] for c in cots]), CURVE, up)
     x = jnp.concatenate([lax.ppermute(high, CURVE, up), low], axis=0)
     x = jnp.broadcast_to(x[None], (D // WIDTH, PATCH, WIDTH))
     x = swap(x.reshape(-1, WIDTH), "head").reshape(D // WIDTH, PATCH, WIDTH)
@@ -355,9 +377,8 @@
         [of(3, PATCH, WIDTH), of(WIDTH, PATCH), of(HERE, PATCH)],
         x, win, bias, scratch=[(WIDTH, PATCH)] + [(HERE, PATCH, WIDTH)] * 2, room=24,
     )
-    before = lax.ppermute(cot[:, HALF:], CURVE, up)
     (dqkv,) = call(
-        backward_kernel, [of(3, PATCH, WIDTH)], qkv, attended, lse, before, cot, output_proj, bias,
+        backward_kernel, [of(3, PATCH, WIDTH)], head, qkv, attended, lse, before, *cots, output_proj, bias, scalars=1,
         scratch=[(WIDTH, PATCH)] * 3 + [(PATCH, WIDTH)] + [(HERE, PATCH, WIDTH)] * 4, room=24,
     )
     dx, done = call(
@@ -366,11 +387,11 @@
     dx = swap(dx.reshape(-1, WIDTH), "head").reshape(D // WIDTH, PATCH, WIDTH)
     dx_early, dx_late = call(add_kernel, [of(HALF, WIDTH)] * 2, dx)
     keep, send = call(
-        weights_kernel, [of(BLOCKS, SIDE, WIDTH)] * 2, core, x, dqkv, attended, before, cot, done, scalars=1
-    )
-    (out,) = call(output_kernel, [of(D // WIDTH, PATCH, WIDTH)], attended, output_proj, done)
-    out = lax.psum_scatter(out, "head", scatter_dimension=0)
-    branch_out = jnp.concatenate([out[HALF:], lax.ppermute(out[:HALF], CURVE, down)], axis=0)
+        weights_kernel, [of(BLOCKS, SIDE, WIDTH)] * 2, core, head, x, dqkv, attended, before, *cots, done, scalars=2
+    )
+    out = call(output_kernel, [of(PATCH, WIDTH)] * heads, head, attended, output_proj, done, scalars=1)
+    out = [out[0]] + [ahead(out[s], s) for s in (1, 2, 3)]
+    out_early, out_late = call(sum_kernel, [of(HALF, WIDTH)] * 2, *out)
     sums = keep + lax.ppermute(send, "core", [(0, 1), (1, 0)])
     sums, dx_early = lax.optimization_barrier((sums, dx_early))
     sums = swap(sums.reshape(-1, WIDTH), PLANE).reshape(BLOCKS, SIDE, WIDTH)
@@ -383,9 +404,10 @@
         functools.partial(unpack_kernel, each), [of(BLOCKS, SIDE, WIDTH)], message,
         sent=1, scratch=[(SIDE, WIDTH)], sems=[(BLOCKS,)],
     )
-    sums, branch_out = lax.optimization_barrier((sums, branch_out))
+    sums, out_early = lax.optimization_barrier((sums, out_early))
     sums = swap(sums.reshape(-1, WIDTH), PLANE).reshape(BLOCKS, SIDE, WIDTH)
-    sums, message = lax.optimization_barrier((sums, message))
+    branch_out = jnp.concatenate([out_late, lax.ppermute(out_early, CURVE, down)], axis=0)
+    sums, message, branch_out = lax.optimization_barrier((sums, message, branch_out))
     (grad_features,) = call(functools.partial(unsort_kernel, each), [of(PATCH, WIDTH)], index, message)
     grad_inproj, grad_outproj = call(
         finish_kernel, [of(3, D, WIDTH), of(WIDTH, D)],

time: 207 us -> 198 us (0.957)
  starting transfers between devices: 87.6 us -> 111 us
  blocking collectives: 19.6 us -> 0 us
  between operations: 14.3 us -> 0.98 us
  waiting for transfers between devices: 52.6 us -> 50 us
    all_to_all x1 -> x0, blocking collectives: 19.6 us -> none  [swap(): return lax.all_to_all(x, axis, split_axis=0, concat_axis=0, tiled=True)]
    ppermute x2 -> x8, waiting for transfers between devices: 4.45 us -> 23.4 us  [the longest x6 17.2 us: ahead(): lax.ppermute(x, 'head', [(i, (i + step) % heads) for i in range(heads)])]
    ppermute x2 -> x8, starting transfers between devices: 8.64 us -> 25.7 us  [the longest x6 17.9 us: ahead(): lax.ppermute(x, 'head', [(i, (i + step) % heads) for i in range(heads)])]
    all_gather x1 -> x0, waiting for transfers between devices: 11 us -> none  [shards(): cot = lax.all_gather(cotangent, 'head', axis=0)]
    all_to_all x5 -> x6, waiting for transfers between devices: 26 us -> 17.1 us  [swap(): return lax.all_to_all(x, axis, split_axis=0, concat_axis=0, tiled=True)]
    all_to_all x5 -> x6, starting transfers between devices: 53.7 us -> 59.5 us  [swap(): return lax.all_to_all(x, axis, split_axis=0, concat_axis=0, tiled=True)]
    unnamed x28 -> x42, local copies, waits for them, and re-layouts: 6.16 us -> 10.2 us
    pallas_call x12 -> x13, Pallas kernels: 20.5 us -> 20.5 us  [call(): pl.pallas_call(kernel, out_shape=tuple((jax.ShapeDtypeStruct(o, F32) for...]
  transfers between devices with their start and end apart: 14 -> 19, of which waited for: 11 -> 16; matrix products, arithmetic and copies ran while one was open for 2% -> 1% of each run, Pallas kernels for 5% -> 3%
where the time goes in v6:
time: 198 us; the launch traced here: 196 us
  starting transfers between devices  111 us (56%)
  waiting for transfers between devices  50 us (25%)
  Pallas kernels  20.5 us (10%)
  local copies, waits for them, and re-layouts  11.3 us (6%)
  other arithmetic  2.44 us (1%)
    all_to_all x6, starting transfers between devices, swap(): return lax.all_to_all(x, axis, split_axis=0, concat_axis=0, tiled=True)  59.5 us
    pallas_call x13, Pallas kernels, call(): pl.pallas_call(kernel, out_shape=tuple((jax.ShapeDtypeStruct(o, F32) for...  20.5 us
    ppermute x6, starting transfers between devices, ahead(): lax.ppermute(x, 'head', [(i, (i + step) % heads) for i in range(heads)])  17.9 us
    ppermute x6, waiting for transfers between devices, ahead(): lax.ppermute(x, 'head', [(i, (i + step) % heads) for i in range(heads)])  17.2 us
    all_to_all x6, waiting for transfers between devices, swap(): return lax.all_to_all(x, axis, split_axis=0, concat_axis=0, tiled=True)  17.1 us
    unnamed x42, local copies, waits for them, and re-layouts  10.2 us
    ppermute x1, starting transfers between devices, shards(): sums = keep + lax.ppermute(send, 'core', [(0, 1), (1, 0)])  7.76 us
    ppermute x1, waiting for transfers between devices, shards(): lax.ppermute(out_early, CURVE, down)  6.13 us
  transfers between devices with their start and end apart: 19, of which 16 were waited for; matrix products, arithmetic and copies ran while one was open for 1% of the time, Pallas kernels for 3%

profile of v6, /device:TPU:1, one launch (start us, length us, event | category | flops | bytes accessed | tf_op | source)
XLA Modules:
  0.0 196.5 jit_solution(10888739866211410541)
XLA Ops:
  3.9 20.5 %all-to-all-start = ((f32[640,1,128]{2,1,0:T(1,128)}), f32[640,1,128]{2,1,0:T(1,128)S(1)}, u32[]{:S(2)}, u32[]{:S(2)}) async-start(f32[640,1,128]{2,1,0:T(1,128)} %bitcast.2), calls=%async_computation | async-start | bytes 655360 | tf_op jit(solution)/shard_map/all_to_all | solution.py:339
  24.4 4.6 %collective-permute-start.2 = (f32[512,128]{1,0:T(8,128)S(1)}, f32[512,128]{1,0:T(8,128)S(1)}, u32[]{:S(2)}, u32[]{:S(2)}) collective-permute-start(f32[512,128]{1,0:T(8,128)S(1)} %copy-done), channel_id=1, source_target_pairs={{0,3},{1,0},{2,1},{3,2},{4,7},{5,4},{6,5},{7,6},{8,11},{9,8},{10,9... | collective-permute-start | bytes 786440 | tf_op jit(solution)/shard_map/ppermute | solution.py:352
  29.0 2.3 %collective-permute-start.1 = (f32[512,128]{1,0:T(8,128)S(1)}, f32[512,128]{1,0:T(8,128)S(1)}, u32[]{:S(2)}, u32[]{:S(2)}) collective-permute-start(f32[512,128]{1,0:T(8,128)S(1)} %copy-done), channel_id=1, source_target_pairs={{0,2},{1,3},{2,0},{3,1},{4,6},{5,7},{6,4},{7,5},{8,10},{9,11},{10,... | collective-permute-start | bytes 786440 | tf_op jit(solution)/shard_map/ppermute | solution.py:352
  31.3 2.6 %collective-permute-start = (f32[512,128]{1,0:T(8,128)S(1)}, f32[512,128]{1,0:T(8,128)S(1)}, u32[]{:S(2)}, u32[]{:S(2)}) collective-permute-start(f32[512,128]{1,0:T(8,128)S(1)} %copy-done), channel_id=1, source_target_pairs={{0,1},{1,2},{2,3},{3,0},{4,5},{5,6},{6,7},{7,4},{8,9},{9,10},{10,1... | collective-permute-start | bytes 786440 | tf_op jit(solution)/shard_map/ppermute | solution.py:352
  33.9 4.4 %collective-permute-start.3 = (s32[256]{0:T(256)S(1)}, s32[256]{0:T(256)S(1)}, u32[]{:S(2)}, u32[]{:S(2)}) collective-permute-start(s32[256]{0:T(256)S(1)} %get-tuple-element.64), channel_id=1, source_target_pairs={{0,4},{4,8},{8,12},{12,16},{16,20},{20,24},{24,28},{28,32},{32,36}... | collective-permute-start | bytes 3080 | tf_op jit(solution)/shard_map/ppermute | solution.py:365
  39.1 7.2 %collective-permute-done.after1_ref.cot1_ref = f32[512,128]{1,0:T(8,128)S(1)} collective-permute-done((f32[512,128]{1,0:T(8,128)S(1)}, f32[512,128]{1,0:T(8,128)S(1)}, u32[]{:S(2)}, u32[]{:S(2)}) %collective-permute-start) | collective-permute-done | bytes 262176 | tf_op jit(solution)/shard_map/ppermute | solution.py:352
  48.0 4.2 %collective-permute-start.4 = (f32[256,128]{1,0:T(8,128)S(1)}, f32[256,128]{1,0:T(8,128)S(1)}, u32[]{:S(2)}, u32[]{:S(2)}) collective-permute-start(f32[256,128]{1,0:T(8,128)S(1)} %get-tuple-element.36), channel_id=1, source_target_pairs={{0,4},{4,8},{8,12},{12,16},{16,20},{20,24},{24,28},{28,32},{32,36}... | collective-permute-start | bytes 393224 | tf_op jit(solution)/shard_map/ppermute | solution.py:372
  52.2 1.9 collective-permute-done.4
  55.2 4.2 %all-to-all-start.1 = ((f32[4,512,128]{2,1,0:T(8,128)}), f32[4,512,128]{2,1,0:T(8,128)S(1)}, u32[]{:S(2)}, u32[]{:S(2)}) async-start(f32[4,512,128]{2,1,0:T(8,128)} %broadcast_in_dim.2), calls=%async_computation.1 | async-start | bytes 2097152 | tf_op jit(solution)/shard_map/all_to_all | solution.py:339
  60.3 4.8 %collective-permute-start.5 = (f32[4,256,128]{2,1,0:T(8,128)}, f32[4,256,128]{2,1,0:T(8,128)S(1)}, u32[]{:S(2)}, u32[]{:S(2)}) collective-permute-start(f32[4,256,128]{2,1,0:T(8,128)} %pad_maximum_fusion), channel_id=1, source_target_pairs={{0,4},{4,8},{8,12},{12,16},{16,20},{20,24},{24,28},{28,32},{32,36}... | collective-permute-start | bytes 1572872 | tf_op jit(solution)/shard_map/ppermute | solution.py:371
  65.1 4.5 %all-to-all-done.1.x_ref = f32[4,512,128]{2,1,0:T(8,128)S(1)} async-done(((f32[4,512,128]{2,1,0:T(8,128)}), f32[4,512,128]{2,1,0:T(8,128)S(1)}, u32[]{:S(2)}, u32[]{:S(2)}) %all-to-all-start.1) | async-done | bytes 1048608 | tf_op jit(solution)/shard_map/all_to_all | solution.py:339
  70.7 3.7 %shard_map.95 = (f32[3,512,128]{2,1,0:T(8,128)S(1)}, f32[128,512]{1,0:T(8,128)S(1)}, f32[4,512]{1,0:T(4,128)S(1)}) custom-call(f32[4,512,128]{2,1,0:T(8,128)S(1)} %all-to-all-done.1.x_ref, f32[3,512,128]{2,1,0:T(8,128)S(1)} %bitcast.26, f32[512,128]{1,0:T(8,128)S(1)} %get-tuple-element.38.bias_ref), custom_call_target="tpu_custom_call" | custom-call | flops 1000000000 | bytes 3153920 | tf_op jit(solution)/shard_map/pallas_call | solution.py:320
  77.2 5.2 %shard_map.96.dqkv_ref = f32[3,512,128]{2,1,0:T(8,128)S(1)} custom-call(s32[1]{0:T(128)} %bitcast.5.head_ref, f32[3,512,128]{2,1,0:T(8,128)S(1)} %get-tuple-element.39.qkv_ref, f32[128,512]{1,0:T(8,128)S(1)} %get-tuple-element.40.att_ref, f32[4,512]{1,0:T(4,128)S(1)} %get-tuple-element.41.lse_ref, f32[4,256,128]{2,1,0:T(8,128)S(1)} %copy-done.7, ...), custom_call_target="tpu_custom_call" | custom-call | flops 1000000000 | bytes 3940356 | tf_op jit(solution)/shard_map/pallas_call | solution.py:320
  83.2 2.4 %shard_map.97 = (f32[4,512,128]{2,1,0:T(8,128)}, f32[8,128]{1,0:T(8,128)S(1)}) custom-call(f32[3,512,128]{2,1,0:T(8,128)S(1)} %shard_map.96.dqkv_ref, f32[3,512,128]{2,1,0:T(8,128)S(1)} %bitcast.27), custom_call_target="tpu_custom_call" | custom-call | flops 1000000000 | bytes 2625536 | tf_op jit(solution)/shard_map/pallas_call | solution.py:320
  85.6 3.5 %all-to-all-start.2 = ((f32[4,512,128]{2,1,0:T(8,128)}), f32[4,512,128]{2,1,0:T(8,128)S(1)}, u32[]{:S(2)}, u32[]{:S(2)}) async-start(f32[4,512,128]{2,1,0:T(8,128)} %get-tuple-element.42), calls=%async_computation.2 | async-start | bytes 2097152 | tf_op jit(solution)/shard_map/all_to_all | solution.py:339
  94.1 7.8 %collective-permute-start.6 = (f32[16,64,128]{2,1,0:T(8,128)S(1)}, f32[16,64,128]{2,1,0:T(8,128)S(1)}, u32[]{:S(2)}, u32[]{:S(2)}) collective-permute-start(f32[16,64,128]{2,1,0:T(8,128)S(1)} %get-tuple-element.46), channel_id=1, source_target_pairs={{0,4},{4,0},{1,5},{5,1},{2,6},{6,2},{3,7},{7,3},{8,12},{12,8},{9,1... | collective-permute-start | bytes 1572872 | tf_op jit(solution)/shard_map/ppermute | solution.py:395
  104.3 7.8 %all-to-all-start.3 = ((f32[16,64,128]{2,1,0:T(8,128)}), f32[16,64,128]{2,1,0:T(8,128)S(1)}, u32[]{:S(2)}, u32[]{:S(2)}) async-start(f32[16,64,128]{2,1,0:T(8,128)} %add.3), calls=%async_computation.3 | async-start | bytes 1048576 | tf_op jit(solution)/shard_map/all_to_all | solution.py:339
  112.2 5.1 %collective-permute-start.7 = (f32[256,128]{1,0:T(8,128)S(1)}, f32[256,128]{1,0:T(8,128)S(1)}, u32[]{:S(2)}, u32[]{:S(2)}) collective-permute-start(f32[256,128]{1,0:T(8,128)S(1)} %get-tuple-element.48), channel_id=1, source_target_pairs={{4,0},{8,4},{12,8},{16,12},{20,16},{24,20},{28,24},{32,28},{36,32}... | collective-permute-start | bytes 393224 | tf_op jit(solution)/shard_map/ppermute | solution.py:400
  117.3 5.2 %collective-permute-done.7.high_ref = f32[256,128]{1,0:T(8,128)S(1)} collective-permute-done((f32[256,128]{1,0:T(8,128)S(1)}, f32[256,128]{1,0:T(8,128)S(1)}, u32[]{:S(2)}, u32[]{:S(2)}) %collective-permute-start.7) | collective-permute-done | bytes 131104 | tf_op jit(solution)/shard_map/ppermute | solution.py:400
  125.2 17.3 %all-to-all-start.4 = ((f32[768,1,128]{2,1,0:T(1,128)}), f32[768,1,128]{2,1,0:T(1,128)S(1)}, u32[]{:S(2)}, u32[]{:S(2)}) async-start(f32[768,1,128]{2,1,0:T(1,128)} %bitcast.13), calls=%async_computation.4 | async-start | bytes 786432 | tf_op jit(solution)/shard_map/all_to_all | solution.py:339
  143.2 2.2 %collective-permute-start.8 = (f32[512,128]{1,0:T(8,128)S(1)}, f32[512,128]{1,0:T(8,128)S(1)}, u32[]{:S(2)}, u32[]{:S(2)}) collective-permute-start(f32[512,128]{1,0:T(8,128)S(1)} %get-tuple-element.51), channel_id=1, source_target_pairs={{0,1},{1,2},{2,3},{3,0},{4,5},{5,6},{6,7},{7,4},{8,9},{9,10},{10,1... | collective-permute-start | bytes 786440 | tf_op jit(solution)/shard_map/ppermute | solution.py:352
  145.4 3.7 %collective-permute-start.9 = (f32[512,128]{1,0:T(8,128)S(1)}, f32[512,128]{1,0:T(8,128)S(1)}, u32[]{:S(2)}, u32[]{:S(2)}) collective-permute-start(f32[512,128]{1,0:T(8,128)S(1)} %get-tuple-element.52), channel_id=1, source_target_pairs={{0,2},{1,3},{2,0},{3,1},{4,6},{5,7},{6,4},{7,5},{8,10},{9,11},{10,... | collective-permute-start | bytes 786440 | tf_op jit(solution)/shard_map/ppermute | solution.py:352
  149.1 2.5 %collective-permute-start.10 = (f32[512,128]{1,0:T(8,128)S(1)}, f32[512,128]{1,0:T(8,128)S(1)}, u32[]{:S(2)}, u32[]{:S(2)}) collective-permute-start(f32[512,128]{1,0:T(8,128)S(1)} %get-tuple-element.53), channel_id=1, source_target_pairs={{0,3},{1,0},{2,1},{3,2},{4,7},{5,4},{6,5},{7,6},{8,11},{9,8},{10,9... | collective-permute-start | bytes 786440 | tf_op jit(solution)/shard_map/ppermute | solution.py:352
  151.7 2.2 %collective-permute-done.8.second_ref = f32[512,128]{1,0:T(8,128)S(1)} collective-permute-done((f32[512,128]{1,0:T(8,128)S(1)}, f32[512,128]{1,0:T(8,128)S(1)}, u32[]{:S(2)}, u32[]{:S(2)}) %collective-permute-start.8) | collective-permute-done | bytes 262176 | tf_op jit(solution)/shard_map/ppermute | solution.py:352
  153.9 4.5 %collective-permute-done.9.third_ref = f32[512,128]{1,0:T(8,128)S(1)} collective-permute-done((f32[512,128]{1,0:T(8,128)S(1)}, f32[512,128]{1,0:T(8,128)S(1)}, u32[]{:S(2)}, u32[]{:S(2)}) %collective-permute-start.9) | collective-permute-done | bytes 262176 | tf_op jit(solution)/shard_map/ppermute | solution.py:352
  158.3 3.3 %collective-permute-done.10.fourth_ref = f32[512,128]{1,0:T(8,128)S(1)} collective-permute-done((f32[512,128]{1,0:T(8,128)S(1)}, f32[512,128]{1,0:T(8,128)S(1)}, u32[]{:S(2)}, u32[]{:S(2)}) %collective-permute-start.10) | collective-permute-done | bytes 262176 | tf_op jit(solution)/shard_map/ppermute | solution.py:352
  161.7 6.3 %all-to-all-done.4 = f32[768,1,128]{2,1,0:T(1,128)S(1)} async-done(((f32[768,1,128]{2,1,0:T(1,128)}), f32[768,1,128]{2,1,0:T(1,128)S(1)}, u32[]{:S(2)}, u32[]{:S(2)}) %all-to-all-start.4) | async-done | bytes 393248 | tf_op jit(solution)/shard_map/all_to_all | solution.py:339
  169.0 6.1 %all-to-all-start.5 = ((f32[16,64,128]{2,1,0:T(8,128)}), f32[16,64,128]{2,1,0:T(8,128)S(1)}, u32[]{:S(2)}, u32[]{:S(2)}) async-start(f32[16,64,128]{2,1,0:T(8,128)} %shard_map.101), calls=%async_computation.5 | async-start | bytes 1048576 | tf_op jit(solution)/shard_map/all_to_all | solution.py:339
  175.1 3.0 %collective-permute-start.11 = (f32[256,128]{1,0:T(8,128)S(1)}, f32[256,128]{1,0:T(8,128)S(1)}, u32[]{:S(2)}, u32[]{:S(2)}) collective-permute-start(f32[256,128]{1,0:T(8,128)S(1)} %get-tuple-element.57), channel_id=1, source_target_pairs={{4,0},{8,4},{12,8},{16,12},{20,16},{24,20},{28,24},{32,28},{36,32}... | collective-permute-start | bytes 393224 | tf_op jit(solution)/shard_map/ppermute | solution.py:409
  178.1 6.1 %collective-permute-done.11 = f32[256,128]{1,0:T(8,128)S(1)} collective-permute-done((f32[256,128]{1,0:T(8,128)S(1)}, f32[256,128]{1,0:T(8,128)S(1)}, u32[]{:S(2)}, u32[]{:S(2)}) %collective-permute-start.11) | collective-permute-done | bytes 131104 | tf_op jit(solution)/shard_map/ppermute | solution.py:409
  185.0 3.8 %all-to-all-done.5.mine_ref = f32[16,64,128]{2,1,0:T(8,128)S(1)} async-done(((f32[16,64,128]{2,1,0:T(8,128)}), f32[16,64,128]{2,1,0:T(8,128)S(1)}, u32[]{:S(2)}, u32[]{:S(2)}) %all-to-all-start.5) | async-done | bytes 524320 | tf_op jit(solution)/shard_map/all_to_all | solution.py:339
  188.8 4.6 %collective-permute-start.12 = (f32[16,64,128]{2,1,0:T(8,128)S(1)}, f32[16,64,128]{2,1,0:T(8,128)S(1)}, u32[]{:S(2)}, u32[]{:S(2)}) collective-permute-start(f32[16,64,128]{2,1,0:T(8,128)S(1)} %all-to-all-done.5.mine_ref), channel_id=1, source_target_pairs={{0,4},{4,0},{1,5},{5,1},{2,6},{6,2},{3,7},{7,3},{8,12},{12,8},{9,1... | collective-permute-start | bytes 1572872 | tf_op jit(solution)/shard_map/ppermute | solution.py:414
  (72 shorter events, 27.9 us)
Async XLA Ops:
  3.9 20.5 %copy-start = (f32[512,128]{1,0:T(8,128)S(1)}, f32[512,128]{1,0:T(8,128)}, u32[]{:S(2)}) copy-start(f32[512,128]{1,0:T(8,128)} %cot_ref.3) | copy-start | bytes 786436
  3.9 30.1 %copy-start.20 = (s32[512]{0:T(512)S(1)}, s32[512]{0:T(512)}, u32[]{:S(2)}) copy-start(s32[512]{0:T(512)} %param.10) | copy-start | bytes 6148
  3.9 43.5 %all-to-all-start = ((f32[640,1,128]{2,1,0:T(1,128)}), f32[640,1,128]{2,1,0:T(1,128)S(1)}, u32[]{:S(2)}, u32[]{:S(2)}) async-start(f32[640,1,128]{2,1,0:T(1,128)} %bitcast.2), calls=%async_computation | async-start | bytes 655360 | tf_op jit(solution)/shard_map/all_to_all | solution.py:339
  24.4 14.6 %collective-permute-start.2 = (f32[512,128]{1,0:T(8,128)S(1)}, f32[512,128]{1,0:T(8,128)S(1)}, u32[]{:S(2)}, u32[]{:S(2)}) collective-permute-start(f32[512,128]{1,0:T(8,128)S(1)} %copy-done), channel_id=1, source_target_pairs={{0,3},{1,0},{2,1},{3,2},{4,7},{5,4},{6,5},{7,6},{8,11},{9,8},{10,9... | collective-permute-start | bytes 786440 | tf_op jit(solution)/shard_map/ppermute | solution.py:352
  29.0 10.1 %collective-permute-start.1 = (f32[512,128]{1,0:T(8,128)S(1)}, f32[512,128]{1,0:T(8,128)S(1)}, u32[]{:S(2)}, u32[]{:S(2)}) collective-permute-start(f32[512,128]{1,0:T(8,128)S(1)} %copy-done), channel_id=1, source_target_pairs={{0,2},{1,3},{2,0},{3,1},{4,6},{5,7},{6,4},{7,5},{8,10},{9,11},{10,... | collective-permute-start | bytes 786440 | tf_op jit(solution)/shard_map/ppermute | solution.py:352
  31.3 15.0 %collective-permute-start = (f32[512,128]{1,0:T(8,128)S(1)}, f32[512,128]{1,0:T(8,128)S(1)}, u32[]{:S(2)}, u32[]{:S(2)}) collective-permute-start(f32[512,128]{1,0:T(8,128)S(1)} %copy-done), channel_id=1, source_target_pairs={{0,1},{1,2},{2,3},{3,0},{4,5},{5,6},{6,7},{7,4},{8,9},{9,10},{10,1... | collective-permute-start | bytes 786440 | tf_op jit(solution)/shard_map/ppermute | solution.py:352
  33.9 5.1 %collective-permute-start.3 = (s32[256]{0:T(256)S(1)}, s32[256]{0:T(256)S(1)}, u32[]{:S(2)}, u32[]{:S(2)}) collective-permute-start(s32[256]{0:T(256)S(1)} %get-tuple-element.64), channel_id=1, source_target_pairs={{0,4},{4,8},{8,12},{12,16},{16,20},{20,24},{24,28},{28,32},{32,36}... | collective-permute-start | bytes 3080 | tf_op jit(solution)/shard_map/ppermute | solution.py:365
  39.1 36.1 %copy-start.1 = (f32[512,128]{1,0:T(8,128)}, f32[512,128]{1,0:T(8,128)S(1)}, u32[]{:S(2)}) copy-start(f32[512,128]{1,0:T(8,128)S(1)} %collective-permute-done.1.after2_ref.cot2_ref) | copy-start | bytes 786436
  46.3 13.1 %copy-start.3 = (f32[512,128]{1,0:T(8,128)}, f32[512,128]{1,0:T(8,128)S(1)}, u32[]{:S(2)}) copy-start(f32[512,128]{1,0:T(8,128)S(1)} %collective-permute-done.after1_ref.cot1_ref) | copy-start | bytes 786436
  48.0 21.6 %copy-start.14 = (f32[512,128]{1,0:T(8,128)}, f32[512,128]{1,0:T(8,128)S(1)}, u32[]{:S(2)}) copy-start(f32[512,128]{1,0:T(8,128)S(1)} %get-tuple-element.38.bias_ref) | copy-start | bytes 786436
  48.0 6.1 %collective-permute-start.4 = (f32[256,128]{1,0:T(8,128)S(1)}, f32[256,128]{1,0:T(8,128)S(1)}, u32[]{:S(2)}, u32[]{:S(2)}) collective-permute-start(f32[256,128]{1,0:T(8,128)S(1)} %get-tuple-element.36), channel_id=1, source_target_pairs={{0,4},{4,8},{8,12},{12,16},{16,20},{20,24},{24,28},{28,32},{32,36}... | collective-permute-start | bytes 393224 | tf_op jit(solution)/shard_map/ppermute | solution.py:372
  55.2 14.4 %all-to-all-start.1 = ((f32[4,512,128]{2,1,0:T(8,128)}), f32[4,512,128]{2,1,0:T(8,128)S(1)}, u32[]{:S(2)}, u32[]{:S(2)}) async-start(f32[4,512,128]{2,1,0:T(8,128)} %broadcast_in_dim.2), calls=%async_computation.1 | async-start | bytes 2097152 | tf_op jit(solution)/shard_map/all_to_all | solution.py:339
  60.3 14.2 %collective-permute-start.5 = (f32[4,256,128]{2,1,0:T(8,128)}, f32[4,256,128]{2,1,0:T(8,128)S(1)}, u32[]{:S(2)}, u32[]{:S(2)}) collective-permute-start(f32[4,256,128]{2,1,0:T(8,128)} %pad_maximum_fusion), channel_id=1, source_target_pairs={{0,4},{4,8},{8,12},{12,16},{16,20},{20,24},{24,28},{28,32},{32,36}... | collective-permute-start | bytes 1572872 | tf_op jit(solution)/shard_map/ppermute | solution.py:371
  69.6 1.1 copy-start.16
  70.7 4.5 %copy-start.4 = (f32[512,128]{1,0:T(8,128)S(1)}, f32[512,128]{1,0:T(8,128)}, u32[]{:S(2)}) copy-start(f32[512,128]{1,0:T(8,128)} %copy-done.3) | copy-start | bytes 786436
  70.7 4.5 %copy-start.9 = (f32[128,512]{1,0:T(8,128)S(1)}, f32[128,512]{1,0:T(8,128)}, u32[]{:S(2)}) copy-start(f32[128,512]{1,0:T(8,128)} %wout_ref.3) | copy-start | bytes 786436
  75.2 1.0 copy-start.7
  77.2 5.9 %copy-start.17 = (f32[512,3,128]{2,0,1:T(8,128)S(1)}, f32[512,3,128]{2,0,1:T(8,128)}, u32[]{:S(2)}) copy-start(f32[512,3,128]{2,0,1:T(8,128)} %param.7) | copy-start | bytes 2359300
  85.6 18.7 %all-to-all-start.2 = ((f32[4,512,128]{2,1,0:T(8,128)}), f32[4,512,128]{2,1,0:T(8,128)S(1)}, u32[]{:S(2)}, u32[]{:S(2)}) async-start(f32[4,512,128]{2,1,0:T(8,128)} %get-tuple-element.42), calls=%async_computation.2 | async-start | bytes 2097152 | tf_op jit(solution)/shard_map/all_to_all | solution.py:339
  91.0 1.0 copy-start.8
  94.1 9.3 %collective-permute-start.6 = (f32[16,64,128]{2,1,0:T(8,128)S(1)}, f32[16,64,128]{2,1,0:T(8,128)S(1)}, u32[]{:S(2)}, u32[]{:S(2)}) collective-permute-start(f32[16,64,128]{2,1,0:T(8,128)S(1)} %get-tuple-element.46), channel_id=1, source_target_pairs={{0,4},{4,0},{1,5},{5,1},{2,6},{6,2},{3,7},{7,3},{8,12},{12,8},{9,1... | collective-permute-start | bytes 1572872 | tf_op jit(solution)/shard_map/ppermute | solution.py:395
  104.3 19.5 %all-to-all-start.3 = ((f32[16,64,128]{2,1,0:T(8,128)}), f32[16,64,128]{2,1,0:T(8,128)S(1)}, u32[]{:S(2)}, u32[]{:S(2)}) async-start(f32[16,64,128]{2,1,0:T(8,128)} %add.3), calls=%async_computation.3 | async-start | bytes 1048576 | tf_op jit(solution)/shard_map/all_to_all | solution.py:339
  112.2 10.3 %collective-permute-start.7 = (f32[256,128]{1,0:T(8,128)S(1)}, f32[256,128]{1,0:T(8,128)S(1)}, u32[]{:S(2)}, u32[]{:S(2)}) collective-permute-start(f32[256,128]{1,0:T(8,128)S(1)} %get-tuple-element.48), channel_id=1, source_target_pairs={{4,0},{8,4},{12,8},{16,12},{20,16},{24,20},{28,24},{32,28},{36,32}... | collective-permute-start | bytes 393224 | tf_op jit(solution)/shard_map/ppermute | solution.py:400
  125.2 17.4 %copy-start.10 = (f32[128,512]{1,0:T(8,128)S(1)}, f32[128,512]{1,0:T(8,128)}, u32[]{:S(2)}) copy-start(f32[128,512]{1,0:T(8,128)} %wout_ref.3) | copy-start | bytes 786436
  125.2 17.4 %copy-start.13 = (f32[128,512]{1,0:T(8,128)S(1)}, f32[128,512]{1,0:T(8,128)}, u32[]{:S(2)}) copy-start(f32[128,512]{1,0:T(8,128)} %copy-done.11) | copy-start | bytes 786436
  125.2 42.8 %all-to-all-start.4 = ((f32[768,1,128]{2,1,0:T(1,128)}), f32[768,1,128]{2,1,0:T(1,128)S(1)}, u32[]{:S(2)}, u32[]{:S(2)}) async-start(f32[768,1,128]{2,1,0:T(1,128)} %bitcast.13), calls=%async_computation.4 | async-start | bytes 786432 | tf_op jit(solution)/shard_map/all_to_all | solution.py:339
  143.2 10.6 %collective-permute-start.8 = (f32[512,128]{1,0:T(8,128)S(1)}, f32[512,128]{1,0:T(8,128)S(1)}, u32[]{:S(2)}, u32[]{:S(2)}) collective-permute-start(f32[512,128]{1,0:T(8,128)S(1)} %get-tuple-element.51), channel_id=1, source_target_pairs={{0,1},{1,2},{2,3},{3,0},{4,5},{5,6},{6,7},{7,4},{8,9},{9,10},{10,1... | collective-permute-start | bytes 786440 | tf_op jit(solution)/shard_map/ppermute | solution.py:352
  145.4 12.9 %collective-permute-start.9 = (f32[512,128]{1,0:T(8,128)S(1)}, f32[512,128]{1,0:T(8,128)S(1)}, u32[]{:S(2)}, u32[]{:S(2)}) collective-permute-start(f32[512,128]{1,0:T(8,128)S(1)} %get-tuple-element.52), channel_id=1, source_target_pairs={{0,2},{1,3},{2,0},{3,1},{4,6},{5,7},{6,4},{7,5},{8,10},{9,11},{10,... | collective-permute-start | bytes 786440 | tf_op jit(solution)/shard_map/ppermute | solution.py:352
  149.1 12.5 %collective-permute-start.10 = (f32[512,128]{1,0:T(8,128)S(1)}, f32[512,128]{1,0:T(8,128)S(1)}, u32[]{:S(2)}, u32[]{:S(2)}) collective-permute-start(f32[512,128]{1,0:T(8,128)S(1)} %get-tuple-element.53), channel_id=1, source_target_pairs={{0,3},{1,0},{2,1},{3,2},{4,7},{5,4},{6,5},{7,6},{8,11},{9,8},{10,9... | collective-permute-start | bytes 786440 | tf_op jit(solution)/shard_map/ppermute | solution.py:352
  169.0 19.8 %all-to-all-start.5 = ((f32[16,64,128]{2,1,0:T(8,128)}), f32[16,64,128]{2,1,0:T(8,128)S(1)}, u32[]{:S(2)}, u32[]{:S(2)}) async-start(f32[16,64,128]{2,1,0:T(8,128)} %shard_map.101), calls=%async_computation.5 | async-start | bytes 1048576 | tf_op jit(solution)/shard_map/all_to_all | solution.py:339
  175.1 9.1 %collective-permute-start.11 = (f32[256,128]{1,0:T(8,128)S(1)}, f32[256,128]{1,0:T(8,128)S(1)}, u32[]{:S(2)}, u32[]{:S(2)}) collective-permute-start(f32[256,128]{1,0:T(8,128)S(1)} %get-tuple-element.57), channel_id=1, source_target_pairs={{4,0},{8,4},{12,8},{16,12},{20,16},{24,20},{28,24},{32,28},{36,32}... | collective-permute-start | bytes 393224 | tf_op jit(solution)/shard_map/ppermute | solution.py:409
  188.8 6.1 %collective-permute-start.12 = (f32[16,64,128]{2,1,0:T(8,128)S(1)}, f32[16,64,128]{2,1,0:T(8,128)S(1)}, u32[]{:S(2)}, u32[]{:S(2)}) collective-permute-start(f32[16,64,128]{2,1,0:T(8,128)S(1)} %all-to-all-done.5.mine_ref), channel_id=1, source_target_pairs={{0,4},{4,0},{1,5},{5,1},{2,6},{6,2},{3,7},{7,3},{8,12},{12,8},{9,1... | collective-permute-start | bytes 1572872 | tf_op jit(solution)/shard_map/ppermute | solution.py:414
  (8 other events, 6.9 us)

commit v7 on v6

--- a/solution.py
+++ b/solution.py
@@ -76,7 +76,7 @@
     return ref[pl.ds(first, ref.shape[0] // step, stride=step), :]
 
 
-def sort_kernel(each, dest_ref, feat_ref, message_ref, index_ref):
+def index_kernel(each, dest_ref, index_ref, lists_ref):
     peers = PATCH // each
     dest = dest_ref[...]
     block = dest // PATCH
@@ -84,17 +84,21 @@
     block = block.astype(F32)
     same = (wide(column(block)) == block) & (iota(0) < iota(1))
     rank = jnp.sum(jnp.where(same, 1.0, 0.0), axis=0, keepdims=True)
-    index = rank * peers + block
-    index_ref[...] = index
-    rows = select_rows(one_hot(iota(0) == index), feat_ref[...])
+    index_ref[...] = rank * peers + block
+    high, low = split(jnp.where(iota(1, (PATCH, WIDTH)) == column(rank), column(local), 0.0))
+    mine = one_hot(iota(0, (peers, PATCH)) == block)
+    lists_ref[...] = mm(mine, high) + mm(mine, low)
+
+
+def sort_kernel(each, index_ref, lists_ref, feat_ref, message_ref):
+    peers = PATCH // each
+    rows = select_rows(one_hot(iota(0) == index_ref[...]), feat_ref[...])
     for turn in range(each):
         message_ref[pl.ds(turn, peers, stride=each + 1), :] = rows[turn * peers : (turn + 1) * peers]
-    high, low = split(jnp.where(iota(1, (PATCH, WIDTH)) == column(rank), column(local), 0.0))
-    mine = one_hot(iota(0, (peers, PATCH)) == block)
-    message_ref[pl.ds(each, peers, stride=each + 1), :] = mm(mine, high) + mm(mine, low)
-
-
-def place_kernel(each, after1_ref, after2_ref, after3_ref, message_ref, valid_ref, low_ref, high_ref, position_ref, bias_ref):
+    message_ref[pl.ds(each, peers, stride=each + 1), :] = lists_ref[...]
+
+
+def place_kernel(each, after1_ref, after2_ref, after3_ref, message_ref, low_ref, high_ref, position_ref):
     del after1_ref, after2_ref, after3_ref
     turned = jnp.transpose(every(message_ref, each, each + 1))
     position = jnp.concatenate([turned[turn : turn + 1] for turn in range(each)], axis=1)
@@ -103,7 +107,6 @@
     placed = select_rows(one_hot(iota(0) == position), arrived)
     low_ref[...] = placed[:HALF]
     high_ref[...] = placed[HALF:]
-    bias_ref[...] = column(jnp.where(valid_ref[...] > 0, 0.0, -jnp.inf))
 
 
 def add_kernel(parts_ref, early_ref, late_ref):
@@ -124,8 +127,10 @@
         sums += sums_ref[part]
     near = SIDE // ADDED
     for turn in range(ADDED):
-        rows = jnp.concatenate([sums[turn * near : (turn + 1) * near]] * (peers // near), axis=0)
-        message_ref[pl.ds(each + turn, peers, stride=size), :] = rows
+        for core in range(2):
+            first = turn * near + core * BLOCKS
+            rows = jnp.concatenate([sums[first : first + BLOCKS]] * (peers // near), axis=0)
+            message_ref[pl.ds(core * size + each + turn, peers // 2, stride=2 * size), :] = rows
 
 
 def unpack_kernel(each, message_ref, out_hbm, sums_ref, sems):
@@ -148,7 +153,7 @@
     out_ref[...] = select_rows(one_hot(wide(column(index_ref[...])) == iota(1)), returned)
 
 
-def finish_kernel(core_ref, mine_ref, other_ref, din_ref, dout_ref, out_ref):
+def finish_kernel(core_ref, mine_ref, other_ref, din_ref, dout_ref):
     core = core_ref[0]
     near = SIDE // ADDED
     for own, ref in ((core, mine_ref), (1 - core, other_ref)):
@@ -157,13 +162,11 @@
             for side in range(2):
                 for turn in range(ADDED):
                     got = ref[:, turn * near + 2 * block + side, :]
-                    first = side * SIDE + turn * near + own
+                    first = pl.multiple_of(side * SIDE + turn * near + own * BLOCKS, BLOCKS)
                     if t < 3:
-                        din_ref[t, pl.ds(part * WIDTH + first, BLOCKS, stride=2), :] = got
+                        din_ref[t, pl.ds(part * WIDTH + first, BLOCKS), :] = got
                     else:
-                        out_ref[part, pl.ds(first, BLOCKS, stride=2), :] = got
-    for part in range(D // WIDTH):
-        dout_ref[:, part * WIDTH : (part + 1) * WIDTH] = out_ref[part]
+                        dout_ref[pl.ds(first, BLOCKS), part * WIDTH : (part + 1) * WIDTH] = got
 
 
 def head_mask(head):
@@ -191,7 +194,7 @@
         ref[i] = part
 
 
-def forward_kernel(x_ref, win_ref, bias_ref, qkv_ref, att_ref, lse_ref, vt_ref, q_ref, k_ref):
+def forward_kernel(x_ref, win_ref, valid_ref, qkv_ref, att_ref, lse_ref, vt_ref, q_ref, k_ref):
     x = jnp.concatenate([x_ref[part] for part in range(D // WIDTH)], axis=1)
     win = jnp.concatenate([win_ref[t] for t in range(3)], axis=1)
     qkv = mm3(split(x), split(win))
@@ -200,7 +203,7 @@
     vt_ref[...] = jnp.transpose(qkv_ref[2])
     keep(q_ref, turned(qkv_ref[0] * (SCALE * LOG2E), "hhll"))
     keep(k_ref, turned(qkv_ref[1], "hlhl"))
-    bias = wide(bias_ref[...])
+    bias = wide(column(jnp.where(valid_ref[...] > 0, 0.0, -jnp.inf)))
 
     def one(head, carry):
         scores = mm(of_head(k_ref, head), of_head(q_ref, head), NT) + bias
@@ -219,6 +222,16 @@
     lax.fori_loop(0, HERE, one, 0, unroll=True)
 
 
+def cot_kernel(head_ref, cot_ref, cot1_ref, cot2_ref, cot3_ref, wout_ref, early_ref, late_ref, send_ref):
+    cots = [ref[...] for ref in (cot_ref, cot1_ref, cot2_ref, cot3_ref)]
+    wout = [wout_ref[:, along(head_ref[0] + (D // WIDTH - s))[1]] for s in range(D // WIDTH)]
+    grads = mm3(split(jnp.concatenate(cots, axis=1)), split(jnp.concatenate(wout, axis=1)), NT)
+    early_ref[...] = grads[:HALF]
+    late_ref[...] = grads[HALF:]
+    for s, cot in enumerate(cots):
+        send_ref[s] = cot[HALF:]
+
+
 def along(step):
     part = lax.rem(step, D // WIDTH)
     return part, pl.ds(pl.multiple_of(part * WIDTH, WIDTH), WIDTH)
@@ -238,20 +251,18 @@
 
 
 def backward_kernel(
-    head_ref, qkv_ref, att_ref, lse_ref, before_ref, cot_ref, cot1_ref, cot2_ref, cot3_ref, wout_ref, bias_ref,
+    qkv_ref, att_ref, lse_ref, before_ref, early_ref, valid_ref,
     dqkv_ref, kt_ref, gt_ref, dqt_ref, grad_ref, q_ref, k_ref, v_ref, g_ref,
 ):
-    cots = [cot_ref, cot1_ref, cot2_ref, cot3_ref]
-    cots = [jnp.concatenate([before_ref[s], ref[:HALF]], axis=0) for s, ref in enumerate(cots)]
-    wout = [wout_ref[:, along(head_ref[0] + (D // WIDTH - s))[1]] for s in range(D // WIDTH)]
-    grad_ref[...] = mm3(split(jnp.concatenate(cots, axis=1)), split(jnp.concatenate(wout, axis=1)), NT)
+    grad_ref[:HALF] = before_ref[...]
+    grad_ref[HALF:] = early_ref[...]
     kt_ref[...] = jnp.transpose(qkv_ref[1])
     gt_ref[...] = jnp.transpose(grad_ref[...])
     keep(q_ref, turned(qkv_ref[0] * (SCALE * LOG2E), "hhll"))
     keep(k_ref, turned(qkv_ref[1], "hlhl"))
     keep(g_ref, turned(grad_ref[...], "hhll"))
     keep(v_ref, turned(qkv_ref[2], "hlhl"))
-    bias = wide(bias_ref[...])
+    bias = wide(column(jnp.where(valid_ref[...] > 0, 0.0, -jnp.inf)))
     dqkv_ref[1] = jnp.zeros((PATCH, WIDTH), F32)
     dqkv_ref[2] = jnp.zeros((PATCH, WIDTH), F32)
 
@@ -355,30 +366,34 @@
         rows = message.shape[0]
         return swap(message.reshape(rows, 1, WIDTH), CURVE).reshape(rows, WIDTH)
 
-    message, index = call(
-        functools.partial(sort_kernel, each), [of(PATCH + peers, WIDTH), of(1, PATCH)],
-        destination.reshape(1, PATCH), features,
-    )
+    index, lists = call(
+        functools.partial(index_kernel, each), [of(1, PATCH), of(peers, WIDTH)], destination.reshape(1, PATCH)
+    )
+    (message,) = call(functools.partial(sort_kernel, each), [of(PATCH + peers, WIDTH)], index, lists, features)
     arrived = exchange(message)
     cots = [cotangent] + [ahead(cotangent, s) for s in (1, 2, 3)]
     win = jnp.transpose(input_proj, (1, 0, 2))
     valid = jnp.concatenate([lax.ppermute(real_points[HALF:], CURVE, up), real_points[:HALF]], axis=0)
     valid = valid.reshape(1, PATCH)
-    low, high, position, bias = call(
+    low, high, position = call(
         functools.partial(place_kernel, each),
-        [of(HALF, WIDTH), of(HALF, WIDTH), of(1, PATCH), of(PATCH, WIDTH)], *cots[1:], arrived, valid, held=3,
-    )
-    before = lax.ppermute(jnp.stack([c[HALF:] for c in cots]), CURVE, up)
+        [of(HALF, WIDTH), of(HALF, WIDTH), of(1, PATCH)], *cots[1:], arrived, held=3,
+    )
+    grad_early, grad_late, cot_late = call(
+        cot_kernel, [of(HALF, WIDTH), of(HALF, WIDTH), of(heads, HALF, WIDTH)], head, *cots, output_proj, scalars=1,
+    )
+    grad_before = lax.ppermute(grad_late, CURVE, up)
+    before = lax.ppermute(cot_late, CURVE, up)
     x = jnp.concatenate([lax.ppermute(high, CURVE, up), low], axis=0)
     x = jnp.broadcast_to(x[None], (D // WIDTH, PATCH, WIDTH))
     x = swap(x.reshape(-1, WIDTH), "head").reshape(D // WIDTH, PATCH, WIDTH)
     qkv, attended, lse = call(
         forward_kernel,
         [of(3, PATCH, WIDTH), of(WIDTH, PATCH), of(HERE, PATCH)],
-        x, win, bias, scratch=[(WIDTH, PATCH)] + [(HERE, PATCH, WIDTH)] * 2, room=24,
+        x, win, valid, scratch=[(WIDTH, PATCH)] + [(HERE, PATCH, WIDTH)] * 2, room=24,
     )
     (dqkv,) = call(
-        backward_kernel, [of(3, PATCH, WIDTH)], head, qkv, attended, lse, before, *cots, output_proj, bias, scalars=1,
+        backward_kernel, [of(3, PATCH, WIDTH)], qkv, attended, lse, grad_before, grad_early, valid,
         scratch=[(WIDTH, PATCH)] * 3 + [(PATCH, WIDTH)] + [(HERE, PATCH, WIDTH)] * 4, room=24,
     )
     dx, done = call(
@@ -412,7 +427,6 @@
     grad_inproj, grad_outproj = call(
         finish_kernel, [of(3, D, WIDTH), of(WIDTH, D)],
         core, sums, lax.ppermute(sums, "core", [(0, 1), (1, 0)]), scalars=1,
-        scratch=[(D // WIDTH, WIDTH, WIDTH)],
     )
     return (branch_out, grad_features, jnp.transpose(grad_inproj, (1, 0, 2)), grad_outproj)
 

time: 198 us -> 195 us (0.985)
  starting transfers between devices: 111 us -> 106 us
  waiting for transfers between devices: 50 us -> 54.2 us
    ppermute x6, waiting for transfers between devices: 17.2 us -> 22.3 us  [ahead(): lax.ppermute(x, 'head', [(i, (i + step) % heads) for i in range(heads)])]
    ppermute x1, starting transfers between devices: 7.76 us -> 4 us  [shards(): sums = keep + lax.ppermute(send, 'core', [(0, 1), (1, 0)])]
    unnamed x42 -> x44, local copies, waits for them, and re-layouts: 10.2 us -> 8.54 us
    ppermute x1 -> x2, starting transfers between devices: 4.8 us -> 5.93 us  [the longest x1 4.02 us: shards(): before = lax.ppermute(cot_late, CURVE, up)]
    pallas_call x13 -> x15, Pallas kernels: 20.5 us -> 21.2 us  [call(): pl.pallas_call(kernel, out_shape=tuple((jax.ShapeDtypeStruct(o, F32) for...]
  transfers between devices with their start and end apart: 19 -> 20, of which waited for: 16 -> 16; matrix products, arithmetic and copies ran while one was open for 1% -> 1% of each run, Pallas kernels for 3% -> 8%
where the time goes in v7:
time: 195 us; the launch traced here: 194 us
  starting transfers between devices  106 us (54%)
  waiting for transfers between devices  54.2 us (28%)
  Pallas kernels  21.2 us (11%)
  local copies, waits for them, and re-layouts  9.65 us (5%)
    all_to_all x6, starting transfers between devices, swap(): return lax.all_to_all(x, axis, split_axis=0, concat_axis=0, tiled=True)  58.6 us
    ppermute x6, waiting for transfers between devices, ahead(): lax.ppermute(x, 'head', [(i, (i + step) % heads) for i in range(heads)])  22.3 us
    pallas_call x15, Pallas kernels, call(): pl.pallas_call(kernel, out_shape=tuple((jax.ShapeDtypeStruct(o, F32) for...  21.2 us
    ppermute x6, starting transfers between devices, ahead(): lax.ppermute(x, 'head', [(i, (i + step) % heads) for i in range(heads)])  17.9 us
    all_to_all x6, waiting for transfers between devices, swap(): return lax.all_to_all(x, axis, split_axis=0, concat_axis=0, tiled=True)  16.2 us
    unnamed x44, local copies, waits for them, and re-layouts  8.54 us
    ppermute x1, waiting for transfers between devices, shards(): lax.ppermute(out_early, CURVE, down)  6.13 us
    ppermute x1, waiting for transfers between devices, shards(): lax.ppermute(dx_early, CURVE, down)  5.84 us
  transfers between devices with their start and end apart: 20, of which 16 were waited for; matrix products, arithmetic and copies ran while one was open for 1% of the time, Pallas kernels for 8%

profile of v7, /device:TPU:1, one launch (start us, length us, event | category | flops | bytes accessed | tf_op | source)
XLA Modules:
  0.0 193.8 jit_solution(16335977148394810689)
XLA Ops:
  3.6 20.5 %all-to-all-start = ((f32[640,1,128]{2,1,0:T(1,128)}), f32[640,1,128]{2,1,0:T(1,128)S(1)}, u32[]{:S(2)}, u32[]{:S(2)}) async-start(f32[640,1,128]{2,1,0:T(1,128)} %bitcast.2), calls=%async_computation | async-start | bytes 655360 | tf_op jit(solution)/shard_map/all_to_all | solution.py:350
  24.1 4.6 %collective-permute-start.2 = (f32[512,128]{1,0:T(8,128)S(1)}, f32[512,128]{1,0:T(8,128)S(1)}, u32[]{:S(2)}, u32[]{:S(2)}) collective-permute-start(f32[512,128]{1,0:T(8,128)S(1)} %copy-done.2), channel_id=1, source_target_pairs={{0,3},{1,0},{2,1},{3,2},{4,7},{5,4},{6,5},{7,6},{8,11},{9,8},{10,9... | collective-permute-start | bytes 786440 | tf_op jit(solution)/shard_map/ppermute | solution.py:363
  28.8 2.3 %collective-permute-start.1 = (f32[512,128]{1,0:T(8,128)S(1)}, f32[512,128]{1,0:T(8,128)S(1)}, u32[]{:S(2)}, u32[]{:S(2)}) collective-permute-start(f32[512,128]{1,0:T(8,128)S(1)} %copy-done.2), channel_id=1, source_target_pairs={{0,2},{1,3},{2,0},{3,1},{4,6},{5,7},{6,4},{7,5},{8,10},{9,11},{10,... | collective-permute-start | bytes 786440 | tf_op jit(solution)/shard_map/ppermute | solution.py:363
  31.0 2.6 %collective-permute-start = (f32[512,128]{1,0:T(8,128)S(1)}, f32[512,128]{1,0:T(8,128)S(1)}, u32[]{:S(2)}, u32[]{:S(2)}) collective-permute-start(f32[512,128]{1,0:T(8,128)S(1)} %copy-done.2), channel_id=1, source_target_pairs={{0,1},{1,2},{2,3},{3,0},{4,5},{5,6},{6,7},{7,4},{8,9},{9,10},{10,1... | collective-permute-start | bytes 786440 | tf_op jit(solution)/shard_map/ppermute | solution.py:363
  34.5 4.4 %collective-permute-done.1.after2_ref.cot2_ref = f32[512,128]{1,0:T(8,128)S(1)} collective-permute-done((f32[512,128]{1,0:T(8,128)S(1)}, f32[512,128]{1,0:T(8,128)S(1)}, u32[]{:S(2)}, u32[]{:S(2)}) %collective-permute-start.1) | collective-permute-done | bytes 262176 | tf_op jit(solution)/shard_map/ppermute | solution.py:363
  38.8 7.2 %collective-permute-done.after1_ref.cot1_ref = f32[512,128]{1,0:T(8,128)S(1)} collective-permute-done((f32[512,128]{1,0:T(8,128)S(1)}, f32[512,128]{1,0:T(8,128)S(1)}, u32[]{:S(2)}, u32[]{:S(2)}) %collective-permute-start) | collective-permute-done | bytes 262176 | tf_op jit(solution)/shard_map/ppermute | solution.py:363
  47.8 4.2 %collective-permute-start.3 = (f32[256,128]{1,0:T(8,128)S(1)}, f32[256,128]{1,0:T(8,128)S(1)}, u32[]{:S(2)}, u32[]{:S(2)}) collective-permute-start(f32[256,128]{1,0:T(8,128)S(1)} %get-tuple-element.39), channel_id=1, source_target_pairs={{0,4},{4,8},{8,12},{12,16},{16,20},{20,24},{24,28},{28,32},{32,36}... | collective-permute-start | bytes 393224 | tf_op jit(solution)/shard_map/ppermute | solution.py:387
  55.0 4.3 %all-to-all-start.1 = ((f32[4,512,128]{2,1,0:T(8,128)}), f32[4,512,128]{2,1,0:T(8,128)S(1)}, u32[]{:S(2)}, u32[]{:S(2)}) async-start(f32[4,512,128]{2,1,0:T(8,128)} %broadcast_in_dim.2), calls=%async_computation.1 | async-start | bytes 2097152 | tf_op jit(solution)/shard_map/all_to_all | solution.py:350
  59.3 4.6 %collective-permute-start.4 = (s32[256]{0:T(256)S(1)}, s32[256]{0:T(256)S(1)}, u32[]{:S(2)}, u32[]{:S(2)}) collective-permute-start(s32[256]{0:T(256)S(1)} %get-tuple-element.68), channel_id=1, source_target_pairs={{0,4},{4,8},{8,12},{12,16},{16,20},{20,24},{24,28},{28,32},{32,36}... | collective-permute-start | bytes 3080 | tf_op jit(solution)/shard_map/ppermute | solution.py:376
  69.1 4.0 %collective-permute-start.6 = (f32[4,256,128]{2,1,0:T(8,128)S(1)}, f32[4,256,128]{2,1,0:T(8,128)S(1)}, u32[]{:S(2)}, u32[]{:S(2)}) collective-permute-start(f32[4,256,128]{2,1,0:T(8,128)S(1)} %get-tuple-element.48), channel_id=1, source_target_pairs={{0,4},{4,8},{8,12},{12,16},{16,20},{20,24},{24,28},{28,32},{32,36}... | collective-permute-start | bytes 1572872 | tf_op jit(solution)/shard_map/ppermute | solution.py:386
  73.2 3.7 %shard_map.96 = (f32[3,512,128]{2,1,0:T(8,128)S(1)}, f32[128,512]{1,0:T(8,128)S(1)}, f32[4,512]{1,0:T(4,128)S(1)}) custom-call(f32[4,512,128]{2,1,0:T(8,128)S(1)} %all-to-all-done.1.x_ref, f32[3,512,128]{2,1,0:T(8,128)S(1)} %bitcast.19, s32[1,512]{1,0:T(1,128)S(1)} %bitcast.17), custom_call_target="tpu_custom_call" | custom-call | flops 1000000000 | bytes 2893824 | tf_op jit(solution)/shard_map/pallas_call | solution.py:331
  76.9 4.9 %shard_map.98.dqkv_ref = f32[3,512,128]{2,1,0:T(8,128)S(1)} custom-call(f32[3,512,128]{2,1,0:T(8,128)S(1)} %get-tuple-element.41.qkv_ref, f32[128,512]{1,0:T(8,128)S(1)} %get-tuple-element.42.att_ref, f32[4,512]{1,0:T(4,128)S(1)} %get-tuple-element.43.lse_ref, f32[256,128]{1,0:T(8,128)S(1)} %collective-permute-done.5.before_ref, f32[256,128]{1,0:T(8,128)S(1)} %copy-done.20, ...), custom_call_target="tpu_custom_call" | custom-call | flops 1000000000 | bytes 2107392 | tf_op jit(solution)/shard_map/pallas_call | solution.py:331
  81.8 2.4 %shard_map.99 = (f32[4,512,128]{2,1,0:T(8,128)}, f32[8,128]{1,0:T(8,128)S(1)}) custom-call(f32[3,512,128]{2,1,0:T(8,128)S(1)} %shard_map.98.dqkv_ref, f32[3,512,128]{2,1,0:T(8,128)S(1)} %bitcast.20), custom_call_target="tpu_custom_call" | custom-call | flops 1000000000 | bytes 2625536 | tf_op jit(solution)/shard_map/pallas_call | solution.py:331
  84.3 4.5 %all-to-all-start.2 = ((f32[4,512,128]{2,1,0:T(8,128)}), f32[4,512,128]{2,1,0:T(8,128)S(1)}, u32[]{:S(2)}, u32[]{:S(2)}) async-start(f32[4,512,128]{2,1,0:T(8,128)} %get-tuple-element.46), calls=%async_computation.2 | async-start | bytes 2097152 | tf_op jit(solution)/shard_map/all_to_all | solution.py:350
  94.9 4.0 %collective-permute-start.7 = (f32[16,64,128]{2,1,0:T(8,128)S(1)}, f32[16,64,128]{2,1,0:T(8,128)S(1)}, u32[]{:S(2)}, u32[]{:S(2)}) collective-permute-start(f32[16,64,128]{2,1,0:T(8,128)S(1)} %get-tuple-element.51), channel_id=1, source_target_pairs={{0,4},{4,0},{1,5},{5,1},{2,6},{6,2},{3,7},{7,3},{8,12},{12,8},{9,1... | collective-permute-start | bytes 1572872 | tf_op jit(solution)/shard_map/ppermute | solution.py:410
  101.9 9.4 %all-to-all-start.3 = ((f32[16,64,128]{2,1,0:T(8,128)}), f32[16,64,128]{2,1,0:T(8,128)S(1)}, u32[]{:S(2)}, u32[]{:S(2)}) async-start(f32[16,64,128]{2,1,0:T(8,128)} %add.3), calls=%async_computation.3 | async-start | bytes 1048576 | tf_op jit(solution)/shard_map/all_to_all | solution.py:350
  111.3 3.2 %collective-permute-start.8 = (f32[256,128]{1,0:T(8,128)S(1)}, f32[256,128]{1,0:T(8,128)S(1)}, u32[]{:S(2)}, u32[]{:S(2)}) collective-permute-start(f32[256,128]{1,0:T(8,128)S(1)} %get-tuple-element.53), channel_id=1, source_target_pairs={{4,0},{8,4},{12,8},{16,12},{20,16},{24,20},{28,24},{32,28},{36,32}... | collective-permute-start | bytes 393224 | tf_op jit(solution)/shard_map/ppermute | solution.py:415
  114.5 5.8 %collective-permute-done.8.high_ref = f32[256,128]{1,0:T(8,128)S(1)} collective-permute-done((f32[256,128]{1,0:T(8,128)S(1)}, f32[256,128]{1,0:T(8,128)S(1)}, u32[]{:S(2)}, u32[]{:S(2)}) %collective-permute-start.8) | collective-permute-done | bytes 131104 | tf_op jit(solution)/shard_map/ppermute | solution.py:415
  120.4 4.4 %all-to-all-done.3.sums_ref = f32[16,64,128]{2,1,0:T(8,128)S(1)} async-done(((f32[16,64,128]{2,1,0:T(8,128)}), f32[16,64,128]{2,1,0:T(8,128)S(1)}, u32[]{:S(2)}, u32[]{:S(2)}) %all-to-all-start.3) | async-done | bytes 524320 | tf_op jit(solution)/shard_map/all_to_all | solution.py:350
  126.2 13.7 %all-to-all-start.4 = ((f32[768,1,128]{2,1,0:T(1,128)}), f32[768,1,128]{2,1,0:T(1,128)S(1)}, u32[]{:S(2)}, u32[]{:S(2)}) async-start(f32[768,1,128]{2,1,0:T(1,128)} %bitcast.9), calls=%async_computation.4 | async-start | bytes 786432 | tf_op jit(solution)/shard_map/all_to_all | solution.py:350
  140.5 2.2 %collective-permute-start.9 = (f32[512,128]{1,0:T(8,128)S(1)}, f32[512,128]{1,0:T(8,128)S(1)}, u32[]{:S(2)}, u32[]{:S(2)}) collective-permute-start(f32[512,128]{1,0:T(8,128)S(1)} %get-tuple-element.56), channel_id=1, source_target_pairs={{0,1},{1,2},{2,3},{3,0},{4,5},{5,6},{6,7},{7,4},{8,9},{9,10},{10,1... | collective-permute-start | bytes 786440 | tf_op jit(solution)/shard_map/ppermute | solution.py:363
  142.7 3.7 %collective-permute-start.10 = (f32[512,128]{1,0:T(8,128)S(1)}, f32[512,128]{1,0:T(8,128)S(1)}, u32[]{:S(2)}, u32[]{:S(2)}) collective-permute-start(f32[512,128]{1,0:T(8,128)S(1)} %get-tuple-element.57), channel_id=1, source_target_pairs={{0,2},{1,3},{2,0},{3,1},{4,6},{5,7},{6,4},{7,5},{8,10},{9,11},{10,... | collective-permute-start | bytes 786440 | tf_op jit(solution)/shard_map/ppermute | solution.py:363
  146.4 2.5 %collective-permute-start.11 = (f32[512,128]{1,0:T(8,128)S(1)}, f32[512,128]{1,0:T(8,128)S(1)}, u32[]{:S(2)}, u32[]{:S(2)}) collective-permute-start(f32[512,128]{1,0:T(8,128)S(1)} %get-tuple-element.58), channel_id=1, source_target_pairs={{0,3},{1,0},{2,1},{3,2},{4,7},{5,4},{6,5},{7,6},{8,11},{9,8},{10,9... | collective-permute-start | bytes 786440 | tf_op jit(solution)/shard_map/ppermute | solution.py:363
  149.0 2.2 %collective-permute-done.9.second_ref = f32[512,128]{1,0:T(8,128)S(1)} collective-permute-done((f32[512,128]{1,0:T(8,128)S(1)}, f32[512,128]{1,0:T(8,128)S(1)}, u32[]{:S(2)}, u32[]{:S(2)}) %collective-permute-start.9) | collective-permute-done | bytes 262176 | tf_op jit(solution)/shard_map/ppermute | solution.py:363
  151.1 4.5 %collective-permute-done.10.third_ref = f32[512,128]{1,0:T(8,128)S(1)} collective-permute-done((f32[512,128]{1,0:T(8,128)S(1)}, f32[512,128]{1,0:T(8,128)S(1)}, u32[]{:S(2)}, u32[]{:S(2)}) %collective-permute-start.10) | collective-permute-done | bytes 262176 | tf_op jit(solution)/shard_map/ppermute | solution.py:363
  155.6 3.3 %collective-permute-done.11.fourth_ref = f32[512,128]{1,0:T(8,128)S(1)} collective-permute-done((f32[512,128]{1,0:T(8,128)S(1)}, f32[512,128]{1,0:T(8,128)S(1)}, u32[]{:S(2)}, u32[]{:S(2)}) %collective-permute-start.11) | collective-permute-done | bytes 262176 | tf_op jit(solution)/shard_map/ppermute | solution.py:363
  159.0 6.3 %all-to-all-done.4 = f32[768,1,128]{2,1,0:T(1,128)S(1)} async-done(((f32[768,1,128]{2,1,0:T(1,128)}), f32[768,1,128]{2,1,0:T(1,128)S(1)}, u32[]{:S(2)}, u32[]{:S(2)}) %all-to-all-start.4) | async-done | bytes 393248 | tf_op jit(solution)/shard_map/all_to_all | solution.py:350
  166.2 6.1 %all-to-all-start.5 = ((f32[16,64,128]{2,1,0:T(8,128)}), f32[16,64,128]{2,1,0:T(8,128)S(1)}, u32[]{:S(2)}, u32[]{:S(2)}) async-start(f32[16,64,128]{2,1,0:T(8,128)} %shard_map.103), calls=%async_computation.5 | async-start | bytes 1048576 | tf_op jit(solution)/shard_map/all_to_all | solution.py:350
  172.4 3.0 %collective-permute-start.12 = (f32[256,128]{1,0:T(8,128)S(1)}, f32[256,128]{1,0:T(8,128)S(1)}, u32[]{:S(2)}, u32[]{:S(2)}) collective-permute-start(f32[256,128]{1,0:T(8,128)S(1)} %get-tuple-element.62), channel_id=1, source_target_pairs={{4,0},{8,4},{12,8},{16,12},{20,16},{24,20},{28,24},{32,28},{36,32}... | collective-permute-start | bytes 393224 | tf_op jit(solution)/shard_map/ppermute | solution.py:424
  175.4 6.1 %collective-permute-done.12 = f32[256,128]{1,0:T(8,128)S(1)} collective-permute-done((f32[256,128]{1,0:T(8,128)S(1)}, f32[256,128]{1,0:T(8,128)S(1)}, u32[]{:S(2)}, u32[]{:S(2)}) %collective-permute-start.12) | collective-permute-done | bytes 131104 | tf_op jit(solution)/shard_map/ppermute | solution.py:424
  182.3 3.8 %all-to-all-done.5.mine_ref = f32[16,64,128]{2,1,0:T(8,128)S(1)} async-done(((f32[16,64,128]{2,1,0:T(8,128)}), f32[16,64,128]{2,1,0:T(8,128)S(1)}, u32[]{:S(2)}, u32[]{:S(2)}) %all-to-all-start.5) | async-done | bytes 524320 | tf_op jit(solution)/shard_map/all_to_all | solution.py:350
  186.1 4.6 %collective-permute-start.13 = (f32[16,64,128]{2,1,0:T(8,128)S(1)}, f32[16,64,128]{2,1,0:T(8,128)S(1)}, u32[]{:S(2)}, u32[]{:S(2)}) collective-permute-start(f32[16,64,128]{2,1,0:T(8,128)S(1)} %all-to-all-done.5.mine_ref), channel_id=1, source_target_pairs={{0,4},{4,0},{1,5},{5,1},{2,6},{6,2},{3,7},{7,3},{8,12},{12,8},{9,1... | collective-permute-start | bytes 1572872 | tf_op jit(solution)/shard_map/ppermute | solution.py:429
  (73 shorter events, 29.4 us)
Async XLA Ops:
  3.6 20.5 %copy-start.2 = (f32[512,128]{1,0:T(8,128)S(1)}, f32[512,128]{1,0:T(8,128)}, u32[]{:S(2)}) copy-start(f32[512,128]{1,0:T(8,128)} %cot_ref.3) | copy-start | bytes 786436
  3.6 43.5 %all-to-all-start = ((f32[640,1,128]{2,1,0:T(1,128)}), f32[640,1,128]{2,1,0:T(1,128)S(1)}, u32[]{:S(2)}, u32[]{:S(2)}) async-start(f32[640,1,128]{2,1,0:T(1,128)} %bitcast.2), calls=%async_computation | async-start | bytes 655360 | tf_op jit(solution)/shard_map/all_to_all | solution.py:350
  24.1 10.3 %collective-permute-start.2 = (f32[512,128]{1,0:T(8,128)S(1)}, f32[512,128]{1,0:T(8,128)S(1)}, u32[]{:S(2)}, u32[]{:S(2)}) collective-permute-start(f32[512,128]{1,0:T(8,128)S(1)} %copy-done.2), channel_id=1, source_target_pairs={{0,3},{1,0},{2,1},{3,2},{4,7},{5,4},{6,5},{7,6},{8,11},{9,8},{10,9... | collective-permute-start | bytes 786440 | tf_op jit(solution)/shard_map/ppermute | solution.py:363
  28.8 10.1 %collective-permute-start.1 = (f32[512,128]{1,0:T(8,128)S(1)}, f32[512,128]{1,0:T(8,128)S(1)}, u32[]{:S(2)}, u32[]{:S(2)}) collective-permute-start(f32[512,128]{1,0:T(8,128)S(1)} %copy-done.2), channel_id=1, source_target_pairs={{0,2},{1,3},{2,0},{3,1},{4,6},{5,7},{6,4},{7,5},{8,10},{9,11},{10,... | collective-permute-start | bytes 786440 | tf_op jit(solution)/shard_map/ppermute | solution.py:363
  31.0 15.0 %collective-permute-start = (f32[512,128]{1,0:T(8,128)S(1)}, f32[512,128]{1,0:T(8,128)S(1)}, u32[]{:S(2)}, u32[]{:S(2)}) collective-permute-start(f32[512,128]{1,0:T(8,128)S(1)} %copy-done.2), channel_id=1, source_target_pairs={{0,1},{1,2},{2,3},{3,0},{4,5},{5,6},{6,7},{7,4},{8,9},{9,10},{10,1... | collective-permute-start | bytes 786440 | tf_op jit(solution)/shard_map/ppermute | solution.py:363
  34.4 29.5 %copy-start.5 = (f32[512,128]{1,0:T(8,128)}, f32[512,128]{1,0:T(8,128)S(1)}, u32[]{:S(2)}) copy-start(f32[512,128]{1,0:T(8,128)S(1)} %collective-permute-done.2.after3_ref.cot3_ref) | copy-start | bytes 786436
  38.8 8.9 %copy-start.7 = (f32[512,128]{1,0:T(8,128)}, f32[512,128]{1,0:T(8,128)S(1)}, u32[]{:S(2)}) copy-start(f32[512,128]{1,0:T(8,128)S(1)} %collective-permute-done.1.after2_ref.cot2_ref) | copy-start | bytes 786436
  46.0 1.7 copy-start.10
  47.8 6.1 %collective-permute-start.3 = (f32[256,128]{1,0:T(8,128)S(1)}, f32[256,128]{1,0:T(8,128)S(1)}, u32[]{:S(2)}, u32[]{:S(2)}) collective-permute-start(f32[256,128]{1,0:T(8,128)S(1)} %get-tuple-element.39), channel_id=1, source_target_pairs={{0,4},{4,8},{8,12},{12,16},{16,20},{20,24},{24,28},{28,32},{32,36}... | collective-permute-start | bytes 393224 | tf_op jit(solution)/shard_map/ppermute | solution.py:387
  55.0 4.3 %copy-start.21 = (s32[512]{0:T(512)S(1)}, s32[512]{0:T(512)}, u32[]{:S(2)}) copy-start(s32[512]{0:T(512)} %param.10) | copy-start | bytes 6148
  55.0 9.0 %copy-start.3 = (f32[128,512]{1,0:T(8,128)S(1)}, f32[128,512]{1,0:T(8,128)}, u32[]{:S(2)}) copy-start(f32[128,512]{1,0:T(8,128)} %wout_ref.3) | copy-start | bytes 786436
  55.0 18.1 %all-to-all-start.1 = ((f32[4,512,128]{2,1,0:T(8,128)}), f32[4,512,128]{2,1,0:T(8,128)S(1)}, u32[]{:S(2)}, u32[]{:S(2)}) async-start(f32[4,512,128]{2,1,0:T(8,128)} %broadcast_in_dim.2), calls=%async_computation.1 | async-start | bytes 2097152 | tf_op jit(solution)/shard_map/all_to_all | solution.py:350
  59.3 13.8 %collective-permute-start.4 = (s32[256]{0:T(256)S(1)}, s32[256]{0:T(256)S(1)}, u32[]{:S(2)}, u32[]{:S(2)}) collective-permute-start(s32[256]{0:T(256)S(1)} %get-tuple-element.68), channel_id=1, source_target_pairs={{0,4},{4,8},{8,12},{12,16},{16,20},{20,24},{24,28},{28,32},{32,36}... | collective-permute-start | bytes 3080 | tf_op jit(solution)/shard_map/ppermute | solution.py:376
  65.9 7.2 %copy-start = (f32[512,3,128]{2,0,1:T(8,128)S(1)}, f32[512,3,128]{2,0,1:T(8,128)}, u32[]{:S(2)}) copy-start(f32[512,3,128]{2,0,1:T(8,128)} %param.7) | copy-start | bytes 2359300
  67.2 9.7 %collective-permute-start.5 = (f32[256,128]{1,0:T(8,128)S(1)}, f32[256,128]{1,0:T(8,128)S(1)}, u32[]{:S(2)}, u32[]{:S(2)}) collective-permute-start(f32[256,128]{1,0:T(8,128)S(1)} %get-tuple-element.44), channel_id=1, source_target_pairs={{0,4},{4,8},{8,12},{12,16},{16,20},{20,24},{24,28},{28,32},{32,36}... | collective-permute-start | bytes 393224 | tf_op jit(solution)/shard_map/ppermute | solution.py:385
  69.1 19.7 %collective-permute-start.6 = (f32[4,256,128]{2,1,0:T(8,128)S(1)}, f32[4,256,128]{2,1,0:T(8,128)S(1)}, u32[]{:S(2)}, u32[]{:S(2)}) collective-permute-start(f32[4,256,128]{2,1,0:T(8,128)S(1)} %get-tuple-element.48), channel_id=1, source_target_pairs={{0,4},{4,8},{8,12},{12,16},{16,20},{20,24},{24,28},{28,32},{32,36}... | collective-permute-start | bytes 1572872 | tf_op jit(solution)/shard_map/ppermute | solution.py:386
  73.1 3.7 %copy-start.20 = (f32[256,128]{1,0:T(8,128)S(1)}, f32[256,128]{1,0:T(8,128)}, u32[]{:S(2)}) copy-start(f32[256,128]{1,0:T(8,128)} %copy-done.19) | copy-start | bytes 393220
  76.8 5.0 %copy-start.16 = (f32[128,512]{1,0:T(8,128)}, f32[128,512]{1,0:T(8,128)S(1)}, u32[]{:S(2)}) copy-start(f32[128,512]{1,0:T(8,128)S(1)} %get-tuple-element.42.att_ref) | copy-start | bytes 786436
  81.8 2.4 %copy-start.14 = (f32[3,512,128]{2,1,0:T(8,128)}, f32[3,512,128]{2,1,0:T(8,128)S(1)}, u32[]{:S(2)}) copy-start(f32[3,512,128]{2,1,0:T(8,128)S(1)} %shard_map.98.dqkv_ref) | copy-start | bytes 2359300
  84.3 17.5 %all-to-all-start.2 = ((f32[4,512,128]{2,1,0:T(8,128)}), f32[4,512,128]{2,1,0:T(8,128)S(1)}, u32[]{:S(2)}, u32[]{:S(2)}) async-start(f32[4,512,128]{2,1,0:T(8,128)} %get-tuple-element.46), calls=%async_computation.2 | async-start | bytes 2097152 | tf_op jit(solution)/shard_map/all_to_all | solution.py:350
  94.9 5.5 %collective-permute-start.7 = (f32[16,64,128]{2,1,0:T(8,128)S(1)}, f32[16,64,128]{2,1,0:T(8,128)S(1)}, u32[]{:S(2)}, u32[]{:S(2)}) collective-permute-start(f32[16,64,128]{2,1,0:T(8,128)S(1)} %get-tuple-element.51), channel_id=1, source_target_pairs={{0,4},{4,0},{1,5},{5,1},{2,6},{6,2},{3,7},{7,3},{8,12},{12,8},{9,1... | collective-permute-start | bytes 1572872 | tf_op jit(solution)/shard_map/ppermute | solution.py:410
  101.9 22.9 %all-to-all-start.3 = ((f32[16,64,128]{2,1,0:T(8,128)}), f32[16,64,128]{2,1,0:T(8,128)S(1)}, u32[]{:S(2)}, u32[]{:S(2)}) async-start(f32[16,64,128]{2,1,0:T(8,128)} %add.3), calls=%async_computation.3 | async-start | bytes 1048576 | tf_op jit(solution)/shard_map/all_to_all | solution.py:350
  111.3 9.1 %collective-permute-start.8 = (f32[256,128]{1,0:T(8,128)S(1)}, f32[256,128]{1,0:T(8,128)S(1)}, u32[]{:S(2)}, u32[]{:S(2)}) collective-permute-start(f32[256,128]{1,0:T(8,128)S(1)} %get-tuple-element.53), channel_id=1, source_target_pairs={{4,0},{8,4},{12,8},{16,12},{20,16},{24,20},{28,24},{32,28},{36,32}... | collective-permute-start | bytes 393224 | tf_op jit(solution)/shard_map/ppermute | solution.py:415
  126.1 13.7 %copy-start.4 = (f32[128,512]{1,0:T(8,128)S(1)}, f32[128,512]{1,0:T(8,128)}, u32[]{:S(2)}) copy-start(f32[128,512]{1,0:T(8,128)} %wout_ref.3) | copy-start | bytes 786436
  126.1 13.7 %copy-start.18 = (f32[128,512]{1,0:T(8,128)S(1)}, f32[128,512]{1,0:T(8,128)}, u32[]{:S(2)}) copy-start(f32[128,512]{1,0:T(8,128)} %copy-done.16) | copy-start | bytes 786436
  126.2 39.2 %all-to-all-start.4 = ((f32[768,1,128]{2,1,0:T(1,128)}), f32[768,1,128]{2,1,0:T(1,128)S(1)}, u32[]{:S(2)}, u32[]{:S(2)}) async-start(f32[768,1,128]{2,1,0:T(1,128)} %bitcast.9), calls=%async_computation.4 | async-start | bytes 786432 | tf_op jit(solution)/shard_map/all_to_all | solution.py:350
  140.5 10.6 %collective-permute-start.9 = (f32[512,128]{1,0:T(8,128)S(1)}, f32[512,128]{1,0:T(8,128)S(1)}, u32[]{:S(2)}, u32[]{:S(2)}) collective-permute-start(f32[512,128]{1,0:T(8,128)S(1)} %get-tuple-element.56), channel_id=1, source_target_pairs={{0,1},{1,2},{2,3},{3,0},{4,5},{5,6},{6,7},{7,4},{8,9},{9,10},{10,1... | collective-permute-start | bytes 786440 | tf_op jit(solution)/shard_map/ppermute | solution.py:363
  142.7 12.9 %collective-permute-start.10 = (f32[512,128]{1,0:T(8,128)S(1)}, f32[512,128]{1,0:T(8,128)S(1)}, u32[]{:S(2)}, u32[]{:S(2)}) collective-permute-start(f32[512,128]{1,0:T(8,128)S(1)} %get-tuple-element.57), channel_id=1, source_target_pairs={{0,2},{1,3},{2,0},{3,1},{4,6},{5,7},{6,4},{7,5},{8,10},{9,11},{10,... | collective-permute-start | bytes 786440 | tf_op jit(solution)/shard_map/ppermute | solution.py:363
  146.4 12.5 %collective-permute-start.11 = (f32[512,128]{1,0:T(8,128)S(1)}, f32[512,128]{1,0:T(8,128)S(1)}, u32[]{:S(2)}, u32[]{:S(2)}) collective-permute-start(f32[512,128]{1,0:T(8,128)S(1)} %get-tuple-element.58), channel_id=1, source_target_pairs={{0,3},{1,0},{2,1},{3,2},{4,7},{5,4},{6,5},{7,6},{8,11},{9,8},{10,9... | collective-permute-start | bytes 786440 | tf_op jit(solution)/shard_map/ppermute | solution.py:363
  166.2 19.8 %all-to-all-start.5 = ((f32[16,64,128]{2,1,0:T(8,128)}), f32[16,64,128]{2,1,0:T(8,128)S(1)}, u32[]{:S(2)}, u32[]{:S(2)}) async-start(f32[16,64,128]{2,1,0:T(8,128)} %shard_map.103), calls=%async_computation.5 | async-start | bytes 1048576 | tf_op jit(solution)/shard_map/all_to_all | solution.py:350
  172.4 9.1 %collective-permute-start.12 = (f32[256,128]{1,0:T(8,128)S(1)}, f32[256,128]{1,0:T(8,128)S(1)}, u32[]{:S(2)}, u32[]{:S(2)}) collective-permute-start(f32[256,128]{1,0:T(8,128)S(1)} %get-tuple-element.62), channel_id=1, source_target_pairs={{4,0},{8,4},{12,8},{16,12},{20,16},{24,20},{28,24},{32,28},{36,32}... | collective-permute-start | bytes 393224 | tf_op jit(solution)/shard_map/ppermute | solution.py:424
  186.1 6.1 %collective-permute-start.13 = (f32[16,64,128]{2,1,0:T(8,128)S(1)}, f32[16,64,128]{2,1,0:T(8,128)S(1)}, u32[]{:S(2)}, u32[]{:S(2)}) collective-permute-start(f32[16,64,128]{2,1,0:T(8,128)S(1)} %all-to-all-done.5.mine_ref), channel_id=1, source_target_pairs={{0,4},{4,0},{1,5},{5,1},{2,6},{6,2},{3,7},{7,3},{8,12},{12,8},{9,1... | collective-permute-start | bytes 1572872 | tf_op jit(solution)/shard_map/ppermute | solution.py:429
  (10 other events, 9.1 us)

commit v8 on v7

--- a/solution.py
+++ b/solution.py
@@ -222,13 +222,14 @@
     lax.fori_loop(0, HERE, one, 0, unroll=True)
 
 
-def cot_kernel(head_ref, cot_ref, cot1_ref, cot2_ref, cot3_ref, wout_ref, early_ref, late_ref, send_ref):
+def cot_kernel(head_ref, cot_ref, cot1_ref, cot2_ref, cot3_ref, wout_ref, early_ref, late_ref, stay_ref, send_ref):
     cots = [ref[...] for ref in (cot_ref, cot1_ref, cot2_ref, cot3_ref)]
     wout = [wout_ref[:, along(head_ref[0] + (D // WIDTH - s))[1]] for s in range(D // WIDTH)]
     grads = mm3(split(jnp.concatenate(cots, axis=1)), split(jnp.concatenate(wout, axis=1)), NT)
     early_ref[...] = grads[:HALF]
     late_ref[...] = grads[HALF:]
     for s, cot in enumerate(cots):
+        stay_ref[s] = cot[:HALF]
         send_ref[s] = cot[HALF:]
 
 
@@ -289,11 +290,10 @@
 
     lax.fori_loop(0, HERE, one, 0, unroll=True)
     dqkv_ref[0] = jnp.transpose(dqt_ref[...])
-
-
-def weights_kernel(
-    core_ref, head_ref, x_ref, dqkv_ref, att_ref, before_ref, cot_ref, cot1_ref, cot2_ref, cot3_ref, after_ref, keep_ref, send_ref
-):
+    dqkv_ref[3] = jnp.transpose(att_ref[...])
+
+
+def weights_kernel(core_ref, head_ref, x_ref, dqkv_ref, before_ref, early_ref, after_ref, keep_ref, send_ref):
     del after_ref
     second = core_ref[0] == 1
 
@@ -307,9 +307,8 @@
         grads = jnp.transpose(mm3(split(jnp.transpose(dqkv_ref[t])), x))
         for part in range(D // WIDTH):
             put(t * (D // WIDTH) + part, grads[part * WIDTH : (part + 1) * WIDTH])
-    cots = [cot_ref, cot1_ref, cot2_ref, cot3_ref]
-    cots = [jnp.concatenate([before_ref[s], ref[:HALF]], axis=0) for s, ref in enumerate(cots)]
-    grads = mm3(split(att_ref[...]), split(jnp.concatenate(cots, axis=1)))
+    cots = [jnp.concatenate([before_ref[s], early_ref[s]], axis=0) for s in range(D // WIDTH)]
+    grads = mm3(split(jnp.transpose(dqkv_ref[3])), split(jnp.concatenate(cots, axis=1)))
     for s in range(D // WIDTH):
         part = along(head_ref[0] + (D // WIDTH - s))[0]
         put(3 * (D // WIDTH) + part, grads[:, s * WIDTH : (s + 1) * WIDTH])
@@ -379,13 +378,14 @@
         functools.partial(place_kernel, each),
         [of(HALF, WIDTH), of(HALF, WIDTH), of(1, PATCH)], *cots[1:], arrived, held=3,
     )
-    grad_early, grad_late, cot_late = call(
-        cot_kernel, [of(HALF, WIDTH), of(HALF, WIDTH), of(heads, HALF, WIDTH)], head, *cots, output_proj, scalars=1,
+    grad_early, grad_late, cot_early, cot_late = call(
+        cot_kernel, [of(HALF, WIDTH)] * 2 + [of(heads, HALF, WIDTH)] * 2, head, *cots, output_proj, scalars=1,
     )
     grad_before = lax.ppermute(grad_late, CURVE, up)
     before = lax.ppermute(cot_late, CURVE, up)
     x = jnp.concatenate([lax.ppermute(high, CURVE, up), low], axis=0)
     x = jnp.broadcast_to(x[None], (D // WIDTH, PATCH, WIDTH))
+    x, grad_early = lax.optimization_barrier((x, grad_early))
     x = swap(x.reshape(-1, WIDTH), "head").reshape(D // WIDTH, PATCH, WIDTH)
     qkv, attended, lse = call(
         forward_kernel,
@@ -393,7 +393,7 @@
         x, win, valid, scratch=[(WIDTH, PATCH)] + [(HERE, PATCH, WIDTH)] * 2, room=24,
     )
     (dqkv,) = call(
-        backward_kernel, [of(3, PATCH, WIDTH)], qkv, attended, lse, grad_before, grad_early, valid,
+        backward_kernel, [of(4, PATCH, WIDTH)], qkv, attended, lse, grad_before, grad_early, valid,
         scratch=[(WIDTH, PATCH)] * 3 + [(PATCH, WIDTH)] + [(HERE, PATCH, WIDTH)] * 4, room=24,
     )
     dx, done = call(
@@ -402,7 +402,7 @@
     dx = swap(dx.reshape(-1, WIDTH), "head").reshape(D // WIDTH, PATCH, WIDTH)
     dx_early, dx_late = call(add_kernel, [of(HALF, WIDTH)] * 2, dx)
     keep, send = call(
-        weights_kernel, [of(BLOCKS, SIDE, WIDTH)] * 2, core, head, x, dqkv, attended, before, *cots, done, scalars=2
+        weights_kernel, [of(BLOCKS, SIDE, WIDTH)] * 2, core, head, x, dqkv, before, cot_early, done, scalars=2
     )
     out = call(output_kernel, [of(PATCH, WIDTH)] * heads, head, attended, output_proj, done, scalars=1)
     out = [out[0]] + [ahead(out[s], s) for s in (1, 2, 3)]

time: 195 us -> 192 us (0.985)
  starting transfers between devices: 106 us -> 113 us
  waiting for transfers between devices: 54.2 us -> 48.8 us
  local copies, waits for them, and re-layouts: 9.65 us -> 5.33 us
    ppermute x6, waiting for transfers between devices: 22.3 us -> 15.3 us  [ahead(): lax.ppermute(x, 'head', [(i, (i + step) % heads) for i in range(heads)])]
    unnamed x44 -> x28, local copies, waits for them, and re-layouts: 8.54 us -> 4.27 us
    all_to_all x6, waiting for transfers between devices: 16.2 us -> 19.5 us  [swap(): return lax.all_to_all(x, axis, split_axis=0, concat_axis=0, tiled=True)]
    ppermute x1, starting transfers between devices: 4 us -> 6.46 us  [shards(): sums = keep + lax.ppermute(send, 'core', [(0, 1), (1, 0)])]
  transfers between devices with their start and end apart: 20 -> 20, of which waited for: 16 -> 13; matrix products, arithmetic and copies ran while one was open for 1% -> 1% of each run, Pallas kernels for 8% -> 8%
where the time goes in v8:
time: 192 us; the launch traced here: 191 us
  starting transfers between devices  113 us (59%)
  waiting for transfers between devices  48.8 us (25%)
  Pallas kernels  21.3 us (11%)
  local copies, waits for them, and re-layouts  5.33 us (3%)
    all_to_all x6, starting transfers between devices, swap(): return lax.all_to_all(x, axis, split_axis=0, concat_axis=0, tiled=True)  60.5 us
    pallas_call x15, Pallas kernels, call(): pl.pallas_call(kernel, out_shape=tuple((jax.ShapeDtypeStruct(o, F32) for...  21.3 us
    ppermute x6, starting transfers between devices, ahead(): lax.ppermute(x, 'head', [(i, (i + step) % heads) for i in range(heads)])  19.7 us
    all_to_all x6, waiting for transfers between devices, swap(): return lax.all_to_all(x, axis, split_axis=0, concat_axis=0, tiled=True)  19.5 us
    ppermute x6, waiting for transfers between devices, ahead(): lax.ppermute(x, 'head', [(i, (i + step) % heads) for i in range(heads)])  15.3 us
    ppermute x1, starting transfers between devices, shards(): sums = keep + lax.ppermute(send, 'core', [(0, 1), (1, 0)])  6.46 us
    ppermute x1, waiting for transfers between devices, shards(): lax.ppermute(out_early, CURVE, down)  6.13 us
    ppermute x1, waiting for transfers between devices, shards(): lax.ppermute(dx_early, CURVE, down)  5.73 us
  transfers between devices with their start and end apart: 20, of which 13 were waited for; matrix products, arithmetic and copies ran while one was open for 1% of the time, Pallas kernels for 8%

profile of v8, /device:TPU:1, one launch (start us, length us, event | category | flops | bytes accessed | tf_op | source)
XLA Modules:
  0.0 190.9 jit_solution(9957866203636369522)
XLA Ops:
  3.6 20.5 %all-to-all-start = ((f32[640,1,128]{2,1,0:T(1,128)}), f32[640,1,128]{2,1,0:T(1,128)S(1)}, u32[]{:S(2)}, u32[]{:S(2)}) async-start(f32[640,1,128]{2,1,0:T(1,128)} %bitcast.2), calls=%async_computation | async-start | bytes 655360 | tf_op jit(solution)/shard_map/all_to_all | solution.py:349
  24.1 4.8 %collective-permute-start.1 = (f32[512,128]{1,0:T(8,128)S(1)}, f32[512,128]{1,0:T(8,128)S(1)}, u32[]{:S(2)}, u32[]{:S(2)}) collective-permute-start(f32[512,128]{1,0:T(8,128)S(1)} %copy-done.2), channel_id=1, source_target_pairs={{0,2},{1,3},{2,0},{3,1},{4,6},{5,7},{6,4},{7,5},{8,10},{9,11},{10,... | collective-permute-start | bytes 786440 | tf_op jit(solution)/shard_map/ppermute | solution.py:362
  29.0 2.3 %collective-permute-start = (f32[512,128]{1,0:T(8,128)S(1)}, f32[512,128]{1,0:T(8,128)S(1)}, u32[]{:S(2)}, u32[]{:S(2)}) collective-permute-start(f32[512,128]{1,0:T(8,128)S(1)} %copy-done.2), channel_id=1, source_target_pairs={{0,1},{1,2},{2,3},{3,0},{4,5},{5,6},{6,7},{7,4},{8,9},{9,10},{10,1... | collective-permute-start | bytes 786440 | tf_op jit(solution)/shard_map/ppermute | solution.py:362
  31.3 4.2 %collective-permute-start.2 = (f32[512,128]{1,0:T(8,128)S(1)}, f32[512,128]{1,0:T(8,128)S(1)}, u32[]{:S(2)}, u32[]{:S(2)}) collective-permute-start(f32[512,128]{1,0:T(8,128)S(1)} %copy-done.2), channel_id=1, source_target_pairs={{0,3},{1,0},{2,1},{3,2},{4,7},{5,4},{6,5},{7,6},{8,11},{9,8},{10,9... | collective-permute-start | bytes 786440 | tf_op jit(solution)/shard_map/ppermute | solution.py:362
  35.5 5.3 %collective-permute-done.after1_ref.cot1_ref = f32[512,128]{1,0:T(8,128)S(1)} collective-permute-done((f32[512,128]{1,0:T(8,128)S(1)}, f32[512,128]{1,0:T(8,128)S(1)}, u32[]{:S(2)}, u32[]{:S(2)}) %collective-permute-start) | collective-permute-done | bytes 262176 | tf_op jit(solution)/shard_map/ppermute | solution.py:362
  40.8 6.4 %all-to-all-done = f32[640,1,128]{2,1,0:T(1,128)S(1)} async-done(((f32[640,1,128]{2,1,0:T(1,128)}), f32[640,1,128]{2,1,0:T(1,128)S(1)}, u32[]{:S(2)}, u32[]{:S(2)}) %all-to-all-start) | async-done | bytes 327712 | tf_op jit(solution)/shard_map/all_to_all | solution.py:349
  47.8 4.2 %collective-permute-start.3 = (f32[256,128]{1,0:T(8,128)S(1)}, f32[256,128]{1,0:T(8,128)S(1)}, u32[]{:S(2)}, u32[]{:S(2)}) collective-permute-start(f32[256,128]{1,0:T(8,128)S(1)} %get-tuple-element.42), channel_id=1, source_target_pairs={{0,4},{4,8},{8,12},{12,16},{16,20},{20,24},{24,28},{28,32},{32,36}... | collective-permute-start | bytes 393224 | tf_op jit(solution)/shard_map/ppermute | solution.py:386
  55.1 4.3 %all-to-all-start.1 = ((f32[4,512,128]{2,1,0:T(8,128)}), f32[4,512,128]{2,1,0:T(8,128)S(1)}, u32[]{:S(2)}, u32[]{:S(2)}) async-start(f32[4,512,128]{2,1,0:T(8,128)} %broadcast_in_dim.2), calls=%async_computation.1 | async-start | bytes 2097152 | tf_op jit(solution)/shard_map/all_to_all | solution.py:349
  59.4 4.5 %collective-permute-start.4 = (s32[256]{0:T(256)S(1)}, s32[256]{0:T(256)S(1)}, u32[]{:S(2)}, u32[]{:S(2)}) collective-permute-start(s32[256]{0:T(256)S(1)} %get-tuple-element.74), channel_id=1, source_target_pairs={{0,4},{4,8},{8,12},{12,16},{16,20},{20,24},{24,28},{28,32},{32,36}... | collective-permute-start | bytes 3080 | tf_op jit(solution)/shard_map/ppermute | solution.py:375
  65.8 4.0 %collective-permute-start.6 = (f32[4,256,128]{2,1,0:T(8,128)S(1)}, f32[4,256,128]{2,1,0:T(8,128)S(1)}, u32[]{:S(2)}, u32[]{:S(2)}) collective-permute-start(f32[4,256,128]{2,1,0:T(8,128)S(1)} %get-tuple-element.53), channel_id=1, source_target_pairs={{0,4},{4,8},{8,12},{12,16},{16,20},{20,24},{24,28},{28,32},{32,36}... | collective-permute-start | bytes 1572872 | tf_op jit(solution)/shard_map/ppermute | solution.py:385
  70.0 3.7 %shard_map.97 = (f32[3,512,128]{2,1,0:T(8,128)S(1)}, f32[128,512]{1,0:T(8,128)S(1)}, f32[4,512]{1,0:T(4,128)S(1)}) custom-call(f32[4,512,128]{2,1,0:T(8,128)S(1)} %all-to-all-done.1.x_ref, f32[3,512,128]{2,1,0:T(8,128)S(1)} %bitcast.19, s32[1,512]{1,0:T(1,128)S(1)} %bitcast.17), custom_call_target="tpu_custom_call" | custom-call | flops 1000000000 | bytes 2893824 | tf_op jit(solution)/shard_map/pallas_call | solution.py:330
  73.7 5.0 %shard_map.98.dqkv_ref = f32[4,512,128]{2,1,0:T(8,128)S(1)} custom-call(f32[3,512,128]{2,1,0:T(8,128)S(1)} %get-tuple-element.46.qkv_ref, f32[128,512]{1,0:T(8,128)S(1)} %get-tuple-element.47.att_ref, f32[4,512]{1,0:T(4,128)S(1)} %get-tuple-element.48.lse_ref, f32[256,128]{1,0:T(8,128)S(1)} %collective-permute-done.5.before_ref, f32[256,128]{1,0:T(8,128)S(1)} %copy-done.12, ...), custom_call_target="tpu_custom_call" | custom-call | flops 1000000000 | bytes 2369536 | tf_op jit(solution)/shard_map/pallas_call | solution.py:330
  78.7 2.4 %shard_map.99 = (f32[4,512,128]{2,1,0:T(8,128)}, f32[8,128]{1,0:T(8,128)S(1)}) custom-call(f32[4,512,128]{2,1,0:T(8,128)S(1)} %shard_map.98.dqkv_ref, f32[3,512,128]{2,1,0:T(8,128)S(1)} %bitcast.20), custom_call_target="tpu_custom_call" | custom-call | flops 1000000000 | bytes 2887680 | tf_op jit(solution)/shard_map/pallas_call | solution.py:330
  81.1 4.5 %all-to-all-start.2 = ((f32[4,512,128]{2,1,0:T(8,128)}), f32[4,512,128]{2,1,0:T(8,128)S(1)}, u32[]{:S(2)}, u32[]{:S(2)}) async-start(f32[4,512,128]{2,1,0:T(8,128)} %get-tuple-element.51), calls=%async_computation.2 | async-start | bytes 2097152 | tf_op jit(solution)/shard_map/all_to_all | solution.py:349
  89.1 6.5 %collective-permute-start.7 = (f32[16,64,128]{2,1,0:T(8,128)S(1)}, f32[16,64,128]{2,1,0:T(8,128)S(1)}, u32[]{:S(2)}, u32[]{:S(2)}) collective-permute-start(f32[16,64,128]{2,1,0:T(8,128)S(1)} %get-tuple-element.57), channel_id=1, source_target_pairs={{0,4},{4,0},{1,5},{5,1},{2,6},{6,2},{3,7},{7,3},{8,12},{12,8},{9,1... | collective-permute-start | bytes 1572872 | tf_op jit(solution)/shard_map/ppermute | solution.py:410
  98.0 10.8 %all-to-all-start.3 = ((f32[16,64,128]{2,1,0:T(8,128)}), f32[16,64,128]{2,1,0:T(8,128)S(1)}, u32[]{:S(2)}, u32[]{:S(2)}) async-start(f32[16,64,128]{2,1,0:T(8,128)} %add.3), calls=%async_computation.3 | async-start | bytes 1048576 | tf_op jit(solution)/shard_map/all_to_all | solution.py:349
  108.8 4.1 %collective-permute-start.8 = (f32[256,128]{1,0:T(8,128)S(1)}, f32[256,128]{1,0:T(8,128)S(1)}, u32[]{:S(2)}, u32[]{:S(2)}) collective-permute-start(f32[256,128]{1,0:T(8,128)S(1)} %get-tuple-element.59), channel_id=1, source_target_pairs={{4,0},{8,4},{12,8},{16,12},{20,16},{24,20},{28,24},{32,28},{36,32}... | collective-permute-start | bytes 393224 | tf_op jit(solution)/shard_map/ppermute | solution.py:415
  112.9 5.7 %collective-permute-done.8.high_ref = f32[256,128]{1,0:T(8,128)S(1)} collective-permute-done((f32[256,128]{1,0:T(8,128)S(1)}, f32[256,128]{1,0:T(8,128)S(1)}, u32[]{:S(2)}, u32[]{:S(2)}) %collective-permute-start.8) | collective-permute-done | bytes 131104 | tf_op jit(solution)/shard_map/ppermute | solution.py:415
  118.6 2.9 %all-to-all-done.3.sums_ref = f32[16,64,128]{2,1,0:T(8,128)S(1)} async-done(((f32[16,64,128]{2,1,0:T(8,128)}), f32[16,64,128]{2,1,0:T(8,128)S(1)}, u32[]{:S(2)}, u32[]{:S(2)}) %all-to-all-start.3) | async-done | bytes 524320 | tf_op jit(solution)/shard_map/all_to_all | solution.py:349
  122.9 14.2 %all-to-all-start.4 = ((f32[768,1,128]{2,1,0:T(1,128)}), f32[768,1,128]{2,1,0:T(1,128)S(1)}, u32[]{:S(2)}, u32[]{:S(2)}) async-start(f32[768,1,128]{2,1,0:T(1,128)} %bitcast.9), calls=%async_computation.4 | async-start | bytes 786432 | tf_op jit(solution)/shard_map/all_to_all | solution.py:349
  137.7 2.2 %collective-permute-start.9 = (f32[512,128]{1,0:T(8,128)S(1)}, f32[512,128]{1,0:T(8,128)S(1)}, u32[]{:S(2)}, u32[]{:S(2)}) collective-permute-start(f32[512,128]{1,0:T(8,128)S(1)} %get-tuple-element.62), channel_id=1, source_target_pairs={{0,1},{1,2},{2,3},{3,0},{4,5},{5,6},{6,7},{7,4},{8,9},{9,10},{10,1... | collective-permute-start | bytes 786440 | tf_op jit(solution)/shard_map/ppermute | solution.py:362
  139.9 3.7 %collective-permute-start.10 = (f32[512,128]{1,0:T(8,128)S(1)}, f32[512,128]{1,0:T(8,128)S(1)}, u32[]{:S(2)}, u32[]{:S(2)}) collective-permute-start(f32[512,128]{1,0:T(8,128)S(1)} %get-tuple-element.63), channel_id=1, source_target_pairs={{0,2},{1,3},{2,0},{3,1},{4,6},{5,7},{6,4},{7,5},{8,10},{9,11},{10,... | collective-permute-start | bytes 786440 | tf_op jit(solution)/shard_map/ppermute | solution.py:362
  143.6 2.5 %collective-permute-start.11 = (f32[512,128]{1,0:T(8,128)S(1)}, f32[512,128]{1,0:T(8,128)S(1)}, u32[]{:S(2)}, u32[]{:S(2)}) collective-permute-start(f32[512,128]{1,0:T(8,128)S(1)} %get-tuple-element.64), channel_id=1, source_target_pairs={{0,3},{1,0},{2,1},{3,2},{4,7},{5,4},{6,5},{7,6},{8,11},{9,8},{10,9... | collective-permute-start | bytes 786440 | tf_op jit(solution)/shard_map/ppermute | solution.py:362
  146.1 2.2 %collective-permute-done.9.second_ref = f32[512,128]{1,0:T(8,128)S(1)} collective-permute-done((f32[512,128]{1,0:T(8,128)S(1)}, f32[512,128]{1,0:T(8,128)S(1)}, u32[]{:S(2)}, u32[]{:S(2)}) %collective-permute-start.9) | collective-permute-done | bytes 262176 | tf_op jit(solution)/shard_map/ppermute | solution.py:362
  148.3 4.5 %collective-permute-done.10.third_ref = f32[512,128]{1,0:T(8,128)S(1)} collective-permute-done((f32[512,128]{1,0:T(8,128)S(1)}, f32[512,128]{1,0:T(8,128)S(1)}, u32[]{:S(2)}, u32[]{:S(2)}) %collective-permute-start.10) | collective-permute-done | bytes 262176 | tf_op jit(solution)/shard_map/ppermute | solution.py:362
  152.8 3.3 %collective-permute-done.11.fourth_ref = f32[512,128]{1,0:T(8,128)S(1)} collective-permute-done((f32[512,128]{1,0:T(8,128)S(1)}, f32[512,128]{1,0:T(8,128)S(1)}, u32[]{:S(2)}, u32[]{:S(2)}) %collective-permute-start.11) | collective-permute-done | bytes 262176 | tf_op jit(solution)/shard_map/ppermute | solution.py:362
  156.2 6.3 %all-to-all-done.4 = f32[768,1,128]{2,1,0:T(1,128)S(1)} async-done(((f32[768,1,128]{2,1,0:T(1,128)}), f32[768,1,128]{2,1,0:T(1,128)S(1)}, u32[]{:S(2)}, u32[]{:S(2)}) %all-to-all-start.4) | async-done | bytes 393248 | tf_op jit(solution)/shard_map/all_to_all | solution.py:349
  163.4 6.1 %all-to-all-start.5 = ((f32[16,64,128]{2,1,0:T(8,128)}), f32[16,64,128]{2,1,0:T(8,128)S(1)}, u32[]{:S(2)}, u32[]{:S(2)}) async-start(f32[16,64,128]{2,1,0:T(8,128)} %shard_map.103), calls=%async_computation.5 | async-start | bytes 1048576 | tf_op jit(solution)/shard_map/all_to_all | solution.py:349
  169.6 3.0 %collective-permute-start.12 = (f32[256,128]{1,0:T(8,128)S(1)}, f32[256,128]{1,0:T(8,128)S(1)}, u32[]{:S(2)}, u32[]{:S(2)}) collective-permute-start(f32[256,128]{1,0:T(8,128)S(1)} %get-tuple-element.68), channel_id=1, source_target_pairs={{4,0},{8,4},{12,8},{16,12},{20,16},{24,20},{28,24},{32,28},{36,32}... | collective-permute-start | bytes 393224 | tf_op jit(solution)/shard_map/ppermute | solution.py:424
  172.6 6.1 %collective-permute-done.12 = f32[256,128]{1,0:T(8,128)S(1)} collective-permute-done((f32[256,128]{1,0:T(8,128)S(1)}, f32[256,128]{1,0:T(8,128)S(1)}, u32[]{:S(2)}, u32[]{:S(2)}) %collective-permute-start.12) | collective-permute-done | bytes 131104 | tf_op jit(solution)/shard_map/ppermute | solution.py:424
  179.4 3.8 %all-to-all-done.5.mine_ref = f32[16,64,128]{2,1,0:T(8,128)S(1)} async-done(((f32[16,64,128]{2,1,0:T(8,128)}), f32[16,64,128]{2,1,0:T(8,128)S(1)}, u32[]{:S(2)}, u32[]{:S(2)}) %all-to-all-start.5) | async-done | bytes 524320 | tf_op jit(solution)/shard_map/all_to_all | solution.py:349
  183.3 4.6 %collective-permute-start.13 = (f32[16,64,128]{2,1,0:T(8,128)S(1)}, f32[16,64,128]{2,1,0:T(8,128)S(1)}, u32[]{:S(2)}, u32[]{:S(2)}) collective-permute-start(f32[16,64,128]{2,1,0:T(8,128)S(1)} %all-to-all-done.5.mine_ref), channel_id=1, source_target_pairs={{0,4},{4,0},{1,5},{5,1},{2,6},{6,2},{3,7},{7,3},{8,12},{12,8},{9,1... | collective-permute-start | bytes 1572872 | tf_op jit(solution)/shard_map/ppermute | solution.py:429
  (57 shorter events, 21.3 us)
Async XLA Ops:
  1.3 0.9 copy-start.1
  3.6 20.5 %copy-start.2 = (f32[512,128]{1,0:T(8,128)S(1)}, f32[512,128]{1,0:T(8,128)}, u32[]{:S(2)}) copy-start(f32[512,128]{1,0:T(8,128)} %cot_ref.1) | copy-start | bytes 786436
  3.6 43.5 %all-to-all-start = ((f32[640,1,128]{2,1,0:T(1,128)}), f32[640,1,128]{2,1,0:T(1,128)S(1)}, u32[]{:S(2)}, u32[]{:S(2)}) async-start(f32[640,1,128]{2,1,0:T(1,128)} %bitcast.2), calls=%async_computation | async-start | bytes 655360 | tf_op jit(solution)/shard_map/all_to_all | solution.py:349
  24.1 11.3 %collective-permute-start.1 = (f32[512,128]{1,0:T(8,128)S(1)}, f32[512,128]{1,0:T(8,128)S(1)}, u32[]{:S(2)}, u32[]{:S(2)}) collective-permute-start(f32[512,128]{1,0:T(8,128)S(1)} %copy-done.2), channel_id=1, source_target_pairs={{0,2},{1,3},{2,0},{3,1},{4,6},{5,7},{6,4},{7,5},{8,10},{9,11},{10,... | collective-permute-start | bytes 786440 | tf_op jit(solution)/shard_map/ppermute | solution.py:362
  29.0 11.8 %collective-permute-start = (f32[512,128]{1,0:T(8,128)S(1)}, f32[512,128]{1,0:T(8,128)S(1)}, u32[]{:S(2)}, u32[]{:S(2)}) collective-permute-start(f32[512,128]{1,0:T(8,128)S(1)} %copy-done.2), channel_id=1, source_target_pairs={{0,1},{1,2},{2,3},{3,0},{4,5},{5,6},{6,7},{7,4},{8,9},{9,10},{10,1... | collective-permute-start | bytes 786440 | tf_op jit(solution)/shard_map/ppermute | solution.py:362
  31.3 9.5 %collective-permute-start.2 = (f32[512,128]{1,0:T(8,128)S(1)}, f32[512,128]{1,0:T(8,128)S(1)}, u32[]{:S(2)}, u32[]{:S(2)}) collective-permute-start(f32[512,128]{1,0:T(8,128)S(1)} %copy-done.2), channel_id=1, source_target_pairs={{0,3},{1,0},{2,1},{3,2},{4,7},{5,4},{6,5},{7,6},{8,11},{9,8},{10,9... | collective-permute-start | bytes 786440 | tf_op jit(solution)/shard_map/ppermute | solution.py:362
  47.1 4.8 %copy-start.3 = (f32[128,512]{1,0:T(8,128)S(1)}, f32[128,512]{1,0:T(8,128)}, u32[]{:S(2)}) copy-start(f32[128,512]{1,0:T(8,128)} %wout_ref.3) | copy-start | bytes 786436
  47.8 6.1 %collective-permute-start.3 = (f32[256,128]{1,0:T(8,128)S(1)}, f32[256,128]{1,0:T(8,128)S(1)}, u32[]{:S(2)}, u32[]{:S(2)}) collective-permute-start(f32[256,128]{1,0:T(8,128)S(1)} %get-tuple-element.42), channel_id=1, source_target_pairs={{0,4},{4,8},{8,12},{12,16},{16,20},{20,24},{24,28},{28,32},{32,36}... | collective-permute-start | bytes 393224 | tf_op jit(solution)/shard_map/ppermute | solution.py:386
  52.6 0.8 copy-start.7
  55.1 4.3 %copy-start.13 = (s32[512]{0:T(512)S(1)}, s32[512]{0:T(512)}, u32[]{:S(2)}) copy-start(s32[512]{0:T(512)} %param.10) | copy-start | bytes 6148
  55.1 14.8 %copy-start = (f32[512,3,128]{2,0,1:T(8,128)S(1)}, f32[512,3,128]{2,0,1:T(8,128)}, u32[]{:S(2)}) copy-start(f32[512,3,128]{2,0,1:T(8,128)} %param.7) | copy-start | bytes 2359300
  55.1 14.8 %all-to-all-start.1 = ((f32[4,512,128]{2,1,0:T(8,128)}), f32[4,512,128]{2,1,0:T(8,128)S(1)}, u32[]{:S(2)}, u32[]{:S(2)}) async-start(f32[4,512,128]{2,1,0:T(8,128)} %broadcast_in_dim.2), calls=%async_computation.1 | async-start | bytes 2097152 | tf_op jit(solution)/shard_map/all_to_all | solution.py:349
  59.4 10.5 %collective-permute-start.4 = (s32[256]{0:T(256)S(1)}, s32[256]{0:T(256)S(1)}, u32[]{:S(2)}, u32[]{:S(2)}) collective-permute-start(s32[256]{0:T(256)S(1)} %get-tuple-element.74), channel_id=1, source_target_pairs={{0,4},{4,8},{8,12},{12,16},{16,20},{20,24},{24,28},{28,32},{32,36}... | collective-permute-start | bytes 3080 | tf_op jit(solution)/shard_map/ppermute | solution.py:375
  63.9 9.7 %collective-permute-start.5 = (f32[256,128]{1,0:T(8,128)S(1)}, f32[256,128]{1,0:T(8,128)S(1)}, u32[]{:S(2)}, u32[]{:S(2)}) collective-permute-start(f32[256,128]{1,0:T(8,128)S(1)} %get-tuple-element.49), channel_id=1, source_target_pairs={{0,4},{4,8},{8,12},{12,16},{16,20},{20,24},{24,28},{28,32},{32,36}... | collective-permute-start | bytes 393224 | tf_op jit(solution)/shard_map/ppermute | solution.py:384
  65.8 19.8 %collective-permute-start.6 = (f32[4,256,128]{2,1,0:T(8,128)S(1)}, f32[4,256,128]{2,1,0:T(8,128)S(1)}, u32[]{:S(2)}, u32[]{:S(2)}) collective-permute-start(f32[4,256,128]{2,1,0:T(8,128)S(1)} %get-tuple-element.53), channel_id=1, source_target_pairs={{0,4},{4,8},{8,12},{12,16},{16,20},{20,24},{24,28},{28,32},{32,36}... | collective-permute-start | bytes 1572872 | tf_op jit(solution)/shard_map/ppermute | solution.py:385
  69.9 3.7 %copy-start.12 = (f32[256,128]{1,0:T(8,128)S(1)}, f32[256,128]{1,0:T(8,128)}, u32[]{:S(2)}) copy-start(f32[256,128]{1,0:T(8,128)} %copy-done.11) | copy-start | bytes 393220
  73.6 5.0 %copy-start.9 = (f32[128,512]{1,0:T(8,128)}, f32[128,512]{1,0:T(8,128)S(1)}, u32[]{:S(2)}) copy-start(f32[128,512]{1,0:T(8,128)S(1)} %get-tuple-element.47.att_ref) | copy-start | bytes 786436
  78.7 2.4 %copy-start.5 = (f32[4,512,128]{2,1,0:T(8,128)}, f32[4,512,128]{2,1,0:T(8,128)S(1)}, u32[]{:S(2)}) copy-start(f32[4,512,128]{2,1,0:T(8,128)S(1)} %shard_map.98.dqkv_ref) | copy-start | bytes 3145732
  81.1 16.8 %all-to-all-start.2 = ((f32[4,512,128]{2,1,0:T(8,128)}), f32[4,512,128]{2,1,0:T(8,128)S(1)}, u32[]{:S(2)}, u32[]{:S(2)}) async-start(f32[4,512,128]{2,1,0:T(8,128)} %get-tuple-element.51), calls=%async_computation.2 | async-start | bytes 2097152 | tf_op jit(solution)/shard_map/all_to_all | solution.py:349
  85.6 1.2 copy-start.6
  86.8 1.0 copy-start.8
  89.1 8.0 %collective-permute-start.7 = (f32[16,64,128]{2,1,0:T(8,128)S(1)}, f32[16,64,128]{2,1,0:T(8,128)S(1)}, u32[]{:S(2)}, u32[]{:S(2)}) collective-permute-start(f32[16,64,128]{2,1,0:T(8,128)S(1)} %get-tuple-element.57), channel_id=1, source_target_pairs={{0,4},{4,0},{1,5},{5,1},{2,6},{6,2},{3,7},{7,3},{8,12},{12,8},{9,1... | collective-permute-start | bytes 1572872 | tf_op jit(solution)/shard_map/ppermute | solution.py:410
  98.0 23.5 %all-to-all-start.3 = ((f32[16,64,128]{2,1,0:T(8,128)}), f32[16,64,128]{2,1,0:T(8,128)S(1)}, u32[]{:S(2)}, u32[]{:S(2)}) async-start(f32[16,64,128]{2,1,0:T(8,128)} %add.3), calls=%async_computation.3 | async-start | bytes 1048576 | tf_op jit(solution)/shard_map/all_to_all | solution.py:349
  108.8 9.8 %collective-permute-start.8 = (f32[256,128]{1,0:T(8,128)S(1)}, f32[256,128]{1,0:T(8,128)S(1)}, u32[]{:S(2)}, u32[]{:S(2)}) collective-permute-start(f32[256,128]{1,0:T(8,128)S(1)} %get-tuple-element.59), channel_id=1, source_target_pairs={{4,0},{8,4},{12,8},{16,12},{20,16},{24,20},{28,24},{32,28},{36,32}... | collective-permute-start | bytes 393224 | tf_op jit(solution)/shard_map/ppermute | solution.py:415
  122.9 14.2 %copy-start.10 = (f32[128,512]{1,0:T(8,128)S(1)}, f32[128,512]{1,0:T(8,128)}, u32[]{:S(2)}) copy-start(f32[128,512]{1,0:T(8,128)} %copy-done.9) | copy-start | bytes 786436
  122.9 39.6 %all-to-all-start.4 = ((f32[768,1,128]{2,1,0:T(1,128)}), f32[768,1,128]{2,1,0:T(1,128)S(1)}, u32[]{:S(2)}, u32[]{:S(2)}) async-start(f32[768,1,128]{2,1,0:T(1,128)} %bitcast.9), calls=%async_computation.4 | async-start | bytes 786432 | tf_op jit(solution)/shard_map/all_to_all | solution.py:349
  137.7 10.6 %collective-permute-start.9 = (f32[512,128]{1,0:T(8,128)S(1)}, f32[512,128]{1,0:T(8,128)S(1)}, u32[]{:S(2)}, u32[]{:S(2)}) collective-permute-start(f32[512,128]{1,0:T(8,128)S(1)} %get-tuple-element.62), channel_id=1, source_target_pairs={{0,1},{1,2},{2,3},{3,0},{4,5},{5,6},{6,7},{7,4},{8,9},{9,10},{10,1... | collective-permute-start | bytes 786440 | tf_op jit(solution)/shard_map/ppermute | solution.py:362
  139.9 12.9 %collective-permute-start.10 = (f32[512,128]{1,0:T(8,128)S(1)}, f32[512,128]{1,0:T(8,128)S(1)}, u32[]{:S(2)}, u32[]{:S(2)}) collective-permute-start(f32[512,128]{1,0:T(8,128)S(1)} %get-tuple-element.63), channel_id=1, source_target_pairs={{0,2},{1,3},{2,0},{3,1},{4,6},{5,7},{6,4},{7,5},{8,10},{9,11},{10,... | collective-permute-start | bytes 786440 | tf_op jit(solution)/shard_map/ppermute | solution.py:362
  143.6 12.5 %collective-permute-start.11 = (f32[512,128]{1,0:T(8,128)S(1)}, f32[512,128]{1,0:T(8,128)S(1)}, u32[]{:S(2)}, u32[]{:S(2)}) collective-permute-start(f32[512,128]{1,0:T(8,128)S(1)} %get-tuple-element.64), channel_id=1, source_target_pairs={{0,3},{1,0},{2,1},{3,2},{4,7},{5,4},{6,5},{7,6},{8,11},{9,8},{10,9... | collective-permute-start | bytes 786440 | tf_op jit(solution)/shard_map/ppermute | solution.py:362
  163.4 19.8 %all-to-all-start.5 = ((f32[16,64,128]{2,1,0:T(8,128)}), f32[16,64,128]{2,1,0:T(8,128)S(1)}, u32[]{:S(2)}, u32[]{:S(2)}) async-start(f32[16,64,128]{2,1,0:T(8,128)} %shard_map.103), calls=%async_computation.5 | async-start | bytes 1048576 | tf_op jit(solution)/shard_map/all_to_all | solution.py:349
  169.6 9.1 %collective-permute-start.12 = (f32[256,128]{1,0:T(8,128)S(1)}, f32[256,128]{1,0:T(8,128)S(1)}, u32[]{:S(2)}, u32[]{:S(2)}) collective-permute-start(f32[256,128]{1,0:T(8,128)S(1)} %get-tuple-element.68), channel_id=1, source_target_pairs={{4,0},{8,4},{12,8},{16,12},{20,16},{24,20},{28,24},{32,28},{36,32}... | collective-permute-start | bytes 393224 | tf_op jit(solution)/shard_map/ppermute | solution.py:424
  183.3 6.1 %collective-permute-start.13 = (f32[16,64,128]{2,1,0:T(8,128)S(1)}, f32[16,64,128]{2,1,0:T(8,128)S(1)}, u32[]{:S(2)}, u32[]{:S(2)}) collective-permute-start(f32[16,64,128]{2,1,0:T(8,128)S(1)} %all-to-all-done.5.mine_ref), channel_id=1, source_target_pairs={{0,4},{4,0},{1,5},{5,1},{2,6},{6,2},{3,7},{7,3},{8,12},{12,8},{9,1... | collective-permute-start | bytes 1572872 | tf_op jit(solution)/shard_map/ppermute | solution.py:429
  (2 other events, 1.3 us)

commit v9 on v8

--- a/solution.py
+++ b/solution.py
@@ -98,8 +98,8 @@
     message_ref[pl.ds(each, peers, stride=each + 1), :] = lists_ref[...]
 
 
-def place_kernel(each, after1_ref, after2_ref, after3_ref, message_ref, low_ref, high_ref, position_ref):
-    del after1_ref, after2_ref, after3_ref
+def place_kernel(each, after1_ref, after2_ref, after3_ref, after4_ref, message_ref, low_ref, high_ref, position_ref):
+    del after1_ref, after2_ref, after3_ref, after4_ref
     turned = jnp.transpose(every(message_ref, each, each + 1))
     position = jnp.concatenate([turned[turn : turn + 1] for turn in range(each)], axis=1)
     position_ref[...] = position
@@ -314,13 +314,18 @@
         put(3 * (D // WIDTH) + part, grads[:, s * WIDTH : (s + 1) * WIDTH])
 
 
-def rows_kernel(dqkv_ref, win_ref, dx_ref, done_ref):
+def rows_kernel(dqkv_ref, win_ref, dx_hbm, done_ref, dx_ref, sems):
     done_ref[...] = jnp.zeros_like(done_ref)
     grads = split(jnp.concatenate([dqkv_ref[t] for t in range(3)], axis=1))
+    copies = []
     for part in range(D // WIDTH):
         rows = slice(part * WIDTH, (part + 1) * WIDTH)
         win = jnp.concatenate([win_ref[t, rows] for t in range(3)], axis=1)
         dx_ref[part] = mm3(grads, split(win), NT)
+        copies.append(pltpu.make_async_copy(dx_ref.at[part], dx_hbm.at[part], sems.at[part]))
+        copies[-1].start()
+    for copy in copies:
+        copy.wait()
 
 
 def call(kernel, outs, *args, scratch=(), sems=(), scalars=0, held=0, sent=0, room=8, flops=10**9):
@@ -376,7 +381,7 @@
     valid = valid.reshape(1, PATCH)
     low, high, position = call(
         functools.partial(place_kernel, each),
-        [of(HALF, WIDTH), of(HALF, WIDTH), of(1, PATCH)], *cots[1:], arrived, held=3,
+        [of(HALF, WIDTH), of(HALF, WIDTH), of(1, PATCH)], *cots[1:], valid, arrived, held=4,
     )
     grad_early, grad_late, cot_early, cot_late = call(
         cot_kernel, [of(HALF, WIDTH)] * 2 + [of(heads, HALF, WIDTH)] * 2, head, *cots, output_proj, scalars=1,
@@ -397,7 +402,8 @@
         scratch=[(WIDTH, PATCH)] * 3 + [(PATCH, WIDTH)] + [(HERE, PATCH, WIDTH)] * 4, room=24,
     )
     dx, done = call(
-        rows_kernel, [of(D // WIDTH, PATCH, WIDTH), of(8, WIDTH)], dqkv, win
+        rows_kernel, [of(D // WIDTH, PATCH, WIDTH), of(8, WIDTH)], dqkv, win,
+        sent=1, scratch=[(D // WIDTH, PATCH, WIDTH)], sems=[(D // WIDTH,)],
     )
     dx = swap(dx.reshape(-1, WIDTH), "head").reshape(D // WIDTH, PATCH, WIDTH)
     dx_early, dx_late = call(add_kernel, [of(HALF, WIDTH)] * 2, dx)

time: 192 us -> 192 us (level)
  waiting for transfers between devices: 48.8 us -> 46.3 us
  starting transfers between devices: 113 us -> 115 us
    ppermute x6, waiting for transfers between devices: 15.3 us -> 10.1 us  [ahead(): lax.ppermute(x, 'head', [(i, (i + step) % heads) for i in range(heads)])]
    ppermute x1, starting transfers between devices: 6.46 us -> 8.8 us  [shards(): sums = keep + lax.ppermute(send, 'core', [(0, 1), (1, 0)])]
    all_to_all x6, waiting for transfers between devices: 19.5 us -> 21.4 us  [swap(): return lax.all_to_all(x, axis, split_axis=0, concat_axis=0, tiled=True)]
  transfers between devices with their start and end apart: 20 -> 20, of which waited for: 13 -> 15; matrix products, arithmetic and copies ran while one was open for 1% -> 1% of each run, Pallas kernels for 8% -> 8%
where the time goes in v9:
time: 192 us; the launch traced here: 191 us
  starting transfers between devices  115 us (60%)
  waiting for transfers between devices  46.3 us (24%)
  Pallas kernels  21.2 us (11%)
  local copies, waits for them, and re-layouts  5.33 us (3%)
    all_to_all x6, starting transfers between devices, swap(): return lax.all_to_all(x, axis, split_axis=0, concat_axis=0, tiled=True)  59.3 us
    all_to_all x6, waiting for transfers between devices, swap(): return lax.all_to_all(x, axis, split_axis=0, concat_axis=0, tiled=True)  21.4 us
    pallas_call x15, Pallas kernels, call(): pl.pallas_call(kernel, out_shape=tuple((jax.ShapeDtypeStruct(o, F32) for...  21.2 us
    ppermute x6, starting transfers between devices, ahead(): lax.ppermute(x, 'head', [(i, (i + step) % heads) for i in range(heads)])  19.7 us
    ppermute x6, waiting for transfers between devices, ahead(): lax.ppermute(x, 'head', [(i, (i + step) % heads) for i in range(heads)])  10.1 us
    ppermute x1, starting transfers between devices, shards(): sums = keep + lax.ppermute(send, 'core', [(0, 1), (1, 0)])  8.8 us
    ppermute x1, waiting for transfers between devices, shards(): lax.ppermute(out_early, CURVE, down)  6.13 us
    ppermute x1, waiting for transfers between devices, shards(): lax.ppermute(dx_early, CURVE, down)  5.77 us
  transfers between devices with their start and end apart: 20, of which 15 were waited for; matrix products, arithmetic and copies ran while one was open for 1% of the time, Pallas kernels for 8%

profile of v9, /device:TPU:1, one launch (start us, length us, event | category | flops | bytes accessed | tf_op | source)
XLA Modules:
  0.0 190.9 jit_solution(8622873436783015572)
XLA Ops:
  3.6 20.5 %all-to-all-start = ((f32[640,1,128]{2,1,0:T(1,128)}), f32[640,1,128]{2,1,0:T(1,128)S(1)}, u32[]{:S(2)}, u32[]{:S(2)}) async-start(f32[640,1,128]{2,1,0:T(1,128)} %bitcast.3), calls=%async_computation | async-start | bytes 655360 | tf_op jit(solution)/shard_map/all_to_all | solution.py:354
  24.1 4.8 %collective-permute-start.1 = (f32[512,128]{1,0:T(8,128)S(1)}, f32[512,128]{1,0:T(8,128)S(1)}, u32[]{:S(2)}, u32[]{:S(2)}) collective-permute-start(f32[512,128]{1,0:T(8,128)S(1)} %copy-done.2), channel_id=1, source_target_pairs={{0,2},{1,3},{2,0},{3,1},{4,6},{5,7},{6,4},{7,5},{8,10},{9,11},{10,... | collective-permute-start | bytes 786440 | tf_op jit(solution)/shard_map/ppermute | solution.py:367
  29.0 2.3 %collective-permute-start = (f32[512,128]{1,0:T(8,128)S(1)}, f32[512,128]{1,0:T(8,128)S(1)}, u32[]{:S(2)}, u32[]{:S(2)}) collective-permute-start(f32[512,128]{1,0:T(8,128)S(1)} %copy-done.2), channel_id=1, source_target_pairs={{0,1},{1,2},{2,3},{3,0},{4,5},{5,6},{6,7},{7,4},{8,9},{9,10},{10,1... | collective-permute-start | bytes 786440 | tf_op jit(solution)/shard_map/ppermute | solution.py:367
  31.3 4.2 %collective-permute-start.2 = (f32[512,128]{1,0:T(8,128)S(1)}, f32[512,128]{1,0:T(8,128)S(1)}, u32[]{:S(2)}, u32[]{:S(2)}) collective-permute-start(f32[512,128]{1,0:T(8,128)S(1)} %copy-done.2), channel_id=1, source_target_pairs={{0,3},{1,0},{2,1},{3,2},{4,7},{5,4},{6,5},{7,6},{8,11},{9,8},{10,9... | collective-permute-start | bytes 786440 | tf_op jit(solution)/shard_map/ppermute | solution.py:367
  35.5 4.4 %collective-permute-start.3 = (s32[256]{0:T(256)S(1)}, s32[256]{0:T(256)S(1)}, u32[]{:S(2)}, u32[]{:S(2)}) collective-permute-start(s32[256]{0:T(256)S(1)} %get-tuple-element.74), channel_id=1, source_target_pairs={{0,4},{4,8},{8,12},{12,16},{16,20},{20,24},{24,28},{28,32},{32,36}... | collective-permute-start | bytes 3080 | tf_op jit(solution)/shard_map/ppermute | solution.py:380
  40.8 6.4 %all-to-all-done = f32[640,1,128]{2,1,0:T(1,128)S(1)} async-done(((f32[640,1,128]{2,1,0:T(1,128)}), f32[640,1,128]{2,1,0:T(1,128)S(1)}, u32[]{:S(2)}, u32[]{:S(2)}) %all-to-all-start) | async-done | bytes 327712 | tf_op jit(solution)/shard_map/all_to_all | solution.py:354
  47.8 4.2 %collective-permute-start.4 = (f32[256,128]{1,0:T(8,128)S(1)}, f32[256,128]{1,0:T(8,128)S(1)}, u32[]{:S(2)}, u32[]{:S(2)}) collective-permute-start(f32[256,128]{1,0:T(8,128)S(1)} %get-tuple-element.42), channel_id=1, source_target_pairs={{0,4},{4,8},{8,12},{12,16},{16,20},{20,24},{24,28},{28,32},{32,36}... | collective-permute-start | bytes 393224 | tf_op jit(solution)/shard_map/ppermute | solution.py:391
  55.1 4.3 %all-to-all-start.1 = ((f32[4,512,128]{2,1,0:T(8,128)}), f32[4,512,128]{2,1,0:T(8,128)S(1)}, u32[]{:S(2)}, u32[]{:S(2)}) async-start(f32[4,512,128]{2,1,0:T(8,128)} %broadcast_in_dim.2), calls=%async_computation.1 | async-start | bytes 2097152 | tf_op jit(solution)/shard_map/all_to_all | solution.py:354
  59.4 4.5 %collective-permute-start.6 = (f32[4,256,128]{2,1,0:T(8,128)S(1)}, f32[4,256,128]{2,1,0:T(8,128)S(1)}, u32[]{:S(2)}, u32[]{:S(2)}) collective-permute-start(f32[4,256,128]{2,1,0:T(8,128)S(1)} %get-tuple-element.53), channel_id=1, source_target_pairs={{0,4},{4,8},{8,12},{12,16},{16,20},{20,24},{24,28},{28,32},{32,36}... | collective-permute-start | bytes 1572872 | tf_op jit(solution)/shard_map/ppermute | solution.py:390
  63.9 2.1 %collective-permute-start.5 = (f32[256,128]{1,0:T(8,128)S(1)}, f32[256,128]{1,0:T(8,128)S(1)}, u32[]{:S(2)}, u32[]{:S(2)}) collective-permute-start(f32[256,128]{1,0:T(8,128)S(1)} %get-tuple-element.49), channel_id=1, source_target_pairs={{0,4},{4,8},{8,12},{12,16},{16,20},{20,24},{24,28},{28,32},{32,36}... | collective-permute-start | bytes 393224 | tf_op jit(solution)/shard_map/ppermute | solution.py:389
  66.0 3.8 %all-to-all-done.1.x_ref = f32[4,512,128]{2,1,0:T(8,128)S(1)} async-done(((f32[4,512,128]{2,1,0:T(8,128)}), f32[4,512,128]{2,1,0:T(8,128)S(1)}, u32[]{:S(2)}, u32[]{:S(2)}) %all-to-all-start.1) | async-done | bytes 1048608 | tf_op jit(solution)/shard_map/all_to_all | solution.py:354
  69.8 3.7 %shard_map.97 = (f32[3,512,128]{2,1,0:T(8,128)S(1)}, f32[128,512]{1,0:T(8,128)S(1)}, f32[4,512]{1,0:T(4,128)S(1)}) custom-call(f32[4,512,128]{2,1,0:T(8,128)S(1)} %all-to-all-done.1.x_ref, f32[3,512,128]{2,1,0:T(8,128)S(1)} %bitcast.20, s32[1,512]{1,0:T(1,128)S(1)} %bitcast.18), custom_call_target="tpu_custom_call" | custom-call | flops 1000000000 | bytes 2893824 | tf_op jit(solution)/shard_map/pallas_call | solution.py:335
  73.5 5.0 %shard_map.98.dqkv_ref = f32[4,512,128]{2,1,0:T(8,128)S(1)} custom-call(f32[3,512,128]{2,1,0:T(8,128)S(1)} %get-tuple-element.46.qkv_ref, f32[128,512]{1,0:T(8,128)S(1)} %get-tuple-element.47.att_ref, f32[4,512]{1,0:T(4,128)S(1)} %get-tuple-element.48.lse_ref, f32[256,128]{1,0:T(8,128)S(1)} %collective-permute-done.5.before_ref, f32[256,128]{1,0:T(8,128)S(1)} %copy-done.12, ...), custom_call_target="tpu_custom_call" | custom-call | flops 1000000000 | bytes 2369536 | tf_op jit(solution)/shard_map/pallas_call | solution.py:335
  78.6 2.2 %shard_map.99 = (f32[4,512,128]{2,1,0:T(8,128)}, f32[8,128]{1,0:T(8,128)S(1)}) custom-call(f32[4,512,128]{2,1,0:T(8,128)S(1)} %shard_map.98.dqkv_ref, f32[3,512,128]{2,1,0:T(8,128)S(1)} %bitcast.21), custom_call_target="tpu_custom_call" | custom-call | flops 1000000000 | bytes 2887680 | tf_op jit(solution)/shard_map/pallas_call | solution.py:335
  80.8 3.5 %all-to-all-start.2 = ((f32[4,512,128]{2,1,0:T(8,128)}), f32[4,512,128]{2,1,0:T(8,128)S(1)}, u32[]{:S(2)}, u32[]{:S(2)}) async-start(f32[4,512,128]{2,1,0:T(8,128)} %get-tuple-element.51), calls=%async_computation.2 | async-start | bytes 2097152 | tf_op jit(solution)/shard_map/all_to_all | solution.py:354
  87.8 8.8 %collective-permute-start.7 = (f32[16,64,128]{2,1,0:T(8,128)S(1)}, f32[16,64,128]{2,1,0:T(8,128)S(1)}, u32[]{:S(2)}, u32[]{:S(2)}) collective-permute-start(f32[16,64,128]{2,1,0:T(8,128)S(1)} %get-tuple-element.57), channel_id=1, source_target_pairs={{0,4},{4,0},{1,5},{5,1},{2,6},{6,2},{3,7},{7,3},{8,12},{12,8},{9,1... | collective-permute-start | bytes 1572872 | tf_op jit(solution)/shard_map/ppermute | solution.py:416
  99.0 8.6 %all-to-all-start.3 = ((f32[16,64,128]{2,1,0:T(8,128)}), f32[16,64,128]{2,1,0:T(8,128)S(1)}, u32[]{:S(2)}, u32[]{:S(2)}) async-start(f32[16,64,128]{2,1,0:T(8,128)} %add.3), calls=%async_computation.3 | async-start | bytes 1048576 | tf_op jit(solution)/shard_map/all_to_all | solution.py:354
  107.6 4.9 %collective-permute-start.8 = (f32[256,128]{1,0:T(8,128)S(1)}, f32[256,128]{1,0:T(8,128)S(1)}, u32[]{:S(2)}, u32[]{:S(2)}) collective-permute-start(f32[256,128]{1,0:T(8,128)S(1)} %get-tuple-element.59), channel_id=1, source_target_pairs={{4,0},{8,4},{12,8},{16,12},{20,16},{24,20},{28,24},{32,28},{36,32}... | collective-permute-start | bytes 393224 | tf_op jit(solution)/shard_map/ppermute | solution.py:421
  112.5 5.8 %collective-permute-done.8.high_ref = f32[256,128]{1,0:T(8,128)S(1)} collective-permute-done((f32[256,128]{1,0:T(8,128)S(1)}, f32[256,128]{1,0:T(8,128)S(1)}, u32[]{:S(2)}, u32[]{:S(2)}) %collective-permute-start.8) | collective-permute-done | bytes 131104 | tf_op jit(solution)/shard_map/ppermute | solution.py:421
  120.8 16.2 %all-to-all-start.4 = ((f32[768,1,128]{2,1,0:T(1,128)}), f32[768,1,128]{2,1,0:T(1,128)S(1)}, u32[]{:S(2)}, u32[]{:S(2)}) async-start(f32[768,1,128]{2,1,0:T(1,128)} %bitcast.9), calls=%async_computation.4 | async-start | bytes 786432 | tf_op jit(solution)/shard_map/all_to_all | solution.py:354
  137.6 2.2 %collective-permute-start.9 = (f32[512,128]{1,0:T(8,128)S(1)}, f32[512,128]{1,0:T(8,128)S(1)}, u32[]{:S(2)}, u32[]{:S(2)}) collective-permute-start(f32[512,128]{1,0:T(8,128)S(1)} %get-tuple-element.62), channel_id=1, source_target_pairs={{0,1},{1,2},{2,3},{3,0},{4,5},{5,6},{6,7},{7,4},{8,9},{9,10},{10,1... | collective-permute-start | bytes 786440 | tf_op jit(solution)/shard_map/ppermute | solution.py:367
  139.8 3.7 %collective-permute-start.10 = (f32[512,128]{1,0:T(8,128)S(1)}, f32[512,128]{1,0:T(8,128)S(1)}, u32[]{:S(2)}, u32[]{:S(2)}) collective-permute-start(f32[512,128]{1,0:T(8,128)S(1)} %get-tuple-element.63), channel_id=1, source_target_pairs={{0,2},{1,3},{2,0},{3,1},{4,6},{5,7},{6,4},{7,5},{8,10},{9,11},{10,... | collective-permute-start | bytes 786440 | tf_op jit(solution)/shard_map/ppermute | solution.py:367
  143.5 2.5 %collective-permute-start.11 = (f32[512,128]{1,0:T(8,128)S(1)}, f32[512,128]{1,0:T(8,128)S(1)}, u32[]{:S(2)}, u32[]{:S(2)}) collective-permute-start(f32[512,128]{1,0:T(8,128)S(1)} %get-tuple-element.64), channel_id=1, source_target_pairs={{0,3},{1,0},{2,1},{3,2},{4,7},{5,4},{6,5},{7,6},{8,11},{9,8},{10,9... | collective-permute-start | bytes 786440 | tf_op jit(solution)/shard_map/ppermute | solution.py:367
  146.1 2.2 %collective-permute-done.9.second_ref = f32[512,128]{1,0:T(8,128)S(1)} collective-permute-done((f32[512,128]{1,0:T(8,128)S(1)}, f32[512,128]{1,0:T(8,128)S(1)}, u32[]{:S(2)}, u32[]{:S(2)}) %collective-permute-start.9) | collective-permute-done | bytes 262176 | tf_op jit(solution)/shard_map/ppermute | solution.py:367
  148.2 4.5 %collective-permute-done.10.third_ref = f32[512,128]{1,0:T(8,128)S(1)} collective-permute-done((f32[512,128]{1,0:T(8,128)S(1)}, f32[512,128]{1,0:T(8,128)S(1)}, u32[]{:S(2)}, u32[]{:S(2)}) %collective-permute-start.10) | collective-permute-done | bytes 262176 | tf_op jit(solution)/shard_map/ppermute | solution.py:367
  152.7 3.3 %collective-permute-done.11.fourth_ref = f32[512,128]{1,0:T(8,128)S(1)} collective-permute-done((f32[512,128]{1,0:T(8,128)S(1)}, f32[512,128]{1,0:T(8,128)S(1)}, u32[]{:S(2)}, u32[]{:S(2)}) %collective-permute-start.11) | collective-permute-done | bytes 262176 | tf_op jit(solution)/shard_map/ppermute | solution.py:367
  156.1 6.3 %all-to-all-done.4 = f32[768,1,128]{2,1,0:T(1,128)S(1)} async-done(((f32[768,1,128]{2,1,0:T(1,128)}), f32[768,1,128]{2,1,0:T(1,128)S(1)}, u32[]{:S(2)}, u32[]{:S(2)}) %all-to-all-start.4) | async-done | bytes 393248 | tf_op jit(solution)/shard_map/all_to_all | solution.py:354
  163.3 6.1 %all-to-all-start.5 = ((f32[16,64,128]{2,1,0:T(8,128)}), f32[16,64,128]{2,1,0:T(8,128)S(1)}, u32[]{:S(2)}, u32[]{:S(2)}) async-start(f32[16,64,128]{2,1,0:T(8,128)} %shard_map.103), calls=%async_computation.5 | async-start | bytes 1048576 | tf_op jit(solution)/shard_map/all_to_all | solution.py:354
  169.5 3.0 %collective-permute-start.12 = (f32[256,128]{1,0:T(8,128)S(1)}, f32[256,128]{1,0:T(8,128)S(1)}, u32[]{:S(2)}, u32[]{:S(2)}) collective-permute-start(f32[256,128]{1,0:T(8,128)S(1)} %get-tuple-element.68), channel_id=1, source_target_pairs={{4,0},{8,4},{12,8},{16,12},{20,16},{24,20},{28,24},{32,28},{36,32}... | collective-permute-start | bytes 393224 | tf_op jit(solution)/shard_map/ppermute | solution.py:430
  172.5 6.1 %collective-permute-done.12 = f32[256,128]{1,0:T(8,128)S(1)} collective-permute-done((f32[256,128]{1,0:T(8,128)S(1)}, f32[256,128]{1,0:T(8,128)S(1)}, u32[]{:S(2)}, u32[]{:S(2)}) %collective-permute-start.12) | collective-permute-done | bytes 131104 | tf_op jit(solution)/shard_map/ppermute | solution.py:430
  179.4 3.8 %all-to-all-done.5.mine_ref = f32[16,64,128]{2,1,0:T(8,128)S(1)} async-done(((f32[16,64,128]{2,1,0:T(8,128)}), f32[16,64,128]{2,1,0:T(8,128)S(1)}, u32[]{:S(2)}, u32[]{:S(2)}) %all-to-all-start.5) | async-done | bytes 524320 | tf_op jit(solution)/shard_map/all_to_all | solution.py:354
  183.2 4.6 %collective-permute-start.13 = (f32[16,64,128]{2,1,0:T(8,128)S(1)}, f32[16,64,128]{2,1,0:T(8,128)S(1)}, u32[]{:S(2)}, u32[]{:S(2)}) collective-permute-start(f32[16,64,128]{2,1,0:T(8,128)S(1)} %all-to-all-done.5.mine_ref), channel_id=1, source_target_pairs={{0,4},{4,0},{1,5},{5,1},{2,6},{6,2},{3,7},{7,3},{8,12},{12,8},{9,1... | collective-permute-start | bytes 1572872 | tf_op jit(solution)/shard_map/ppermute | solution.py:435
  (57 shorter events, 21.4 us)
Async XLA Ops:
  1.3 0.9 copy-start.1
  3.6 20.5 %copy-start.2 = (f32[512,128]{1,0:T(8,128)S(1)}, f32[512,128]{1,0:T(8,128)}, u32[]{:S(2)}) copy-start(f32[512,128]{1,0:T(8,128)} %cot_ref.1) | copy-start | bytes 786436
  3.6 31.9 %copy-start.13 = (s32[512]{0:T(512)S(1)}, s32[512]{0:T(512)}, u32[]{:S(2)}) copy-start(s32[512]{0:T(512)} %param.10) | copy-start | bytes 6148
  3.6 43.5 %all-to-all-start = ((f32[640,1,128]{2,1,0:T(1,128)}), f32[640,1,128]{2,1,0:T(1,128)S(1)}, u32[]{:S(2)}, u32[]{:S(2)}) async-start(f32[640,1,128]{2,1,0:T(1,128)} %bitcast.3), calls=%async_computation | async-start | bytes 655360 | tf_op jit(solution)/shard_map/all_to_all | solution.py:354
  24.1 16.5 %collective-permute-start.1 = (f32[512,128]{1,0:T(8,128)S(1)}, f32[512,128]{1,0:T(8,128)S(1)}, u32[]{:S(2)}, u32[]{:S(2)}) collective-permute-start(f32[512,128]{1,0:T(8,128)S(1)} %copy-done.2), channel_id=1, source_target_pairs={{0,2},{1,3},{2,0},{3,1},{4,6},{5,7},{6,4},{7,5},{8,10},{9,11},{10,... | collective-permute-start | bytes 786440 | tf_op jit(solution)/shard_map/ppermute | solution.py:367
  29.0 11.8 %collective-permute-start = (f32[512,128]{1,0:T(8,128)S(1)}, f32[512,128]{1,0:T(8,128)S(1)}, u32[]{:S(2)}, u32[]{:S(2)}) collective-permute-start(f32[512,128]{1,0:T(8,128)S(1)} %copy-done.2), channel_id=1, source_target_pairs={{0,1},{1,2},{2,3},{3,0},{4,5},{5,6},{6,7},{7,4},{8,9},{9,10},{10,1... | collective-permute-start | bytes 786440 | tf_op jit(solution)/shard_map/ppermute | solution.py:367
  31.3 9.5 %collective-permute-start.2 = (f32[512,128]{1,0:T(8,128)S(1)}, f32[512,128]{1,0:T(8,128)S(1)}, u32[]{:S(2)}, u32[]{:S(2)}) collective-permute-start(f32[512,128]{1,0:T(8,128)S(1)} %copy-done.2), channel_id=1, source_target_pairs={{0,3},{1,0},{2,1},{3,2},{4,7},{5,4},{6,5},{7,6},{8,11},{9,8},{10,9... | collective-permute-start | bytes 786440 | tf_op jit(solution)/shard_map/ppermute | solution.py:367
  35.5 5.1 %collective-permute-start.3 = (s32[256]{0:T(256)S(1)}, s32[256]{0:T(256)S(1)}, u32[]{:S(2)}, u32[]{:S(2)}) collective-permute-start(s32[256]{0:T(256)S(1)} %get-tuple-element.74), channel_id=1, source_target_pairs={{0,4},{4,8},{8,12},{12,16},{16,20},{20,24},{24,28},{28,32},{32,36}... | collective-permute-start | bytes 3080 | tf_op jit(solution)/shard_map/ppermute | solution.py:380
  47.1 4.8 %copy-start.3 = (f32[128,512]{1,0:T(8,128)S(1)}, f32[128,512]{1,0:T(8,128)}, u32[]{:S(2)}) copy-start(f32[128,512]{1,0:T(8,128)} %wout_ref.3) | copy-start | bytes 786436
  47.8 6.1 %collective-permute-start.4 = (f32[256,128]{1,0:T(8,128)S(1)}, f32[256,128]{1,0:T(8,128)S(1)}, u32[]{:S(2)}, u32[]{:S(2)}) collective-permute-start(f32[256,128]{1,0:T(8,128)S(1)} %get-tuple-element.42), channel_id=1, source_target_pairs={{0,4},{4,8},{8,12},{12,16},{16,20},{20,24},{24,28},{28,32},{32,36}... | collective-permute-start | bytes 393224 | tf_op jit(solution)/shard_map/ppermute | solution.py:391
  52.6 0.8 copy-start.7
  55.1 14.7 %copy-start = (f32[512,3,128]{2,0,1:T(8,128)S(1)}, f32[512,3,128]{2,0,1:T(8,128)}, u32[]{:S(2)}) copy-start(f32[512,3,128]{2,0,1:T(8,128)} %param.7) | copy-start | bytes 2359300
  55.1 14.7 %all-to-all-start.1 = ((f32[4,512,128]{2,1,0:T(8,128)}), f32[4,512,128]{2,1,0:T(8,128)S(1)}, u32[]{:S(2)}, u32[]{:S(2)}) async-start(f32[4,512,128]{2,1,0:T(8,128)} %broadcast_in_dim.2), calls=%async_computation.1 | async-start | bytes 2097152 | tf_op jit(solution)/shard_map/all_to_all | solution.py:354
  59.4 24.9 %collective-permute-start.6 = (f32[4,256,128]{2,1,0:T(8,128)S(1)}, f32[4,256,128]{2,1,0:T(8,128)S(1)}, u32[]{:S(2)}, u32[]{:S(2)}) collective-permute-start(f32[4,256,128]{2,1,0:T(8,128)S(1)} %get-tuple-element.53), channel_id=1, source_target_pairs={{0,4},{4,8},{8,12},{12,16},{16,20},{20,24},{24,28},{28,32},{32,36}... | collective-permute-start | bytes 1572872 | tf_op jit(solution)/shard_map/ppermute | solution.py:390
  63.9 9.6 %collective-permute-start.5 = (f32[256,128]{1,0:T(8,128)S(1)}, f32[256,128]{1,0:T(8,128)S(1)}, u32[]{:S(2)}, u32[]{:S(2)}) collective-permute-start(f32[256,128]{1,0:T(8,128)S(1)} %get-tuple-element.49), channel_id=1, source_target_pairs={{0,4},{4,8},{8,12},{12,16},{16,20},{20,24},{24,28},{28,32},{32,36}... | collective-permute-start | bytes 393224 | tf_op jit(solution)/shard_map/ppermute | solution.py:389
  69.8 3.7 %copy-start.12 = (f32[256,128]{1,0:T(8,128)S(1)}, f32[256,128]{1,0:T(8,128)}, u32[]{:S(2)}) copy-start(f32[256,128]{1,0:T(8,128)} %copy-done.11) | copy-start | bytes 393220
  73.5 5.1 %copy-start.9 = (f32[128,512]{1,0:T(8,128)}, f32[128,512]{1,0:T(8,128)S(1)}, u32[]{:S(2)}) copy-start(f32[128,512]{1,0:T(8,128)S(1)} %get-tuple-element.47.att_ref) | copy-start | bytes 786436
  78.5 2.2 %copy-start.5 = (f32[4,512,128]{2,1,0:T(8,128)}, f32[4,512,128]{2,1,0:T(8,128)S(1)}, u32[]{:S(2)}) copy-start(f32[4,512,128]{2,1,0:T(8,128)S(1)} %shard_map.98.dqkv_ref) | copy-start | bytes 3145732
  80.8 18.2 %all-to-all-start.2 = ((f32[4,512,128]{2,1,0:T(8,128)}), f32[4,512,128]{2,1,0:T(8,128)S(1)}, u32[]{:S(2)}, u32[]{:S(2)}) async-start(f32[4,512,128]{2,1,0:T(8,128)} %get-tuple-element.51), calls=%async_computation.2 | async-start | bytes 2097152 | tf_op jit(solution)/shard_map/all_to_all | solution.py:354
  84.3 1.2 copy-start.6
  85.5 1.0 copy-start.8
  87.8 10.3 %collective-permute-start.7 = (f32[16,64,128]{2,1,0:T(8,128)S(1)}, f32[16,64,128]{2,1,0:T(8,128)S(1)}, u32[]{:S(2)}, u32[]{:S(2)}) collective-permute-start(f32[16,64,128]{2,1,0:T(8,128)S(1)} %get-tuple-element.57), channel_id=1, source_target_pairs={{0,4},{4,0},{1,5},{5,1},{2,6},{6,2},{3,7},{7,3},{8,12},{12,8},{9,1... | collective-permute-start | bytes 1572872 | tf_op jit(solution)/shard_map/ppermute | solution.py:416
  99.0 20.4 %all-to-all-start.3 = ((f32[16,64,128]{2,1,0:T(8,128)}), f32[16,64,128]{2,1,0:T(8,128)S(1)}, u32[]{:S(2)}, u32[]{:S(2)}) async-start(f32[16,64,128]{2,1,0:T(8,128)} %add.3), calls=%async_computation.3 | async-start | bytes 1048576 | tf_op jit(solution)/shard_map/all_to_all | solution.py:354
  107.6 10.7 %collective-permute-start.8 = (f32[256,128]{1,0:T(8,128)S(1)}, f32[256,128]{1,0:T(8,128)S(1)}, u32[]{:S(2)}, u32[]{:S(2)}) collective-permute-start(f32[256,128]{1,0:T(8,128)S(1)} %get-tuple-element.59), channel_id=1, source_target_pairs={{4,0},{8,4},{12,8},{16,12},{20,16},{24,20},{28,24},{32,28},{36,32}... | collective-permute-start | bytes 393224 | tf_op jit(solution)/shard_map/ppermute | solution.py:421
  120.8 16.2 %copy-start.10 = (f32[128,512]{1,0:T(8,128)S(1)}, f32[128,512]{1,0:T(8,128)}, u32[]{:S(2)}) copy-start(f32[128,512]{1,0:T(8,128)} %copy-done.9) | copy-start | bytes 786436
  120.8 41.6 %all-to-all-start.4 = ((f32[768,1,128]{2,1,0:T(1,128)}), f32[768,1,128]{2,1,0:T(1,128)S(1)}, u32[]{:S(2)}, u32[]{:S(2)}) async-start(f32[768,1,128]{2,1,0:T(1,128)} %bitcast.9), calls=%async_computation.4 | async-start | bytes 786432 | tf_op jit(solution)/shard_map/all_to_all | solution.py:354
  137.6 10.6 %collective-permute-start.9 = (f32[512,128]{1,0:T(8,128)S(1)}, f32[512,128]{1,0:T(8,128)S(1)}, u32[]{:S(2)}, u32[]{:S(2)}) collective-permute-start(f32[512,128]{1,0:T(8,128)S(1)} %get-tuple-element.62), channel_id=1, source_target_pairs={{0,1},{1,2},{2,3},{3,0},{4,5},{5,6},{6,7},{7,4},{8,9},{9,10},{10,1... | collective-permute-start | bytes 786440 | tf_op jit(solution)/shard_map/ppermute | solution.py:367
  139.8 12.9 %collective-permute-start.10 = (f32[512,128]{1,0:T(8,128)S(1)}, f32[512,128]{1,0:T(8,128)S(1)}, u32[]{:S(2)}, u32[]{:S(2)}) collective-permute-start(f32[512,128]{1,0:T(8,128)S(1)} %get-tuple-element.63), channel_id=1, source_target_pairs={{0,2},{1,3},{2,0},{3,1},{4,6},{5,7},{6,4},{7,5},{8,10},{9,11},{10,... | collective-permute-start | bytes 786440 | tf_op jit(solution)/shard_map/ppermute | solution.py:367
  143.5 12.5 %collective-permute-start.11 = (f32[512,128]{1,0:T(8,128)S(1)}, f32[512,128]{1,0:T(8,128)S(1)}, u32[]{:S(2)}, u32[]{:S(2)}) collective-permute-start(f32[512,128]{1,0:T(8,128)S(1)} %get-tuple-element.64), channel_id=1, source_target_pairs={{0,3},{1,0},{2,1},{3,2},{4,7},{5,4},{6,5},{7,6},{8,11},{9,8},{10,9... | collective-permute-start | bytes 786440 | tf_op jit(solution)/shard_map/ppermute | solution.py:367
  163.3 19.8 %all-to-all-start.5 = ((f32[16,64,128]{2,1,0:T(8,128)}), f32[16,64,128]{2,1,0:T(8,128)S(1)}, u32[]{:S(2)}, u32[]{:S(2)}) async-start(f32[16,64,128]{2,1,0:T(8,128)} %shard_map.103), calls=%async_computation.5 | async-start | bytes 1048576 | tf_op jit(solution)/shard_map/all_to_all | solution.py:354
  169.5 9.1 %collective-permute-start.12 = (f32[256,128]{1,0:T(8,128)S(1)}, f32[256,128]{1,0:T(8,128)S(1)}, u32[]{:S(2)}, u32[]{:S(2)}) collective-permute-start(f32[256,128]{1,0:T(8,128)S(1)} %get-tuple-element.68), channel_id=1, source_target_pairs={{4,0},{8,4},{12,8},{16,12},{20,16},{24,20},{28,24},{32,28},{36,32}... | collective-permute-start | bytes 393224 | tf_op jit(solution)/shard_map/ppermute | solution.py:430
  183.2 6.1 %collective-permute-start.13 = (f32[16,64,128]{2,1,0:T(8,128)S(1)}, f32[16,64,128]{2,1,0:T(8,128)S(1)}, u32[]{:S(2)}, u32[]{:S(2)}) collective-permute-start(f32[16,64,128]{2,1,0:T(8,128)S(1)} %all-to-all-done.5.mine_ref), channel_id=1, source_target_pairs={{0,4},{4,0},{1,5},{5,1},{2,6},{6,2},{3,7},{7,3},{8,12},{12,8},{9,1... | collective-permute-start | bytes 1572872 | tf_op jit(solution)/shard_map/ppermute | solution.py:435
  (2 other events, 1.3 us)
